TPU v7x, 32 devices: a whole 2x2x4 slice. The times are simulated.
32 devices in a mesh: dp: 4 (over y, core), mp: 8 (over z, x).
Axes of the slice: x: 2, y: 2, z: 4, core: 2. Of those that a mesh axis runs over, the one named last changes fastest.
Arguments:
- tokens: bfloat16 [32, 2048, 512], P('dp', 'mp'), may hold values from -6 to 6
- lengths: int32 [32, 4], P('dp'), may hold values from 0 to 2048, as said below
- cotangent: bfloat16 [32, 2048, 512], P('dp', 'mp'), may hold values from -6 to 6
- norm1_gain: bfloat16 [512], replicated, may hold values from 0.5 to 1.5
- value_proj: bfloat16 [512, 1024], P(None, 'mp'), may hold values from -0.25 to 0.25
- gate_proj: bfloat16 [512, 1024], P(None, 'mp'), may hold values from -0.25 to 0.25
- gate_bias: float32 [1024], P('mp')
- conv_taps: float32 [4, 1024], P(None, 'mp'), may hold values from -3 to 3
- conv_bias: float32 [1024], P('mp'), may hold values from -3 to 3
- out_proj: bfloat16 [1024, 512], P('mp'), may hold values from -0.375 to 0.375
- norm2_gain: bfloat16 [512], replicated, may hold values from 0.5 to 1.5
- up_proj: bfloat16 [512, 2048], P(None, 'mp'), may hold values from -0.25 to 0.25
- down_proj: bfloat16 [2048, 512], P('mp'), may hold values from -0.1875 to 0.1875
Outputs:
- output: bfloat16 [32, 2048, 512], P('dp', 'mp')
- tokens_grad: float32 [32, 2048, 512], P('dp', 'mp')
- norm1_gain_grad: float32 [512], replicated
- value_proj_grad: float32 [512, 1024], P(None, 'mp')
- gate_proj_grad: float32 [512, 1024], P(None, 'mp')
- gate_bias_grad: float32 [1024], P('mp')
- conv_taps_grad: float32 [4, 1024], P(None, 'mp')
- conv_bias_grad: float32 [1024], P('mp')
- out_proj_grad: float32 [1024, 512], P('mp')
- norm2_gain_grad: float32 [512], replicated
- up_proj_grad: float32 [512, 2048], P(None, 'mp')
- down_proj_grad: float32 [2048, 512], P('mp')
Inputs may be any that keep to these rules, and one draw needn't show every extreme that they name: Each row holds one to 4 sequences packed from position 0, each of 256 tokens or more, followed by empty slots of 0; a row's lengths sum to at most 2048, and row 0 is one sequence of 2048 tokens.
All inputs are finite; a program needn't handle non-finite values.
Results may differ from a plain program's by a relative error of at most 0.0085.
Values may be sent and summed in bfloat16 or wider, within the bound.
A program may use at most 384 MiB of HBM per device.

v0:
```python
import jax
import jax.numpy as jnp
from jax import lax
from jax.sharding import PartitionSpec as P

MODEL_WIDTH = 512
KW = 4


norm_eps = 1e-06
root_half = 0.7071067811865476
inv_root_two_pi = 0.3989422804014327


def layout(lengths, span):
    token_places = jnp.arange(span, dtype=jnp.int32)
    sequence_bounds = jnp.cumsum(lengths, axis=1)
    segment_ids = jnp.sum(
        (token_places[None, :, None] >= sequence_bounds[:, None, :]).astype(jnp.int32), axis=2
    )
    inside = (token_places[None, :] < sequence_bounds[:, -1:]).astype(jnp.float32)
    return (segment_ids, inside)


def delayed(values, shift_by):
    return jnp.concatenate(
        [jnp.zeros_like(values[:, :shift_by]), values[:, : values.shape[1] - shift_by]], axis=1
    )


def advanced(values, shift_by):
    return jnp.concatenate([values[:, shift_by:], jnp.zeros_like(values[:, :shift_by])], axis=1)


def linked(earlier, latter):
    return (earlier[0] * latter[0], latter[0] * earlier[1] + latter[1])


def project(left, right):
    return jnp.einsum("rld,de->rle", left, right, preferred_element_type=jnp.float32)


def project_back(left, right):
    return jnp.einsum("rle,de->rld", left, right, preferred_element_type=jnp.float32)


def outer_sum(left, right):
    return jnp.einsum("rld,rle->de", left, right, preferred_element_type=jnp.float32)


def gelu_slope(pre_act):
    normal_cdf = 0.5 * (1.0 + jax.scipy.special.erf(pre_act * root_half))
    return normal_cdf + pre_act * inv_root_two_pi * jnp.exp(-0.5 * pre_act * pre_act)


def rms_forward(values, gain_vec):
    inv_rms = lax.rsqrt(jnp.mean(values * values, axis=2, keepdims=True) + norm_eps)
    return (values * inv_rms * gain_vec, inv_rms)


def full_rows(row_part):
    return lax.all_gather(row_part, "mp", axis=1, tiled=True)


def branch_total(partial_value):
    return lax.psum_scatter(partial_value, "mp", scatter_dimension=1, tiled=True)


def full_grads(grad_part):
    return lax.all_gather(grad_part, "mp", axis=1, tiled=True)


def grad_total(partial_value):
    return lax.psum_scatter(partial_value, "mp", scatter_dimension=1, tiled=True)


def rms_backward(grad_part, value_part, inv_rms, gain_vec, full_width):
    unit_rows = value_part * inv_rms
    weighted = grad_part * gain_vec
    row_inner = jnp.sum(weighted * unit_rows, axis=2, keepdims=True)
    input_grad = inv_rms * (weighted - unit_rows * row_inner / full_width)
    return (input_grad, jnp.sum(grad_part * unit_rows, axis=(0, 1)))


def per_device(
    tokens,
    lengths,
    cotangent,
    norm1_gain,
    value_proj,
    gate_proj,
    gate_bias,
    conv_taps,
    conv_bias,
    out_proj,
    norm2_gain,
    up_proj,
    down_proj,
):
    local_span = tokens.shape[1]
    span = local_span * lax.axis_size("mp")
    segment_ids, inside_full = layout(lengths, span)
    first_place = lax.axis_index("mp") * local_span
    inside = lax.dynamic_slice_in_dim(inside_full, first_place, local_span, 1)
    row_mask = inside[:, :, None]
    seq_links = []
    for start_offset in range(1, KW):
        matches = (segment_ids[:, start_offset:] == segment_ids[:, : span - start_offset]).astype(
            jnp.float32
        )
        seq_links.append(
            jnp.concatenate(
                [jnp.zeros((matches.shape[0], start_offset), jnp.float32), matches], axis=1
            )[:, :, None]
        )
    continue_flag = jnp.concatenate(
        [
            jnp.zeros((segment_ids.shape[0], 1), jnp.float32),
            (segment_ids[:, 1:] == segment_ids[:, : span - 1]).astype(jnp.float32),
        ],
        axis=1,
    )[:, :, None]
    gain_one_f = norm1_gain.astype(jnp.float32)
    gain_two_f = norm2_gain.astype(jnp.float32)
    token_part = tokens.astype(jnp.float32)
    normed_local, inv_one = rms_forward(token_part, gain_one_f)
    normed_local_b = normed_local.astype(jnp.bfloat16)
    normed_b = full_rows(normed_local_b)
    values = project(normed_b, value_proj)
    gate_pre = project(normed_b, gate_proj) + gate_bias
    mixed_in = conv_bias + conv_taps[0] * values
    for start_offset in range(1, KW):
        mixed_in = (
            mixed_in
            + conv_taps[start_offset] * delayed(values, start_offset) * seq_links[start_offset - 1]
        )
    gate_open = jax.nn.sigmoid(gate_pre)
    keep_rate = (1.0 - gate_open) * continue_flag
    _, states = lax.associative_scan(linked, (keep_rate, gate_open * mixed_in), axis=1)
    states_b = states.astype(jnp.bfloat16)
    branch = branch_total(project(states_b, out_proj))
    residual = token_part + branch
    residual_b = residual.astype(jnp.bfloat16)
    residual_bf = residual_b.astype(jnp.float32)
    normed_two, inv_two = rms_forward(residual_bf, gain_two_f)
    normed_two_local = normed_two.astype(jnp.bfloat16)
    grad_out = cotangent.astype(jnp.float32) * row_mask
    grad_out_b = grad_out.astype(jnp.bfloat16)
    normed_two_b = full_rows(normed_two_local)
    hidden_pre = project(normed_two_b, up_proj)
    hidden_b = jax.nn.gelu(hidden_pre, approximate=False).astype(jnp.bfloat16)
    feed_out = branch_total(project(hidden_b, down_proj))
    grad_feed = full_grads(grad_out_b)
    down_grad = outer_sum(hidden_b, grad_feed)
    hidden_grad = (project_back(grad_feed, down_proj) * gelu_slope(hidden_pre)).astype(jnp.bfloat16)
    up_grad = outer_sum(normed_two_b, hidden_grad)
    normed_grad = grad_total(project_back(hidden_grad, up_proj))
    resid_extra, gain_two_grad = rms_backward(
        normed_grad, residual_bf, inv_two, gain_two_f, MODEL_WIDTH
    )
    resid_grad = grad_out + resid_extra
    mix_local = resid_grad.astype(jnp.bfloat16)
    grad_mix = full_grads(mix_local)
    out_grad = outer_sum(states_b, grad_mix)
    state_grad = project_back(grad_mix, out_proj)
    flipped = (jnp.flip(advanced(keep_rate, 1), 1), jnp.flip(state_grad, 1))
    _, carried = lax.associative_scan(linked, flipped, axis=1)
    carried = jnp.flip(carried, 1)
    rate_grad = carried * delayed(states, 1)
    gate_grad = carried * mixed_in - rate_grad * continue_flag
    mixed_grad = carried * gate_open
    gate_pre_grad = (gate_grad * gate_open * (1.0 - gate_open)).astype(jnp.bfloat16)
    gate_bias_grad = jnp.sum(gate_pre_grad.astype(jnp.float32), axis=(0, 1))
    taps_rows = [jnp.sum(mixed_grad * values, axis=(0, 1))]
    value_grad_f = conv_taps[0] * mixed_grad
    for start_offset in range(1, KW):
        linked_grad = mixed_grad * seq_links[start_offset - 1]
        taps_rows.append(jnp.sum(linked_grad * delayed(values, start_offset), axis=(0, 1)))
        value_grad_f = value_grad_f + conv_taps[start_offset] * advanced(linked_grad, start_offset)
    taps_grad = jnp.stack(taps_rows, axis=0)
    bias_grad = jnp.sum(mixed_grad, axis=(0, 1))
    value_grad_b = value_grad_f.astype(jnp.bfloat16)
    value_weight_grad = outer_sum(normed_b, value_grad_b)
    gate_weight_grad = outer_sum(normed_b, gate_pre_grad)
    normed_grad_one = grad_total(
        project_back(value_grad_b, value_proj) + project_back(gate_pre_grad, gate_proj)
    )
    input_extra, gain_one_grad = rms_backward(
        normed_grad_one, token_part, inv_one, gain_one_f, MODEL_WIDTH
    )
    tokens_grad = resid_grad + input_extra
    gains = lax.psum((gain_one_grad, gain_two_grad), ("dp", "mp"))
    summed = lax.psum(
        (
            value_weight_grad,
            gate_weight_grad,
            gate_bias_grad,
            taps_grad,
            bias_grad,
            out_grad,
            up_grad,
            down_grad,
        ),
        "dp",
    )
    output = ((residual + feed_out) * row_mask).astype(jnp.bfloat16)
    return (
        output,
        tokens_grad,
        gains[0],
        summed[0],
        summed[1],
        summed[2],
        summed[3],
        summed[4],
        summed[5],
        gains[1],
        summed[6],
        summed[7],
    )


def solution(mesh):
    in_specs = (
        P("dp", "mp", None),
        P("dp", None),
        P("dp", "mp", None),
        P(),
        P(None, "mp"),
        P(None, "mp"),
        P("mp"),
        P(None, "mp"),
        P("mp"),
        P("mp", None),
        P(),
        P(None, "mp"),
        P("mp", None),
    )
    out_specs = (
        P("dp", "mp", None),
        P("dp", "mp", None),
        P(),
        P(None, "mp"),
        P(None, "mp"),
        P("mp"),
        P(None, "mp"),
        P("mp"),
        P("mp", None),
        P(),
        P(None, "mp"),
        P("mp", None),
    )
    return jax.shard_map(
        per_device, mesh=mesh, in_specs=in_specs, out_specs=out_specs, check_vma=False
    )
```

profile of v0, /device:TPU:0, one launch (start us, length us, event | category | flops | bytes accessed | tf_op | source)
XLA Modules:
  0.0 3701.3 jit_solution(12189537630332617892)
XLA Ops:
  15.4 229.2 %all-gather.5.cloned.1.call-done = bf16[8,2048,512]{2,1,0:T(8,128)(2,1)} async-done(((bf16[8,256,512]{2,1,0:T(8,128)(2,1)}), bf16[8,2048,512]{2,1,0:T(8,128)(2,1)}) %all-gather.5.cloned.1.call-update) | async-done | bytes 16777232 | tf_op jit(solution)/shard_map/all_gather | solution.py:62
  252.9 20.9 fusion.98
  277.0 22.5 slice.690
  299.5 22.4 slice.612
  321.9 22.4 slice.611
  344.3 22.4 slice.614
  366.8 22.4 slice.610
  528.1 22.5 slice.609
  666.1 540.9 %reduce-scatter.5.cloned.1.call-done = f32[8,256,512]{2,1,0:T(8,128)} async-done(((f32[8,2048,512]{2,1,0:T(8,128)}), f32[8,256,512]{2,1,0:T(8,128)}) %reduce-scatter.5.cloned.1.call-update) | async-done | bytes 4194320 | tf_op jit(solution)/shard_map/reduce_scatter | solution.py:66
  1217.4 222.6 %all-gather.7.cloned.1.call-done = bf16[8,2048,512]{2,1,0:T(8,128)(2,1)} async-done(((bf16[8,256,512]{2,1,0:T(8,128)(2,1)}), bf16[8,2048,512]{2,1,0:T(8,128)(2,1)}) %all-gather.7.cloned.1.call-update) | async-done | bytes 16777232 | tf_op jit(solution)/shard_map/all_gather | solution.py:62
  1455.9 212.0 %all-gather.9.cloned.1.call-done = bf16[8,2048,512]{2,1,0:T(8,128)(2,1)} async-done(((bf16[8,256,512]{2,1,0:T(8,128)(2,1)}), bf16[8,2048,512]{2,1,0:T(8,128)(2,1)}) %all-gather.9.cloned.1.call-update) | async-done | bytes 16777232 | tf_op jit(solution)/shard_map/all_gather | solution.py:70
  1697.9 541.6 %reduce-scatter.9.cloned.1.call-done = f32[8,256,512]{2,1,0:T(8,128)} async-done(((f32[8,2048,512]{2,1,0:T(8,128)}), f32[8,256,512]{2,1,0:T(8,128)}) %reduce-scatter.9.cloned.1.call-update) | async-done | bytes 4194320 | tf_op jit(solution)/shard_map/reduce_scatter | solution.py:74
  2252.9 39.5 %fusion.4 = bf16[8,2048,256]{2,1,0:T(8,128)(2,1)S(1)} fusion(f32[8,2048,256]{2,1,0:T(8,128)} %get-tuple-element.100, u8[2048,256]{1,0:T(8,128)(4,1)S(1)} %get-tuple-element.13, u8[2048,256]{1,0:T(8,128)(4,1)S(1)} %get-tuple-element.12), kind=kLoop, calls=%fused_computation.7 | loop fusion | flops 293601280 | bytes 26214400 | tf_op jit(solution)/shard_map/convert_element_type | solution.py:151
  2316.9 22.4 slice.703
  2339.3 22.6 slice.696
  2361.9 22.4 slice.694
  2384.3 32.5 slice.704
  2416.8 33.5 slice.695
  2450.2 32.4 slice.697
  2504.0 22.5 slice.780
  2526.5 22.5 slice.700
  2549.0 22.5 slice.698
  2571.5 32.4 slice.699
  2603.9 32.5 slice.701
  2774.2 33.5 slice.781
  2909.1 63.9 %rev.6 = f32[8,2048,128]{2,1,0:T(8,128)} reverse(f32[8,2048,128]{2,1,0:T(8,128)} %add.480), dimensions={1} | reverse | bytes 16777216 | tf_op jit(solution)/shard_map/jit(_flip)/rev | solution.py:168
  2973.0 17.1 convert_reduce_fusion
  2990.1 18.0 multiply_reduce_fusion.2
  3054.0 24.6 convolution_add_fusion
  3141.6 480.3 %reduce-scatter.11.cloned.1.call-done = f32[8,256,512]{2,1,0:T(8,128)} async-done(((f32[8,2048,512]{2,1,0:T(8,128)}), f32[8,256,512]{2,1,0:T(8,128)}) %reduce-scatter.11.cloned.1.call-update) | async-done | bytes 4194320 | tf_op jit(solution)/shard_map/reduce_scatter | solution.py:74
  3628.6 39.5 %all-reduce.55 = (f32[512]{0:T(512)}, f32[512]{0:T(512)}) all-reduce(f32[512]{0:T(512)S(1)} %get-tuple-element.51, f32[512]{0:T(512)S(1)} %fusion.29), channel_id=1, replica_groups=mesh['dp'=4,'mp'=8] {'dp','mp'}, use_global_device_ids=true, to_apply=%region_11.12 | all-reduce | flops 1024 | bytes 8192 | tf_op jit(solution)/shard_map/psum | solution.py:192
  3668.1 17.7 fusion.35
  (460 shorter events, 751.6 us)
Async XLA Ops:
  7.2 1432.9 %copy-start = (bf16[512,256]{1,0:T(8,128)(2,1)S(1)}, bf16[512,256]{1,0:T(8,128)(2,1)}, u32[]{:S(2)}) copy-start(bf16[512,256]{1,0:T(8,128)(2,1)} %param.24) | copy-start | bytes 786436
  7.2 237.4 %copy-start.29 = (bf16[512,128]{1,0:T(8,128)(2,1)S(1)}, bf16[512,128]{1,0:T(8,128)(2,1)}, u32[]{:S(2)}) copy-start(bf16[512,128]{1,0:T(8,128)(2,1)} %param.17) | copy-start | bytes 393220
  7.2 237.4 %all-gather.5.cloned.1.call-start = ((), (), s32[]{:S(2)}) async-start(), calls=%async_computation.4 | async-start | bytes 18874368 | tf_op jit(solution)/shard_map/all_gather | solution.py:62
  14.2 1192.9 %reduce-scatter.5.cloned.1.call-start = ((), (), s32[]{:S(2)}) async-start(), calls=%async_computation.5 | async-start | bytes 37748736 | tf_op jit(solution)/shard_map/reduce_scatter | solution.py:66
  14.9 237.9 %copy-start.52 = (f32[128]{0:T(128)}, f32[128]{0:T(128)S(1)}, u32[]{:S(2)}) copy-start(f32[128]{0:T(128)S(1)} %get-tuple-element.93) | copy-start | bytes 1540
  14.9 237.9 %copy-start.54 = (f32[128]{0:T(128)}, f32[128]{0:T(128)S(1)}, u32[]{:S(2)}) copy-start(f32[128]{0:T(128)S(1)} %get-tuple-element.94) | copy-start | bytes 1540
  14.9 237.9 %copy-start.56 = (f32[128]{0:T(128)}, f32[128]{0:T(128)S(1)}, u32[]{:S(2)}) copy-start(f32[128]{0:T(128)S(1)} %get-tuple-element.95) | copy-start | bytes 1540
  14.9 237.9 %copy-start.58 = (f32[128]{0:T(128)}, f32[128]{0:T(128)S(1)}, u32[]{:S(2)}) copy-start(f32[128]{0:T(128)S(1)} %get-tuple-element.96) | copy-start | bytes 1540
  15.1 237.8 %copy-start.26 = (f32[8,2048]{1,0:T(8,128)}, f32[8,2048]{1,0:T(8,128)S(1)}, u32[]{:S(2)}) copy-start(f32[8,2048]{1,0:T(8,128)S(1)} %pad_convert_fusion.2) | copy-start | bytes 196612
  15.4 237.5 %copy-start.34 = (f32[8,2048]{1,0:T(8,128)}, f32[8,2048]{1,0:T(8,128)S(1)}, u32[]{:S(2)}) copy-start(f32[8,2048]{1,0:T(8,128)S(1)} %get-tuple-element.101) | copy-start | bytes 196612
  15.4 237.5 %copy-start.36 = (f32[8,2048]{1,0:T(8,128)}, f32[8,2048]{1,0:T(8,128)S(1)}, u32[]{:S(2)}) copy-start(f32[8,2048]{1,0:T(8,128)S(1)} %get-tuple-element.102) | copy-start | bytes 196612
  15.4 237.5 %copy-start.38 = (bf16[512,128]{1,0:T(8,128)(2,1)S(1)}, bf16[512,128]{1,0:T(8,128)(2,1)}, u32[]{:S(2)}) copy-start(bf16[512,128]{1,0:T(8,128)(2,1)} %param.18) | copy-start | bytes 393220
  15.4 237.5 %copy-start.63 = (f32[128]{0:T(128)S(1)}, f32[128]{0:T(128)}, u32[]{:S(2)}) copy-start(f32[128]{0:T(128)} %param.21) | copy-start | bytes 1540
  15.4 237.5 %copy-start.64 = (f32[128]{0:T(128)S(1)}, f32[128]{0:T(128)}, u32[]{:S(2)}) copy-start(f32[128]{0:T(128)} %param.19) | copy-start | bytes 1540
  665.5 541.6 %copy-start.10 = (bf16[8,256,512]{2,1,0:T(8,128)(2,1)S(1)}, bf16[8,256,512]{2,1,0:T(8,128)(2,1)}, u32[]{:S(2)}) copy-start(bf16[8,256,512]{2,1,0:T(8,128)(2,1)} %param.13) | copy-start | bytes 6291460
  665.5 774.6 %all-gather.7.cloned.1.call-start = ((), (), s32[]{:S(2)}) async-start(), calls=%async_computation.6 | async-start | bytes 18874368 | tf_op jit(solution)/shard_map/all_gather | solution.py:62
  666.1 551.2 %copy-start.49 = (f32[512]{0:T(512)}, f32[512]{0:T(512)S(1)}, u32[]{:S(2)}) copy-start(f32[512]{0:T(512)S(1)} %convert_element_type.68) | copy-start | bytes 6148
  1210.0 1029.6 %copy-start.44 = (f32[8,256]{1,0:T(8,128)}, f32[8,256]{1,0:T(8,128)S(1)}, u32[]{:S(2)}) copy-start(f32[8,256]{1,0:T(8,128)S(1)} %add_rsqrt_fusion) | copy-start | bytes 24580
  1213.2 454.7 %all-gather.9.cloned.1.call-start = ((), (), s32[]{:S(2)}) async-start(), calls=%async_computation.8 | async-start | bytes 18874368 | tf_op jit(solution)/shard_map/all_gather | solution.py:70
  1214.0 1025.6 %copy-start.42 = (f32[8,256]{1,0:T(8,128)}, f32[8,256]{1,0:T(8,128)S(1)}, u32[]{:S(2)}) copy-start(f32[8,256]{1,0:T(8,128)S(1)} %fusion.89) | copy-start | bytes 24580
  1217.4 450.5 %copy-start.31 = (bf16[256,512]{1,0:T(8,128)(2,1)S(1)}, bf16[256,512]{1,0:T(8,128)(2,1)}, u32[]{:S(2)}) copy-start(bf16[256,512]{1,0:T(8,128)(2,1)} %param.25) | copy-start | bytes 786436
  1217.4 1022.1 %reduce-scatter.9.cloned.1.call-start = ((), (), s32[]{:S(2)}) async-start(), calls=%async_computation.9 | async-start | bytes 37748736 | tf_op jit(solution)/shard_map/reduce_scatter | solution.py:74
  1697.9 541.7 %copy-start.16 = (bf16[8,256,512]{2,1,0:T(8,128)(2,1)S(1)}, bf16[8,256,512]{2,1,0:T(8,128)(2,1)}, u32[]{:S(2)}) copy-start(bf16[8,256,512]{2,1,0:T(8,128)(2,1)} %copy-done.15) | copy-start | bytes 6291460
  1697.9 541.7 %copy-start.50 = (f32[512]{0:T(512)S(1)}, f32[512]{0:T(512)}, u32[]{:S(2)}) copy-start(f32[512]{0:T(512)} %copy-done.49) | copy-start | bytes 6148
  1697.9 794.6 %all-gather.11.cloned.1.call-start = ((), (), s32[]{:S(2)}) async-start(), calls=%async_computation.10 | async-start | bytes 18874368 | tf_op jit(solution)/shard_map/all_gather | solution.py:70
  2252.8 888.8 %reduce-scatter.7.cloned.1.call-start = ((), (), s32[]{:S(2)}) async-start(), calls=%async_computation.7 | async-start | bytes 37748736 | tf_op jit(solution)/shard_map/reduce_scatter | solution.py:66
  2309.0 1312.9 %reduce-scatter.11.cloned.1.call-start = ((), (), s32[]{:S(2)}) async-start(), calls=%async_computation.11 | async-start | bytes 37748736 | tf_op jit(solution)/shard_map/reduce_scatter | solution.py:74
  3078.6 607.1 %all-reduce.60.cloned.1.call-start = ((), (), s32[]{:S(2)}) async-start(), calls=%async_computation.12 | async-start | bytes 3670016 | tf_op jit(solution)/shard_map/psum | solution.py:193
  3138.5 483.5 %copy-start.11 = (bf16[8,256,512]{2,1,0:T(8,128)(2,1)S(1)}, bf16[8,256,512]{2,1,0:T(8,128)(2,1)}, u32[]{:S(2)}) copy-start(bf16[8,256,512]{2,1,0:T(8,128)(2,1)} %param.13) | copy-start | bytes 6291460
  3138.5 483.5 %copy-start.41 = (f32[8,256]{1,0:T(8,128)S(1)}, f32[8,256]{1,0:T(8,128)}, u32[]{:S(2)}) copy-start(f32[8,256]{1,0:T(8,128)} %copy-done.40) | copy-start | bytes 24580
  3138.5 483.5 %copy-start.43 = (f32[8,256]{1,0:T(8,128)S(1)}, f32[8,256]{1,0:T(8,128)}, u32[]{:S(2)}) copy-start(f32[8,256]{1,0:T(8,128)} %copy-done.42) | copy-start | bytes 24580
  3141.6 526.5 %copy-start.48 = (f32[512]{0:T(512)S(1)}, f32[512]{0:T(512)}, u32[]{:S(2)}) copy-start(f32[512]{0:T(512)} %copy-done.47) | copy-start | bytes 6148
  (48 other events, 683.9 us)
Sparse Core Ops, SparseCore 0:
  14.3 230.2 all-gather.4
  665.6 541.4 reduce-scatter.4
  1213.3 226.7 all-gather.6
  1442.1 225.7 all-gather.8
  1698.0 541.4 reduce-scatter.8
  2252.9 226.7 all-gather.10
  2483.5 541.4 reduce-scatter.6
  3078.8 543.1 reduce-scatter.10
  3625.8 48.1 all-reduce.59
where the time goes:
time: 3740 us; the launch traced here: 3700 us
  waiting for transfers between devices  2230 us (60%)
  local copies, waits for them, and re-layouts  944 us (25%)
  other arithmetic  267 us (7%)
  matrix products  199 us (5%)
  blocking collectives  47.8 us (1%)
    reduce_scatter x2, waiting for transfers between devices, grad_total(): lax.psum_scatter(partial_value, 'mp', scatter_dimension=1, tiled=True)  1020 us
    reduce_scatter x2, waiting for transfers between devices, branch_total(): lax.psum_scatter(partial_value, 'mp', scatter_dimension=1, tiled=True)  541 us
    all_gather x2, waiting for transfers between devices, full_rows(): return lax.all_gather(row_part, 'mp', axis=1, tiled=True)  452 us
    slice x73, local copies, waits for them, and re-layouts, per_device(): _, carried = lax.associative_scan(linked, flipped, axis=1)  448 us
    slice x67, local copies, waits for them, and re-layouts, per_device(): lax.associative_scan(linked, (keep_rate, gate_open * mixed_in), axis=1)  253 us
    all_gather x2, waiting for transfers between devices, full_grads(): return lax.all_gather(grad_part, 'mp', axis=1, tiled=True)  212 us
    dot_general x5, matrix products, project_back(): jnp.einsum('rle,de->rld', left, right, preferred_element_type=jnp.float32)  75 us
  transfers between devices with their start and end apart: 9, of which 6 were waited for; matrix products, arithmetic and copies ran while one was open for 25% of the time, Pallas kernels for 0%

commit v1 on v0

v1 whole, which is shorter than its diff:
```python
import functools

import jax
import jax.numpy as jnp
from jax import lax
from jax.experimental import pallas as pl
from jax.experimental.pallas import tpu as pltpu
from jax.sharding import PartitionSpec as P

KW = 4
NORM_EPS = 1e-06
BP = 32
CT = 256
FT = 512
MIB = 2**20
F32 = jnp.float32
BF16 = jnp.bfloat16

ERF_A = (0.254829592, -0.284496736, 1.421413741, -1.453152027, 1.061405429)
ERF_P = 0.3275911 * 0.7071067811865476
INV_ROOT_TWO_PI = 0.3989422804014327


def gelu_parts(x):
    t = 1.0 / (1.0 + ERF_P * jnp.abs(x))
    e = jnp.exp(-0.5 * (x * x))
    poly = 0.5 * ERF_A[4]
    for a in (ERF_A[3], ERF_A[2], ERF_A[1], ERF_A[0]):
        poly = poly * t + 0.5 * a
    tail = poly * t * e
    cdf = jnp.where(x >= 0, 1.0 - tail, tail)
    return x * cdf, cdf + x * (e * INV_ROOT_TWO_PI)


def dist_of(bounds_ref, first, count):
    place = (lax.broadcasted_iota(jnp.int32, (count, 8, 128), 0) + first).astype(F32)
    start = jnp.zeros((count, 8, 128), F32)
    for s in range(bounds_ref.shape[0]):
        b = bounds_ref[s][None]
        start = jnp.where(b <= place, jnp.maximum(start, b), start)
    return (place - start).reshape(count * 8, 128)


def wide(d):
    return jnp.concatenate([d] * (CT // 128), axis=1)


def dot(a, b):
    return jnp.dot(a, b, preferred_element_type=F32)


def dot_nt(a, b):
    return lax.dot_general(a, b, (((1,), (1,)), ((), ())), preferred_element_type=F32)


def dot_tn(a, b):
    return lax.dot_general(a, b, (((0,), (0,)), ((), ())), preferred_element_type=F32)


def mixer_kernel(span, x_ref, xh_ref, wv_ref, wg_ref, gain_ref, gb_ref, taps_ref, cb_ref, bounds_ref,
                 vals_ref, g_ref, m_ref, s_ref, a_ref, vbuf, gbuf, dbuf):
    step = pl.program_id(0)
    rows = BP * 8
    width = wv_ref.shape[1]
    gain = gain_ref[...]

    def normed(x):
        x = x.astype(F32)
        inv = lax.rsqrt(jnp.mean(x * x, axis=1, keepdims=True) + NORM_EPS)
        return (x * inv * gain).astype(BF16)

    @pl.when(step == 0)
    def _():
        vbuf[0:32] = dot(normed(xh_ref[...]), wv_ref[...])
        s_ref[...] = jnp.zeros_like(s_ref)
        a_ref[...] = jnp.ones_like(a_ref)

    n = normed(x_ref[...])
    vbuf[32 : 32 + rows] = dot(n, wv_ref[...])
    gbuf[...] = dot(n, wg_ref[...])
    first = lax.axis_index("mp") * span + step * BP
    dbuf[...] = dist_of(bounds_ref, first, BP)
    for c in range(0, width, CT):
        lanes = slice(c, c + CT)
        taps = [jnp.broadcast_to(taps_ref[j : j + 1, lanes], (8, CT)) for j in range(KW)]
        bias = jnp.broadcast_to(gb_ref[:, lanes], (8, CT))
        cb = jnp.broadcast_to(cb_ref[:, lanes], (8, CT))
        state, decay = s_ref[:, lanes], a_ref[:, lanes]
        v1, v2, v3 = vbuf[24:32, lanes], vbuf[16:24, lanes], vbuf[8:16, lanes]
        for p in range(BP):
            at = slice(8 * p, 8 * p + 8)
            v0 = vbuf[32 + 8 * p : 40 + 8 * p, lanes]
            gate = jax.nn.sigmoid(gbuf[at, lanes] + bias)
            d = wide(dbuf[at])
            mixed = cb + taps[0] * v0
            mixed = mixed + jnp.where(d >= 1.0, taps[1] * v1, 0.0)
            mixed = mixed + jnp.where(d >= 2.0, taps[2] * v2, 0.0)
            mixed = mixed + jnp.where(d >= 3.0, taps[3] * v3, 0.0)
            linked = jnp.where(d >= 1.0, state, 0.0)
            state = linked + gate * (mixed - linked)
            decay = jnp.where(d >= 1.0, decay * (1.0 - gate), 0.0)
            g_ref[at, lanes] = gate
            m_ref[at, lanes] = mixed
            v1, v2, v3 = v0, v1, v2
        s_ref[:, lanes], a_ref[:, lanes] = state, decay
    for r in range(0, rows, 32):
        vals_ref[r : r + 32] = vbuf[32 + r : 64 + r].astype(BF16)
    vbuf[0:32] = vbuf[rows : rows + 32]


def feed_kernel(span, x_ref, cot_ref, g_ref, m_ref, s0_ref, wo_ref, wu_ref, wd_ref, gain_ref, bounds_ref,
                out_ref, sg_ref, z_ref, rg_ref, dwo_ref, dwu_ref, dwd_ref, dgain_ref, acc_ref, c2_ref,
                state_ref, dbuf, stb, hp, dh, hb, hg):
    step = pl.program_id(0)
    rows = BP * 8
    width, units = wo_ref.shape[0], wu_ref.shape[1]

    @pl.when(step == 0)
    def _():
        state_ref[...] = s0_ref[...]
        dwo_ref[...] = jnp.zeros_like(dwo_ref)
        dwu_ref[...] = jnp.zeros_like(dwu_ref)
        dwd_ref[...] = jnp.zeros_like(dwd_ref)
        dgain_ref[...] = jnp.zeros_like(dgain_ref)
        acc_ref[...] = jnp.zeros_like(acc_ref)
        c2_ref[...] = jnp.ones_like(c2_ref)

    first = lax.axis_index("mp") * span + step * BP
    dbuf[...] = dist_of(bounds_ref, first, BP)
    for c in range(0, width, CT):
        lanes = slice(c, c + CT)
        state = state_ref[:, lanes]
        for p in range(0, BP, 2):
            pair = []
            for q in (p, p + 1):
                at = slice(8 * q, 8 * q + 8)
                linked = jnp.where(wide(dbuf[at]) >= 1.0, state, 0.0)
                z = m_ref[at, lanes] - linked
                state = linked + g_ref[at, lanes] * z
                z_ref[at, lanes] = z
                pair.append(state)
            stb[8 * p : 8 * p + 16, lanes] = jnp.concatenate(pair, axis=0).astype(BF16)
        state_ref[:, lanes] = state

    gain = gain_ref[...]
    place = (lax.broadcasted_iota(jnp.int32, (BP, 8, 128), 0) + first).astype(F32)
    last = bounds_ref.shape[0] - 1
    inside = jnp.where(place < bounds_ref[last][None], 1.0, 0.0).reshape(rows, 128)[:, 0:1]
    residual = x_ref[...].astype(F32) + dot(stb[...], wo_ref[...])
    resid = residual.astype(BF16).astype(F32)
    inv = lax.rsqrt(jnp.mean(resid * resid, axis=1, keepdims=True) + NORM_EPS)
    unit = resid * inv
    n2 = (unit * gain).astype(BF16)
    grad_out = cot_ref[...].astype(F32) * inside
    fg = grad_out.astype(BF16)
    for f in range(0, units, FT):
        cols = slice(f, f + FT)
        hp[...] = dot(n2, wu_ref[:, cols])
        dh[...] = dot_nt(fg, wd_ref[cols, :])
        for r in range(0, rows, 16):
            at = slice(r, r + 16)
            hidden, slope = gelu_parts(hp[at])
            hb[at, cols] = hidden.astype(BF16)
            hg[at, cols] = (dh[at] * slope).astype(BF16)
    feed_out = dot(hb[...], wd_ref[...])
    out_ref[...] = ((residual + feed_out) * inside).astype(BF16)
    ngrad = dot_nt(hg[...], wu_ref[...])
    dwd_ref[...] += dot_tn(fg, hb[...])
    dwu_ref[...] += dot_tn(n2, hg[...])
    weighted = ngrad * gain
    inner = jnp.mean(weighted * unit, axis=1, keepdims=True)
    rgrad = grad_out + inv * (weighted - unit * inner)
    rg_ref[...] = rgrad
    dgain_ref[...] += jnp.sum((ngrad * unit).reshape(BP, 8, -1), axis=0)
    mix = rgrad.astype(BF16)
    dwo_ref[...] += dot_tn(mix, stb[...])
    sg_ref[...] = dot_nt(mix, wo_ref[...])
    for c in range(0, width, CT):
        lanes = slice(c, c + CT)
        acc, decay = acc_ref[:, lanes], c2_ref[:, lanes]
        for p in range(BP):
            at = slice(8 * p, 8 * p + 8)
            keep = jnp.where(wide(dbuf[at]) >= 1.0, 1.0 - g_ref[at, lanes], 0.0)
            if p < 3:
                keep = jnp.where(step == 0, 1.0, keep)
            decay = decay * keep
            term = decay * sg_ref[at, lanes]
            if p < 2:
                term = jnp.where(step == 0, 0.0, term)
            acc = acc + term
        acc_ref[:, lanes], c2_ref[:, lanes] = acc, decay


def back_kernel(span, blocks, x_ref, sg_ref, g_ref, z_ref, v_ref, rg_ref, u0_ref, gn_ref, wv_ref, wg_ref, gain_ref, taps_ref,
                bounds_ref, tg_ref, dwv_ref, dwg_ref, dgain_ref, sums_ref, u_ref, gdel, dbuf, vg, gpg):
    step = pl.program_id(0)
    rows = BP * 8
    width = wv_ref.shape[1]

    @pl.when(step == 0)
    def _():
        u_ref[...] = u0_ref[...]
        gdel[...] = gn_ref[...]
        dwv_ref[...] = jnp.zeros_like(dwv_ref)
        dwg_ref[...] = jnp.zeros_like(dwg_ref)
        dgain_ref[...] = jnp.zeros_like(dgain_ref)
        sums_ref[...] = jnp.zeros_like(sums_ref)

    first = lax.axis_index("mp") * span + (blocks - 1 - step) * BP
    dbuf[...] = dist_of(bounds_ref, first, BP + 4)
    for c in range(0, width, CT):
        lanes = slice(c, c + CT)
        taps = [jnp.broadcast_to(taps_ref[j : j + 1, lanes], (8, CT)) for j in range(KW)]
        u = u_ref[:, lanes]
        g1, g2, g3 = (gdel[8 * i : 8 * i + 8, lanes] for i in range(3))
        sums = [sums_ref[8 * i : 8 * i + 8, lanes] for i in range(KW + 2)]
        for p in range(BP - 2, -2, -2):
            vals = v_ref[8 * p : 8 * p + 16, lanes].astype(F32)
            vgs, gpgs = [None, None], [None, None]
            for k in (1, 0):
                q = p + k
                at = slice(8 * q, 8 * q + 8)
                gate = g_ref[at, lanes]
                carried = sg_ref[at, lanes] + u
                g0 = carried * gate
                gp = g0 * z_ref[at, lanes] * (1.0 - gate)
                u = jnp.where(wide(dbuf[at]) >= 1.0, carried - g0, 0.0)
                h1 = jnp.where(wide(dbuf[8 * q + 8 : 8 * q + 16]) >= 1.0, g1, 0.0)
                h2 = jnp.where(wide(dbuf[8 * q + 16 : 8 * q + 24]) >= 2.0, g2, 0.0)
                h3 = jnp.where(wide(dbuf[8 * q + 24 : 8 * q + 32]) >= 3.0, g3, 0.0)
                v = vals[8 * k : 8 * k + 8]
                vgs[k] = taps[0] * g0 + taps[1] * h1 + taps[2] * h2 + taps[3] * h3
                gpgs[k] = gp
                for j, h in enumerate((g0, h1, h2, h3)):
                    sums[j] = sums[j] + v * h
                sums[KW] = sums[KW] + g0
                sums[KW + 1] = sums[KW + 1] + gp.astype(BF16).astype(F32)
                g1, g2, g3 = g0, g1, g2
            vg[8 * p : 8 * p + 16, lanes] = jnp.concatenate(vgs, axis=0).astype(BF16)
            gpg[8 * p : 8 * p + 16, lanes] = jnp.concatenate(gpgs, axis=0).astype(BF16)
        u_ref[:, lanes] = u
        for i, g in enumerate((g1, g2, g3)):
            gdel[8 * i : 8 * i + 8, lanes] = g
        for i in range(KW + 2):
            sums_ref[8 * i : 8 * i + 8, lanes] = sums[i]

    gain = gain_ref[...]
    x = x_ref[...].astype(F32)
    inv = lax.rsqrt(jnp.mean(x * x, axis=1, keepdims=True) + NORM_EPS)
    unit = x * inv
    n1 = (unit * gain).astype(BF16)
    dwv_ref[...] += dot_tn(n1, vg[...])
    dwg_ref[...] += dot_tn(n1, gpg[...])
    ngrad = dot_nt(vg[...], wv_ref[...]) + dot_nt(gpg[...], wg_ref[...])
    weighted = ngrad * gain
    inner = jnp.mean(weighted * unit, axis=1, keepdims=True)
    tg_ref[...] = rg_ref[...] + inv * (weighted - unit * inner)
    dgain_ref[...] += jnp.sum((ngrad * unit).reshape(BP, 8, -1), axis=0)


def whole(shape):
    return pl.BlockSpec(shape, lambda i: (0,) * len(shape))


def per_device(tokens, lengths, cotangent, norm1_gain, value_proj, gate_proj, gate_bias, conv_taps, conv_bias, out_proj,
               norm2_gain, up_proj, down_proj):
    rows, span, dim = tokens.shape
    n_mp = lax.axis_size("mp")
    me = lax.axis_index("mp")
    total = rows * span
    blocks = span // BP
    tile = BP * 8

    bounds = [lengths[:, 0]]
    for s in range(1, lengths.shape[1]):
        bounds.append(bounds[-1] + lengths[:, s])
    bounds = jnp.broadcast_to(jnp.stack(bounds, 0).astype(F32)[:, :, None], (lengths.shape[1], rows, 128))

    def time_major(a):
        return jnp.transpose(a, (1, 0, 2)).reshape(-1, a.shape[2])

    def row_major(a):
        return jnp.transpose(a.reshape(span, rows, dim), (1, 0, 2))

    halo = lax.ppermute(tokens[:, span - 4 :], "mp", [(i, i + 1) for i in range(n_mp - 1)])
    x_tm, cot_tm, halo_tm = time_major(tokens), time_major(cotangent), time_major(halo)
    def gather(w, axis):
        return lax.all_gather(w, "mp", axis=axis, tiled=True)
    wv, wg, wo = gather(value_proj, 1), gather(gate_proj, 1), gather(out_proj, 0)
    wu, wd = gather(up_proj, 1), gather(down_proj, 0)
    gate_b, cbias = gather(gate_bias, 0)[None], gather(conv_bias, 0)[None]
    taps = gather(conv_taps, 1)
    gain1, gain2 = norm1_gain.astype(F32)[None], norm2_gain.astype(F32)[None]
    width, units = wv.shape[1], wu.shape[1]

    def blk(w):
        return pl.BlockSpec((tile, w), lambda i: (i, 0))

    def rblk(w):
        return pl.BlockSpec((tile, w), lambda i: (blocks - 1 - i, 0))

    params = pltpu.CompilerParams(vmem_limit_bytes=58 * MIB)

    def sds(shape, t=F32):
        return jax.ShapeDtypeStruct(shape, t)

    vals, gate, mixed, s_end, a_end = pl.pallas_call(
        functools.partial(mixer_kernel, span),
        grid=(blocks,),
        in_specs=[blk(dim), whole((32, dim)), whole((dim, width)), whole((dim, width)), whole((1, dim)), whole((1, width)),
                  whole((KW, width)), whole((1, width)), whole(bounds.shape)],
        out_specs=[blk(width), blk(width), blk(width), whole((8, width)), whole((8, width))],
        out_shape=[sds((total, width), BF16), sds((total, width)), sds((total, width)), sds((8, width)), sds((8, width))],
        scratch_shapes=[pltpu.VMEM((tile + 32, width), F32), pltpu.VMEM((tile, width), F32), pltpu.VMEM((tile, 128), F32)],
        compiler_params=params,
        name="mixer",
    )(x_tm, halo_tm, wv, wg, gain1, gate_b, taps, cbias, bounds)

    s_all, a_all = lax.all_gather(s_end, "mp"), lax.all_gather(a_end, "mp")
    carry = jnp.zeros_like(s_end)
    s0 = carry
    for i in range(n_mp - 1):
        carry = s_all[i] + a_all[i] * carry
        s0 = jnp.where(me == i + 1, carry, s0)

    out_tm, sg, z, rg, dwo, dwu, dwd, dgain2, acc, c2 = pl.pallas_call(
        functools.partial(feed_kernel, span),
        grid=(blocks,),
        in_specs=[blk(dim), blk(dim), blk(width), blk(width), whole((8, width)), whole((width, dim)), whole((dim, units)),
                  whole((units, dim)), whole((1, dim)), whole(bounds.shape)],
        out_specs=[blk(dim), blk(width), blk(width), blk(dim), whole((dim, width)), whole((dim, units)), whole((dim, units)),
                   whole((8, dim)), whole((8, width)), whole((8, width))],
        out_shape=[sds((total, dim), BF16), sds((total, width)), sds((total, width)), sds((total, dim)), sds((dim, width)),
                   sds((dim, units)), sds((dim, units)), sds((8, dim)), sds((8, width)), sds((8, width))],
        scratch_shapes=[pltpu.VMEM((8, width), F32), pltpu.VMEM((tile, 128), F32), pltpu.VMEM((tile, width), BF16),
                        pltpu.VMEM((tile, FT), F32), pltpu.VMEM((tile, FT), F32), pltpu.VMEM((tile, units), BF16),
                        pltpu.VMEM((tile, units), BF16)],
        compiler_params=params,
        name="feed",
    )(x_tm, cot_tm, gate, mixed, s0, wo, wu, wd, gain2, bounds)

    first = me * span
    place = (first + jnp.arange(3)).astype(F32)[:, None]
    link = jnp.zeros((3, rows), bool)
    starts = jnp.concatenate([jnp.zeros_like(bounds[:1, :, 0]), bounds[:, :, 0]], 0)
    link = ~jnp.any(starts[None] == place[:, None], axis=1)
    g3 = gate[: 3 * 8].reshape(3, 8, width)
    k3 = jnp.where(link[:, :, None], 1.0 - g3, 0.0)
    sg2 = sg[: 2 * 8].reshape(2, 8, width)
    acc1 = sg2[1] + k3[2] * acc
    acc0 = sg2[0] + k3[1] * acc1
    c1 = k3[2] * c2
    c0 = k3[1] * c1
    b_all = lax.all_gather(k3[0] * acc0, "mp")
    u = jnp.zeros_like(s_end)
    u0, u_next = u, u
    for i in range(n_mp - 1, 0, -1):
        u_next = jnp.where(me == i - 1, u, u_next)
        u = b_all[i] + a_all[i] * u
        u0 = jnp.where(me == i - 1, u, u0)
    message = jnp.stack([g3[0] * acc0, g3[1] * acc1, g3[2] * acc, g3[0] * c0, g3[1] * c1, g3[2] * c2])
    message = lax.ppermute(message, "mp", [(i + 1, i) for i in range(n_mp - 1)])
    g_next = (message[:3] + message[3:] * u_next).reshape(24, width)

    tg_tm, dwv, dwg, dgain1, sums = pl.pallas_call(
        functools.partial(back_kernel, span, blocks),
        grid=(blocks,),
        in_specs=[rblk(dim), rblk(width), rblk(width), rblk(width), rblk(width), rblk(dim), whole((8, width)), whole((24, width)),
                  whole((dim, width)), whole((dim, width)), whole((1, dim)), whole((KW, width)), whole(bounds.shape)],
        out_specs=[rblk(dim), whole((dim, width)), whole((dim, width)), whole((8, dim)), whole((8 * (KW + 2), width))],
        out_shape=[sds((total, dim)), sds((dim, width)), sds((dim, width)), sds((8, dim)), sds((8 * (KW + 2), width))],
        scratch_shapes=[pltpu.VMEM((8, width), F32), pltpu.VMEM((24, width), F32), pltpu.VMEM((tile + 32, 128), F32),
                        pltpu.VMEM((tile, width), BF16), pltpu.VMEM((tile, width), BF16)],
        compiler_params=params,
        name="back",
    )(x_tm, sg, gate, z, vals, rg, u0, g_next, wv, wg, gain1, taps, bounds)

    def total_cols(g):
        return lax.psum(lax.psum_scatter(g.astype(BF16), "mp", scatter_dimension=1, tiled=True).astype(F32), "dp")

    sums = jnp.sum(sums.reshape(KW + 2, 8, width), axis=1)
    sums = lax.psum(lax.psum_scatter(sums, "mp", scatter_dimension=1, tiled=True), "dp")
    gains = lax.psum(jnp.stack([dgain1.sum(0), dgain2.sum(0)]), ("dp", "mp"))
    return (
        row_major(out_tm),
        row_major(tg_tm),
        gains[0],
        total_cols(dwv),
        total_cols(dwg),
        sums[KW + 1],
        sums[:KW],
        sums[KW],
        total_cols(dwo).T,
        gains[1],
        total_cols(dwu),
        total_cols(dwd).T,
    )


def solution(mesh):
    in_specs = (
        P("dp", "mp", None),
        P("dp", None),
        P("dp", "mp", None),
        P(),
        P(None, "mp"),
        P(None, "mp"),
        P("mp"),
        P(None, "mp"),
        P("mp"),
        P("mp", None),
        P(),
        P(None, "mp"),
        P("mp", None),
    )
    out_specs = (
        P("dp", "mp", None),
        P("dp", "mp", None),
        P(),
        P(None, "mp"),
        P(None, "mp"),
        P("mp"),
        P(None, "mp"),
        P("mp"),
        P("mp", None),
        P(),
        P(None, "mp"),
        P("mp", None),
    )
    return jax.shard_map(per_device, mesh=mesh, in_specs=in_specs, out_specs=out_specs, check_vma=False)
```

time: 3740 us -> 744 us (0.20)
  waiting for transfers between devices: 2230 us -> 338 us
  local copies, waits for them, and re-layouts: 944 us -> 30.8 us
  other arithmetic: 267 us -> 24.6 us
  matrix products: 199 us -> 0 us
  blocking collectives: 47.8 us -> 232 us
  Pallas kernels: 0 us -> 96.7 us
    reduce_scatter x4 -> x3, waiting for transfers between devices: 1560 us -> 137 us  [the longest x2 80 us: total_cols(): lax.psum_scatter(g.astype(BF16), 'mp', scatter_dimension=1, tiled=True)]
    slice x144 -> x3, local copies, waits for them, and re-layouts: 724 us -> 2.03 us  [the longest x1 0.86 us: per_device(): tokens[:, span - 4:]]
    all_gather x4 -> x5, waiting for transfers between devices: 664 us -> 70.9 us  [gather(): return lax.all_gather(w, 'mp', axis=axis, tiled=True)]
    dot_general x15 -> x0, matrix products: 199 us -> none  [the longest x5 75 us: project_back(): jnp.einsum('rle,de->rld', left, right, preferred_element_type=jnp.float32)]
    all_gather x0 -> x6, blocking collectives: none -> 157 us  [the longest x2 63.2 us: per_device(): s_all, a_all = (lax.all_gather(s_end, 'mp'), lax.all_gather(a_end, 'mp'))]
    unnamed x9 -> x15, waiting for transfers between devices: 0.15 us -> 125 us
    pad x40 -> x0, local copies, waits for them, and re-layouts: 122 us -> none  [the longest x20 62.3 us: per_device(): lax.associative_scan(linked, (keep_rate, gate_open * mixed_in), axis=1)]
    pallas_call x0 -> x3, Pallas kernels: none -> 96.7 us  [the longest x1 57 us: per_device(): pl.pallas_call(functools.partial(feed_kernel, span), grid=(blocks,), in_s...]
  transfers between devices with their start and end apart: 9 -> 14, of which waited for: 6 -> 9; matrix products, arithmetic and copies ran while one was open for 25% -> 7% of each run, Pallas kernels for 0% -> 5%
where the time goes in v1:
time: 744 us; the launch traced here: 743 us
  waiting for transfers between devices  338 us (45%)
  blocking collectives  232 us (31%)
  Pallas kernels  96.7 us (13%)
  local copies, waits for them, and re-layouts  30.8 us (4%)
  other arithmetic  24.6 us (3%)
  between operations  14.5 us (2%)
    unnamed x15, waiting for transfers between devices  125 us
    reduce_scatter x2, waiting for transfers between devices, total_cols(): lax.psum_scatter(g.astype(BF16), 'mp', scatter_dimension=1, tiled=True)  80 us
    all_gather x5, waiting for transfers between devices, gather(): return lax.all_gather(w, 'mp', axis=axis, tiled=True)  70.9 us
    all_gather x2, blocking collectives, per_device(): s_all, a_all = (lax.all_gather(s_end, 'mp'), lax.all_gather(a_end, 'mp'))  63.2 us
    all_gather x3, blocking collectives, gather(): return lax.all_gather(w, 'mp', axis=axis, tiled=True)  62.6 us
    pallas_call x1, Pallas kernels, per_device(): pl.pallas_call(functools.partial(feed_kernel, span), grid=(blocks,), in_s...  57 us
    reduce_scatter x1, waiting for transfers between devices, per_device(): lax.psum_scatter(sums, 'mp', scatter_dimension=1, tiled=True)  56.5 us
    psum x1, blocking collectives, per_device(): gains = lax.psum(jnp.stack([dgain1.sum(0), dgain2.sum(0)]), ('dp', 'mp'))  39.6 us
  transfers between devices with their start and end apart: 14, of which 9 were waited for; matrix products, arithmetic and copies ran while one was open for 7% of the time, Pallas kernels for 5%

profile of v1, /device:TPU:0, one launch (start us, length us, event | category | flops | bytes accessed | tf_op | source)
XLA Modules:
  0.0 742.6 jit_solution(5522403848569902515)
XLA Ops:
  11.5 4.8 collective-permute-start
  17.9 4.1 copy.60
  22.6 2.6 copy.59
  25.7 19.2 %all-gather.3 = f32[8,1,128]{2,1,0:T(1,128)} all-gather(f32[1,1,128]{2,1,0:T(1,128)S(1)} %bitcast.164), channel_id=1, replica_groups=mesh['dp'=4,'mp'=8] {'mp'}, dimensions={0}, use_global_device_ids=true | all-gather | bytes 4608 | tf_op jit(solution)/shard_map/all_gather | solution.py:288
  44.9 16.7 %all-gather.4 = f32[8,1,128]{2,1,0:T(1,128)} all-gather(f32[1,1,128]{2,1,0:T(1,128)S(1)} %bitcast.165), channel_id=1, replica_groups=mesh['dp'=4,'mp'=8] {'mp'}, dimensions={0}, use_global_device_ids=true | all-gather | bytes 4608 | tf_op jit(solution)/shard_map/all_gather | solution.py:288
  61.6 26.8 %all_gather.45.taps_ref = f32[4,1024]{1,0:T(4,128)} all-gather(f32[4,128]{1,0:T(4,128)S(1)} %copy-done.8), channel_id=1, replica_groups=mesh['dp'=4,'mp'=8] {'mp'}, dimensions={1}, use_global_device_ids=true | all-gather | bytes 18432 | tf_op jit(solution)/shard_map/all_gather | solution.py:288
  89.0 4.1 all-gather.13.cloned.1.call-done.wg_ref
  93.8 13.4 %mixer.1 = (bf16[2048,1024]{1,0:T(8,128)(2,1)}, f32[2048,1024]{1,0:T(8,128)}, f32[2048,1024]{1,0:T(8,128)}, f32[8,1024]{1,0:T(8,128)}, f32[8,1024]{1,0:T(8,128)}) custom-call(bf16[2048,512]{1,0:T(8,128)(2,1)} %bitcast.137, bf16[32,512]{1,0:T(8,128)(2,1)} %bitcast.150, bf16[512,1024]{1,0:T(8,128)(2,1)} %all-gather.11.cloned.1.call-done.wv_ref, ...), custom_call_target="tpu_custom_call" | custom-call | tf_op jit(solution)/shard_map/mixer/pallas_call | solution.py:307
  107.2 31.5 %all-gather.1 = f32[64,1024]{1,0:T(8,128)S(1)} all-gather(f32[8,1024]{1,0:T(8,128)} %get-tuple-element.35), channel_id=3, replica_groups=mesh['dp'=4,'mp'=8] {'mp'}, dimensions={0}, use_global_device_ids=true | all-gather | bytes 294912 | tf_op jit(solution)/shard_map/all_gather | solution.py:319
  138.7 31.7 %all-gather = f32[64,1024]{1,0:T(8,128)S(1)} all-gather(f32[8,1024]{1,0:T(8,128)} %get-tuple-element.34), channel_id=2, replica_groups=mesh['dp'=4,'mp'=8] {'mp'}, dimensions={0}, use_global_device_ids=true | all-gather | bytes 294912 | tf_op jit(solution)/shard_map/all_gather | solution.py:319
  171.1 17.2 %all-gather.17.cloned.1.call-done.wu_ref = bf16[512,2048]{1,0:T(8,128)(2,1)} async-done(((bf16[512,256]{1,0:T(8,128)(2,1)}), bf16[512,2048]{1,0:T(8,128)(2,1)}) %all-gather.17.cloned.1.call-update) | async-done | bytes 2097168 | tf_op jit(solution)/shard_map/all_gather | solution.py:288
  188.3 49.6 %all-gather.19.cloned.1.call-done.wd_ref = bf16[2048,512]{1,0:T(8,128)(2,1)} async-done(((bf16[256,512]{1,0:T(8,128)(2,1)}), bf16[2048,512]{1,0:T(8,128)(2,1)}) %all-gather.19.cloned.1.call-update) | async-done | bytes 2097168 | tf_op jit(solution)/shard_map/all_gather | solution.py:288
  237.9 57.0 %feed.1 = (bf16[2048,512]{1,0:T(8,128)(2,1)}, f32[2048,1024]{1,0:T(8,128)}, f32[2048,1024]{1,0:T(8,128)}, f32[2048,512]{1,0:T(8,128)}, f32[512,1024]{1,0:T(8,128...) custom-call(bf16[2048,512]{1,0:T(8,128)(2,1)} %bitcast.138, ...), custom_call_target="tpu_custom_call" | custom-call | tf_op jit(solution)/shard_map/feed/pallas_call | solution.py:326
  295.0 1.7 convert_element_type.52
  298.2 3.8 convert_element_type.56
  309.2 31.5 %all-gather.2 = f32[64,1024]{1,0:T(8,128)S(1)} all-gather(f32[8,1024]{1,0:T(8,128)S(1)} %fusion.4), channel_id=4, replica_groups=mesh['dp'=4,'mp'=8] {'mp'}, dimensions={0}, use_global_device_ids=true | all-gather | bytes 294912 | tf_op jit(solution)/shard_map/all_gather | solution.py:354
  342.1 26.3 %back.1 = (f32[2048,512]{1,0:T(8,128)}, f32[512,1024]{1,0:T(8,128)}, f32[512,1024]{1,0:T(8,128)}, f32[8,512]{1,0:T(8,128)}, f32[48,1024]{1,0:T(8,128)}) custom-call(bf16[2048,512]{1,0:T(8,128)(2,1)} %bitcast.139, f32[2048,1024]{1,0:T(8,128)} %get-tuple-element.37.sg_ref, f32[2048,1024]{1,0:T(8,128)} %get-tuple-element.32.g_ref, ...), custom_call_target="tpu_custom_call" | custom-call | tf_op jit(solution)/shard_map/back/pallas_call | solution.py:365
  368.3 1.9 convert_element_type.48
  373.3 4.0 convert_element_type.54
  377.6 2.0 copy.58
  379.6 39.6 %psum.49 = f32[2,512]{1,0:T(2,128)S(1)} all-reduce(f32[2,512]{1,0:T(2,128)S(1)} %pad_maximum_fusion), channel_id=1, replica_groups=mesh['dp'=4,'mp'=8] {'dp','mp'}, use_global_device_ids=true, to_apply=%region_3.4 | all-reduce | flops 1024 | bytes 8192 | tf_op jit(solution)/shard_map/psum | solution.py:383
  421.8 9.9 %reduce-scatter.17.cloned.1.call-done = bf16[512,256]{1,0:T(8,128)(2,1)} async-done(((bf16[512,2048]{1,0:T(8,128)(2,1)}), bf16[512,256]{1,0:T(8,128)(2,1)}) %reduce-scatter.17.cloned.1.call-update) | async-done | bytes 262160 | tf_op jit(solution)/shard_map/reduce_scatter | solution.py:379
  431.7 1.8 convert_bitcast_fusion
  434.1 6.6 copy.57
  440.7 57.1 %reduce-scatter.19.cloned.1.call-done = bf16[128,512]{1,0:T(8,128)(2,1)} async-done(((bf16[1024,512]{1,0:T(8,128)(2,1)}), bf16[128,512]{1,0:T(8,128)(2,1)}) %reduce-scatter.19.cloned.1.call-update) | async-done | bytes 131088
  498.8 64.7 %reduce-scatter.21.cloned.1.call-done = bf16[128,512]{1,0:T(8,128)(2,1)} async-done(((bf16[1024,512]{1,0:T(8,128)(2,1)}), bf16[128,512]{1,0:T(8,128)(2,1)}) %reduce-scatter.21.cloned.1.call-update) | async-done | bytes 131088
  564.6 70.1 %reduce-scatter.15.cloned.1.call-done = bf16[512,256]{1,0:T(8,128)(2,1)} async-done(((bf16[512,2048]{1,0:T(8,128)(2,1)}), bf16[512,256]{1,0:T(8,128)(2,1)}) %reduce-scatter.15.cloned.1.call-update) | async-done | bytes 262160 | tf_op jit(solution)/shard_map/reduce_scatter | solution.py:379
  634.7 56.5 %reduce-scatter.13.cloned.1.call-done = f32[6,128]{1,0:T(8,128)} async-done(((f32[6,1024]{1,0:T(8,128)}), f32[6,128]{1,0:T(8,128)}) %reduce-scatter.13.cloned.1.call-update) | async-done | bytes 3088 | tf_op jit(solution)/shard_map/reduce_scatter | solution.py:382
  691.2 34.5 %all-reduce.7 = (f32[512,128]{1,0:T(8,128)}, f32[512,128]{1,0:T(8,128)}, f32[6,128]{1,0:T(8,128)S(1)}, f32[512,256]{1,0:T(8,128)}) all-reduce(bf16[512,128]{1,0:T(8,128)(2,1)S(1)} %copy.47, bf16[512,128]{1,0:T(8,128)(2,1)S(1)} %copy.49, f32[6,128]{1,0:T(8,128)} %reduce-scatter.13.cloned.1.call-done, ...), channel_id=1, replica_groups=mesh['dp'=4,'mp'=8] {'dp'}, use_global_device_ids=true, to_apply=%region_5.6 | all-reduce | flops 262912 | bytes 1579008 | tf_op jit(solution)/shard_map/psum | solution.py:379
  726.8 5.1 all-reduce.6.cloned.1.call-done
  731.9 2.0 copy.45
  734.0 1.8 copy.44
  (95 shorter events, 28.3 us)
Async XLA Ops:
  7.2 14.8 %copy-start.9 = (bf16[512]{0:T(512)(128)(2,1)S(1)}, bf16[512]{0:T(512)(128)(2,1)}, u32[]{:S(2)}) copy-start(bf16[512]{0:T(512)(128)(2,1)} %param.16) | copy-start | bytes 3076
  7.2 15.4 %copy-start.1 = (bf16[8,256,512]{2,1,0:T(8,128)(2,1)S(1)}, bf16[8,256,512]{2,1,0:T(8,128)(2,1)}, u32[]{:S(2)}) copy-start(bf16[8,256,512]{2,1,0:T(8,128)(2,1)} %param.15) | copy-start | bytes 6291460
  7.2 81.8 %all-gather.11.cloned.1.call-start = ((), (), s32[]{:S(2)}) async-start(), calls=%async_computation.6 | async-start | bytes 1179648 | tf_op jit(solution)/shard_map/all_gather | solution.py:288
  7.9 85.2 %all-gather.13.cloned.1.call-start = ((), (), s32[]{:S(2)}) async-start(), calls=%async_computation.7 | async-start | bytes 1179648 | tf_op jit(solution)/shard_map/all_gather | solution.py:288
  8.7 162.4 %all-gather.15.cloned.1.call-start = ((), (), s32[]{:S(2)}) async-start(), calls=%async_computation.8 | async-start | bytes 1179648 | tf_op jit(solution)/shard_map/all_gather | solution.py:288
  9.4 178.9 %all-gather.17.cloned.1.call-start = ((), (), s32[]{:S(2)}) async-start(), calls=%async_computation.9 | async-start | bytes 2359296 | tf_op jit(solution)/shard_map/all_gather | solution.py:288
  10.0 227.9 %all-gather.19.cloned.1.call-start = ((), (), s32[]{:S(2)}) async-start(), calls=%async_computation.10 | async-start | bytes 2359296 | tf_op jit(solution)/shard_map/all_gather | solution.py:288
  10.6 409.4 %reduce-scatter.23.cloned.1.call-start = ((), (), s32[]{:S(2)}) async-start(), calls=%async_computation.16 | async-start | bytes 1179648
  11.5 76.9 %collective-permute-start = (bf16[8,4,512]{2,1,0:T(4,128)(2,1)S(1)}, bf16[8,4,512]{2,1,0:T(4,128)(2,1)S(1)}, u32[]{:S(2)}, u32[]{:S(2)}) collective-permute-start(bf16[8,4,512]{2,1,0:T(4,128)(2,1)S(1)} %slice.152), channel_id=1, source_target_pairs={{0,1},{1,2},{2,3},{3,4},{4,5},{5,6},{6,7},{8,9},{9,10},{10,11},{11... | collective-permute-start | bytes 98312 | tf_op jit(solution)/shard_map/ppermute | solution.py:285
  17.9 7.3 copy-start.10
  17.9 7.9 %copy-start.11 = (f32[128]{0:T(128)S(1)}, f32[128]{0:T(128)}, u32[]{:S(2)}) copy-start(f32[128]{0:T(128)} %param.19) | copy-start | bytes 1540
  17.9 27.0 %copy-start.12 = (f32[128]{0:T(128)S(1)}, f32[128]{0:T(128)}, u32[]{:S(2)}) copy-start(f32[128]{0:T(128)} %param.21) | copy-start | bytes 1540
  17.9 43.7 %copy-start.8 = (f32[4,128]{1,0:T(4,128)S(1)}, f32[4,128]{1,0:T(4,128)}, u32[]{:S(2)}) copy-start(f32[4,128]{1,0:T(4,128)} %param.20) | copy-start | bytes 6148
  298.1 133.6 %reduce-scatter.17.cloned.1.call-start = ((), (), s32[]{:S(2)}) async-start(), calls=%async_computation.13 | async-start | bytes 2359296 | tf_op jit(solution)/shard_map/reduce_scatter | solution.py:379
  298.1 5.0 copy-start.4
  298.1 7.4 copy-start.3
  302.0 195.8 %reduce-scatter.19.cloned.1.call-start = ((), (), s32[]{:S(2)}) async-start(), calls=%async_computation.14 | async-start | bytes 1179648
  307.9 33.5 %collective-permute-start.1 = (f32[6,8,1024]{2,1,0:T(8,128)S(1)}, f32[6,8,1024]{2,1,0:T(8,128)S(1)}, u32[]{:S(2)}, u32[]{:S(2)}) collective-permute-start(f32[6,8,1024]{2,1,0:T(8,128)S(1)} %bitcast_dynamic-update-slice_fusion), channel_id=1, source_target_pairs={{1,0},{2,1},{3,2},{4,3},{5,4},{6,5},{7,6},{9,8},{10,9},{11,10},{12... | collective-permute-start | bytes 589832 | tf_op jit(solution)/shard_map/ppermute | solution.py:362
  368.3 3.3 copy-start
  371.6 191.9 %reduce-scatter.21.cloned.1.call-start = ((), (), s32[]{:S(2)}) async-start(), calls=%async_computation.15 | async-start | bytes 1179648
  373.2 261.5 %reduce-scatter.15.cloned.1.call-start = ((), (), s32[]{:S(2)}) async-start(), calls=%async_computation.12 | async-start | bytes 2359296 | tf_op jit(solution)/shard_map/reduce_scatter | solution.py:379
  373.3 4.3 copy-start.6
  373.3 4.3 copy-start.2
  377.2 2.3 copy-start.7
  377.2 42.0 %copy-start.5 = (f32[48,1024]{1,0:T(8,128)S(1)}, f32[48,1024]{1,0:T(8,128)}, u32[]{:S(2)}) copy-start(f32[48,1024]{1,0:T(8,128)} %get-tuple-element.48) | copy-start | bytes 589828
  377.3 313.9 %reduce-scatter.13.cloned.1.call-start = ((), (), s32[]{:S(2)}) async-start(), calls=%async_computation.11 | async-start | bytes 36864 | tf_op jit(solution)/shard_map/reduce_scatter | solution.py:382
  419.9 312.0 %all-reduce.6.cloned.1.call-start = ((), (), s32[]{:S(2)}) async-start(), calls=%async_computation.17 | async-start | bytes 1572864 | tf_op jit(solution)/shard_map/psum | solution.py:379
Sparse Core Ops, SparseCore 0:
  10.1 42.2 all-gather.10
  54.4 38.6 all-gather.12
  95.3 40.3 all-gather.14
  137.6 50.6 all-gather.16
  190.3 47.6 all-gather.18
  298.2 62.5 reduce-scatter.22
  364.7 66.9 reduce-scatter.16
  435.4 62.3 reduce-scatter.18
  501.2 62.2 reduce-scatter.20
  567.3 67.3 reduce-scatter.14
  638.7 52.4 reduce-scatter.12
  694.2 37.7 all-reduce.5

commit v2 on v1

v2 whole, which is shorter than its diff:
```python
import functools

import jax
import jax.numpy as jnp
from jax import lax
from jax.experimental import pallas as pl
from jax.experimental.pallas import tpu as pltpu
from jax.sharding import PartitionSpec as P

KW = 4
NORM_EPS = 1e-06
BP = 32
CT = 256
FT = 512
MIB = 2**20
F32 = jnp.float32
BF16 = jnp.bfloat16
MESH = pl.DeviceIdType.MESH
ANY = pl.BlockSpec(memory_space=pl.ANY)

ERF_A = (0.254829592, -0.284496736, 1.421413741, -1.453152027, 1.061405429)
ERF_P = 0.3275911 * 0.7071067811865476
INV_ROOT_TWO_PI = 0.3989422804014327


def gelu_parts(x):
    t = 1.0 / (1.0 + ERF_P * jnp.abs(x))
    e = jnp.exp(-0.5 * (x * x))
    poly = 0.5 * ERF_A[4]
    for a in (ERF_A[3], ERF_A[2], ERF_A[1], ERF_A[0]):
        poly = poly * t + 0.5 * a
    tail = poly * t * e
    cdf = jnp.where(x >= 0, 1.0 - tail, tail)
    return x * cdf, cdf + x * (e * INV_ROOT_TWO_PI)


def dist_of(bounds_ref, first, count):
    place = (lax.broadcasted_iota(jnp.int32, (count, 8, 128), 0) + first).astype(F32)
    start = jnp.zeros((count, 8, 128), F32)
    for s in range(bounds_ref.shape[0]):
        b = bounds_ref[s][None]
        start = jnp.where(b <= place, jnp.maximum(start, b), start)
    return (place - start).reshape(count * 8, 128)


def wide(d, width=CT):
    return jnp.concatenate([d] * (width // 128), axis=1)


def dot(a, b):
    return jnp.dot(a, b, preferred_element_type=F32)


def dot_nt(a, b):
    return lax.dot_general(a, b, (((1,), (1,)), ((), ())), preferred_element_type=F32)


def dot_tn(a, b):
    return lax.dot_general(a, b, (((0,), (0,)), ((), ())), preferred_element_type=F32)


class Place:
    def __init__(self):
        self.n_mp, self.n_dp = lax.axis_size("mp"), lax.axis_size("dp")
        self.n_a = self.n_mp // 2
        self.dp, self.mp = lax.axis_index("dp"), lax.axis_index("mp")
        self.a, self.b = self.mp // 2, self.mp % 2
        self.y, self.c = (self.dp // 2) % 2, self.dp % 2
        self.base = self.dp - self.y * 2 - self.c
        self.q = self.y * 2 + self.c

    def line(self, da):
        return (self.dp, lax.rem(self.a + da + self.n_a, self.n_a) * 2 + self.b)

    def pair(self):
        return (self.dp, self.a * 2 + 1 - self.b)

    def beside(self):
        return (self.base + (1 - self.y) * 2 + self.c, self.mp)

    def twin(self):
        return (self.base + self.y * 2 + 1 - self.c, self.mp)

    def across(self):
        return (self.base + (1 - self.y) * 2 + 1 - self.c, self.mp)

    def other(self, dm):
        return (self.dp, lax.rem(self.mp + dm, self.n_mp))

    def partners(self):
        return [self.twin(), self.beside(), self.across()] + [self.other(dm) for dm in range(1, self.n_mp)]

    def barrier(self):
        bar = pltpu.get_barrier_semaphore()
        devices = self.partners()
        for d in devices:
            pl.semaphore_signal(bar, inc=1, device_id=d, device_id_type=MESH)
        pl.semaphore_wait(bar, len(devices))


def remote(src, dst, send, recv, device):
    return pltpu.make_async_remote_copy(src_ref=src, dst_ref=dst, send_sem=send, recv_sem=recv, device_id=device, device_id_type=MESH)


class Gather:
    def __init__(self, here, wall, first, rows, send, recv):
        self.h, self.wall, self.first, self.rows, self.send, self.recv = here, wall, first, rows, send, recv
        n_a = here.n_a
        self.z0, self.x0, self.y0, self.t0 = 0, n_a, 2 * n_a, 4 * n_a
        self.used = []

    def span(self, shard, q):
        n = self.rows // 4
        return self.wall.at[pl.ds(pl.multiple_of(self.first + shard * self.rows + q * n, 16), n)]

    def move(self, sem, shard, q, device):
        s = self.span(shard, q)
        remote(s, s, self.send.at[sem], self.recv.at[sem], device).start()
        self.used.append(sem)

    def landed(self, sem, shard, q):
        s = self.span(shard, q)
        remote(s, s, self.send.at[sem], self.recv.at[sem], self.h.pair()).wait_recv()

    def shard(self, da, other):
        h = self.h
        return lax.rem(h.a - da + h.n_a, h.n_a) * 2 + ((1 - h.b) if other else h.b)

    def slot(self, da, other):
        return 2 * da + (1 if other else 0)

    def open(self):
        h = self.h
        self.move(self.x0, h.mp, h.q, h.pair())
        for da in range(1, h.n_a):
            self.move(self.z0 + da, h.mp, h.q, h.line(da))

    def spread(self, da, other):
        h, s = self.h, self.shard(da, other)
        self.move(self.y0 + self.slot(da, other), s, h.q, h.beside())
        self.move(self.t0 + 2 * self.slot(da, other), s, h.q, h.twin())

    def from_line(self, da):
        h = self.h
        self.landed(self.z0 + da, self.shard(da, False), h.q)
        self.move(self.x0 + da, self.shard(da, False), h.q, h.pair())
        self.spread(da, False)

    def from_pair(self, da):
        self.landed(self.x0 + da, self.shard(da, True), self.h.q)
        self.spread(da, True)

    def from_beside(self, da, other):
        h, s = self.h, self.shard(da, other)
        q = (1 - h.y) * 2 + h.c
        self.landed(self.y0 + self.slot(da, other), s, q)
        self.move(self.t0 + 2 * self.slot(da, other) + 1, s, q, h.twin())

    def from_twin(self, da, other):
        h, s = self.h, self.shard(da, other)
        self.landed(self.t0 + 2 * self.slot(da, other), s, h.y * 2 + 1 - h.c)
        self.landed(self.t0 + 2 * self.slot(da, other) + 1, s, (1 - h.y) * 2 + 1 - h.c)

    def close(self):
        s = self.wall.at[pl.ds(self.first, self.rows // 4)]
        for sem in self.used:
            remote(s, s, self.send.at[sem], self.recv.at[sem], self.h.pair()).wait_send()


def front_kernel(span, x_ref, cot_ref, wv_in, wg_in, wo_in, wu_in, wd_in, small_in, gain1_ref, gain2_ref, bounds_ref,
                 out_ref, sg_ref, rg_ref, dgain_ref, acc_ref, c2_ref, aend_ref, send_ref, g_out, z_out, v_out, wv_out, wg_out,
                 du_out, dd_out, do_out,
                 wall, nbuf, gsc, msc, vsc, vbuf, gbuf, dbuf, smalls, halo, carry, state_ref, stb, hp, dh, hb, hg,
                 dwo, dwu, dwd, stage, w_send, w_recv, s_send, s_recv, h_sem, c_send, c_recv, l_sem, z_sem, st_sem):
    here = Place()
    n_mp, n_a = here.n_mp, here.n_a
    dim = x_ref.shape[1]
    local_c, local_f = wv_in.shape[1], wu_in.shape[1]
    width, units = local_c * n_mp, local_f * n_mp
    tile_c = 2 * local_c
    rows = BP * 8
    blocks = span // BP
    step = pl.program_id(0)
    sections, first = {}, 0
    for k, (name, count) in enumerate((("wu", local_f), ("wd", local_f), ("wv", local_c), ("wg", local_c), ("wo", local_c))):
        sections[name] = Gather(here, wall, first, count, w_send.at[k], w_recv.at[k])
        first += count * n_mp
    wv, wg, wo, wu, wd = (sections[name] for name in ("wv", "wg", "wo", "wu", "wd"))
    far = range(1, n_a)

    def tile_of(da):
        return lax.rem(here.a - da + n_a, n_a)

    def small_copy(dm):
        return remote(smalls.at[here.mp], smalls.at[here.mp], s_send.at[dm], s_recv.at[dm], here.other(dm))

    def halo_copy():
        return remote(x_ref.at[pl.ds(span * 8 - 32, 32)], halo, h_sem.at[0], h_sem.at[1], here.other(1))

    def carry_copy(dm, t):
        lanes = pl.ds(pl.multiple_of(tile_of(t) * tile_c, tile_c), tile_c)
        block = carry.at[here.mp, :, lanes]
        return remote(block, block, c_send.at[dm, t], c_recv.at[dm, t], (here.dp, here.mp + dm))

    def local_copies():
        own = [pltpu.make_async_copy(gsc, g_out, l_sem.at[0]), pltpu.make_async_copy(vsc, v_out, l_sem.at[1])]
        own += [pltpu.make_async_copy(wall.at[pl.ds(s.first, width)], o, l_sem.at[2 + i]) for i, (s, o) in enumerate(((wv, wv_out), (wg, wg_out)))]
        return own

    def z_copy(i):
        at = pl.ds(pl.multiple_of(i * rows, rows), rows)
        return pltpu.make_async_copy(msc.at[at], z_out.at[at], z_sem.at[i])

    def normed(x):
        x = x.astype(F32)
        inv = lax.rsqrt(jnp.mean(x * x, axis=1, keepdims=True) + NORM_EPS)
        return (x * inv * gain1_ref[...]).astype(BF16)

    @pl.when(step == 0)
    def _():
        here.barrier()
        for s, w, turn in ((wv, wv_in, True), (wg, wg_in, True), (wo, wo_in, False), (wu, wu_in, True), (wd, wd_in, False)):
            block = w[...].astype(F32)
            block = block.T if turn else block
            wall[pl.ds(pl.multiple_of(s.first + here.mp * s.rows, 16), s.rows)] = block.astype(BF16)
            if s is wg:
                wv.open()
                wg.open()
        smalls[here.mp] = small_in[...]
        halo_copy().start()
        for dm in range(1, n_mp):
            small_copy(dm).start()

        @pl.loop(0, blocks)
        def _(i):
            nbuf[pl.ds(pl.multiple_of(32 + i * rows, 16), rows)] = normed(x_ref[pl.ds(pl.multiple_of(i * rows, rows), rows)])

        halo_copy().wait_recv()
        nbuf[0:32] = normed(halo[...])
        for dm in range(1, n_mp):
            small_copy(dm).wait_recv()
        for s in (wv, wg):
            s.from_pair(0)
        for da in far:
            for s in (wv, wg):
                s.from_line(da)
        for s in (wo, wu, wd):
            s.open()
        for s in (wv, wg):
            s.from_beside(0, True)

    @pl.when(step < n_a)
    def _():
        for s in (wv, wg):
            s.from_twin(step, True)

            @pl.when(step > 0)
            def _():
                s.from_twin(step, False)

        tile = tile_of(step)
        lanes = pl.ds(pl.multiple_of(tile * tile_c, tile_c), tile_c)
        wv_t = wall[pl.ds(pl.multiple_of(wv.first + tile * tile_c, tile_c), tile_c)]
        wg_t = wall[pl.ds(pl.multiple_of(wg.first + tile * tile_c, tile_c), tile_c)]
        small = jnp.concatenate([smalls[2 * tile, :, 0:local_c], smalls[2 * tile + 1, :, 0:local_c]], axis=1)
        taps = [jnp.broadcast_to(small[j : j + 1], (8, tile_c)) for j in range(KW)]
        bias = jnp.broadcast_to(small[KW : KW + 1], (8, tile_c))
        cb = jnp.broadcast_to(small[KW + 1 : KW + 2], (8, tile_c))
        vbuf[0:32] = dot_nt(nbuf[0:32], wv_t)

        def body(i, held):
            state, decay = held
            at = pl.ds(pl.multiple_of(32 + i * rows, 16), rows)
            vbuf[32 : 32 + rows] = dot_nt(nbuf[at], wv_t)
            gbuf[...] = dot_nt(nbuf[at], wg_t)
            dbuf[0:rows] = dist_of(bounds_ref, here.mp * span + i * BP, BP)
            v1, v2, v3 = vbuf[24:32], vbuf[16:24], vbuf[8:16]
            values = []
            for p in range(BP):
                at = slice(8 * p, 8 * p + 8)
                out_at = pl.ds(pl.multiple_of(i * rows + 8 * p, 8), 8)
                v0 = vbuf[32 + 8 * p : 40 + 8 * p]
                gate = jax.nn.sigmoid(gbuf[at] + bias)
                d = wide(dbuf[at], tile_c)
                mixed = cb + taps[0] * v0
                mixed = mixed + jnp.where(d >= 1.0, taps[1] * v1, 0.0)
                mixed = mixed + jnp.where(d >= 2.0, taps[2] * v2, 0.0)
                mixed = mixed + jnp.where(d >= 3.0, taps[3] * v3, 0.0)
                linked = jnp.where(d >= 1.0, state, 0.0)
                state = linked + gate * (mixed - linked)
                decay = jnp.where(d >= 1.0, decay * (1.0 - gate), 0.0)
                gsc[out_at, lanes] = gate
                msc[out_at, lanes] = mixed
                values.append(v0)
                if p % 2:
                    pair_at = pl.ds(pl.multiple_of(i * rows + 8 * p - 8, 16), 16)
                    vsc[pair_at, lanes] = jnp.concatenate(values, axis=0).astype(BF16)
                    values = []
                v1, v2, v3 = v0, v1, v2
            vbuf[0:32] = vbuf[rows : rows + 32]
            return state, decay

        state, decay = lax.fori_loop(0, blocks, body, (jnp.zeros((8, tile_c), F32), jnp.ones((8, tile_c), F32)))
        carry[here.mp, 0:8, lanes] = state
        carry[here.mp, 8:16, lanes] = decay
        for dm in range(1, n_mp):

            @pl.when(here.mp + dm < n_mp)
            def _():
                carry_copy(dm, step).start()

        @pl.when(step == 0)
        def _():
            for da in far:
                for s in (wv, wg):
                    s.from_pair(da)
            for s in (wv, wg):
                for da in far:
                    s.from_beside(da, False)
            for s in (wv, wg):
                for da in far:
                    s.from_beside(da, True)

        @pl.when(step == min(1, n_a - 1))
        def _():
            wo.from_pair(0)
            for da in far:
                wo.from_line(da)
            for da in far:
                wo.from_pair(da)

        @pl.when(step == min(2, n_a - 1))
        def _():
            wo.from_beside(0, True)
            for da in far:
                wo.from_beside(da, False)
                wo.from_beside(da, True)
            wu.from_pair(0)
            for da in far:
                wu.from_line(da)

        @pl.when(step == min(3, n_a - 1))
        def _():
            for da in far:
                wu.from_pair(da)
            wu.from_beside(0, True)
            for da in far:
                wu.from_beside(da, False)
            wd.from_pair(0)
            for da in far:
                wd.from_line(da)

    @pl.when(step == n_a)
    def _():
        for da in far:
            wd.from_pair(da)
        for da in far:
            wu.from_beside(da, True)
        wd.from_beside(0, True)
        for da in far:
            wd.from_beside(da, False)
            wd.from_beside(da, True)
        for dm in range(1, n_mp):

            @pl.when(here.mp - dm >= 0)
            def _():
                for t in range(n_a):
                    carry_copy(dm, t).wait_recv()

        start = jnp.zeros((8, width), F32)
        state_ref[...] = lax.fori_loop(0, here.mp, lambda i, s: carry[i, 0:8] + carry[i, 8:16] * s, start)
        for s in (wo, wu, wd):
            s.from_twin(0, True)
            for da in far:
                s.from_twin(da, True)
                s.from_twin(da, False)
        for copy in local_copies():
            copy.start()
        dwo[...] = jnp.zeros_like(dwo)
        dwu[...] = jnp.zeros_like(dwu)
        dwd[...] = jnp.zeros_like(dwd)
        dgain_ref[...] = jnp.zeros_like(dgain_ref)
        acc_ref[...] = jnp.zeros_like(acc_ref)
        c2_ref[...] = jnp.ones_like(c2_ref)
        aend_ref[...] = carry[here.mp, 8:16]
        send_ref[...] = carry[here.mp, 0:8]

    @pl.when(step >= n_a)
    def _():
        i = step - n_a
        base = pl.multiple_of(i * rows, rows)
        place0 = here.mp * span + i * BP
        dbuf[0:rows] = dist_of(bounds_ref, place0, BP)
        for c in range(0, width, CT):
            lanes = slice(c, c + CT)
            state = state_ref[:, lanes]
            for p in range(0, BP, 2):
                pair = []
                for q in (p, p + 1):
                    at = pl.ds(pl.multiple_of(base + 8 * q, 8), 8)
                    linked = jnp.where(wide(dbuf[8 * q : 8 * q + 8]) >= 1.0, state, 0.0)
                    z = msc[at, lanes] - linked
                    state = linked + gsc[at, lanes] * z
                    msc[at, lanes] = z
                    pair.append(state)
                stb[8 * p : 8 * p + 16, lanes] = jnp.concatenate(pair, axis=0).astype(BF16)
            state_ref[:, lanes] = state
        z_copy(i).start()

        def part(s, lo=0, hi=None):
            return wall[s.first + lo : s.first + (s.rows * n_mp if hi is None else hi)]

        gain = gain2_ref[...]
        place = (lax.broadcasted_iota(jnp.int32, (BP, 8, 128), 0) + place0).astype(F32)
        last = bounds_ref.shape[0] - 1
        inside = jnp.where(place < bounds_ref[last][None], 1.0, 0.0).reshape(rows, 128)[:, 0:1]
        residual = x_ref[pl.ds(base, rows)].astype(F32) + dot(stb[...], part(wo))
        resid = residual.astype(BF16).astype(F32)
        inv = lax.rsqrt(jnp.mean(resid * resid, axis=1, keepdims=True) + NORM_EPS)
        unit = resid * inv
        n2 = (unit * gain).astype(BF16)
        grad_out = cot_ref[...].astype(F32) * inside
        fg = grad_out.astype(BF16)
        for f in range(0, units, FT):
            cols = slice(f, f + FT)
            hp[...] = dot_nt(n2, part(wu, f, f + FT))
            dh[...] = dot_nt(fg, part(wd, f, f + FT))
            for r in range(0, rows, 16):
                at = slice(r, r + 16)
                hidden, slope = gelu_parts(hp[at])
                hb[at, cols] = hidden.astype(BF16)
                hg[at, cols] = (dh[at] * slope).astype(BF16)
        feed_out = dot(hb[...], part(wd))
        out_ref[...] = ((residual + feed_out) * inside).astype(BF16)
        ngrad = dot(hg[...], part(wu))
        dwd[...] += dot_tn(fg, hb[...])
        dwu[...] += dot_tn(n2, hg[...])
        weighted = ngrad * gain
        inner = jnp.mean(weighted * unit, axis=1, keepdims=True)
        rgrad = grad_out + inv * (weighted - unit * inner)
        rg_ref[...] = rgrad
        dgain_ref[...] += jnp.sum((ngrad * unit).reshape(BP, 8, -1), axis=0)
        mix = rgrad.astype(BF16)
        dwo[...] += dot_tn(mix, stb[...])
        sg_ref[...] = dot_nt(mix, part(wo))
        for c in range(0, width, CT):
            lanes = slice(c, c + CT)
            acc, decay = acc_ref[:, lanes], c2_ref[:, lanes]
            for p in range(BP):
                at = slice(8 * p, 8 * p + 8)
                gate = gsc[pl.ds(pl.multiple_of(base + 8 * p, 8), 8), lanes]
                keep = jnp.where(wide(dbuf[at]) >= 1.0, 1.0 - gate, 0.0)
                if p < 3:
                    keep = jnp.where(i == 0, 1.0, keep)
                decay = decay * keep
                term = decay * sg_ref[at, lanes]
                if p < 2:
                    term = jnp.where(i == 0, 0.0, term)
                acc = acc + term
            acc_ref[:, lanes], c2_ref[:, lanes] = acc, decay

    @pl.when(step == n_a + blocks - 1)
    def _():
        for copy in local_copies():
            copy.wait()
        for i in range(blocks):
            z_copy(i).wait()
        for s in (wv, wg, wo, wu, wd):
            s.close()
        halo_copy().wait_send()
        for dm in range(1, n_mp):
            small_copy(dm).wait_send()

            @pl.when(here.mp + dm < n_mp)
            def _():
                for t in range(n_a):
                    carry_copy(dm, t).wait_send()

        k = 0
        for acc, out, local in ((dwu, du_out, local_f), (dwd, dd_out, local_f), (dwo, do_out, local_c)):
            for s in range(n_mp):
                def move(j, ref, out=out, local=local, s=s):
                    return pltpu.make_async_copy(ref.at[:, 0 : out.shape[2]], out.at[s], st_sem.at[j])
                if k >= 2:
                    st_prev[k % 2]().wait()
                else:
                    st_prev = [None, None] if k == 0 else st_prev
                stage[k % 2, :, 0:local] = acc[:, s * local : (s + 1) * local].astype(BF16)
                copy = functools.partial(move, k % 2, stage.at[k % 2])
                copy().start()
                st_prev[k % 2] = copy
                k += 1
        for copy in st_prev:
            copy().wait()


def back_kernel(span, blocks, x_ref, sg_ref, g_ref, z_ref, v_ref, rg_ref, u0_ref, gn_ref, wv_ref, wg_ref, gain_ref, taps_ref,
                bounds_ref, tg_ref, dwv_ref, dwg_ref, dgain_ref, sums_ref, u_ref, gdel, dbuf, vg, gpg):
    step = pl.program_id(0)
    rows = BP * 8
    width = wv_ref.shape[0]

    @pl.when(step == 0)
    def _():
        u_ref[...] = u0_ref[...]
        gdel[...] = gn_ref[...]
        dwv_ref[...] = jnp.zeros_like(dwv_ref)
        dwg_ref[...] = jnp.zeros_like(dwg_ref)
        dgain_ref[...] = jnp.zeros_like(dgain_ref)
        sums_ref[...] = jnp.zeros_like(sums_ref)

    first = lax.axis_index("mp") * span + (blocks - 1 - step) * BP
    dbuf[...] = dist_of(bounds_ref, first, BP + 4)
    for c in range(0, width, CT):
        lanes = slice(c, c + CT)
        taps = [jnp.broadcast_to(taps_ref[j : j + 1, lanes], (8, CT)) for j in range(KW)]
        u = u_ref[:, lanes]
        g1, g2, g3 = (gdel[8 * i : 8 * i + 8, lanes] for i in range(3))
        sums = [sums_ref[8 * i : 8 * i + 8, lanes] for i in range(KW + 2)]
        for p in range(BP - 2, -2, -2):
            vals = v_ref[8 * p : 8 * p + 16, lanes].astype(F32)
            vgs, gpgs = [None, None], [None, None]
            for k in (1, 0):
                q = p + k
                at = slice(8 * q, 8 * q + 8)
                gate = g_ref[at, lanes]
                carried = sg_ref[at, lanes] + u
                g0 = carried * gate
                gp = g0 * z_ref[at, lanes] * (1.0 - gate)
                u = jnp.where(wide(dbuf[at]) >= 1.0, carried - g0, 0.0)
                h1 = jnp.where(wide(dbuf[8 * q + 8 : 8 * q + 16]) >= 1.0, g1, 0.0)
                h2 = jnp.where(wide(dbuf[8 * q + 16 : 8 * q + 24]) >= 2.0, g2, 0.0)
                h3 = jnp.where(wide(dbuf[8 * q + 24 : 8 * q + 32]) >= 3.0, g3, 0.0)
                v = vals[8 * k : 8 * k + 8]
                vgs[k] = taps[0] * g0 + taps[1] * h1 + taps[2] * h2 + taps[3] * h3
                gpgs[k] = gp
                for j, h in enumerate((g0, h1, h2, h3)):
                    sums[j] = sums[j] + v * h
                sums[KW] = sums[KW] + g0
                sums[KW + 1] = sums[KW + 1] + gp.astype(BF16).astype(F32)
                g1, g2, g3 = g0, g1, g2
            vg[8 * p : 8 * p + 16, lanes] = jnp.concatenate(vgs, axis=0).astype(BF16)
            gpg[8 * p : 8 * p + 16, lanes] = jnp.concatenate(gpgs, axis=0).astype(BF16)
        u_ref[:, lanes] = u
        for i, g in enumerate((g1, g2, g3)):
            gdel[8 * i : 8 * i + 8, lanes] = g
        for i in range(KW + 2):
            sums_ref[8 * i : 8 * i + 8, lanes] = sums[i]

    gain = gain_ref[...]
    x = x_ref[...].astype(F32)
    inv = lax.rsqrt(jnp.mean(x * x, axis=1, keepdims=True) + NORM_EPS)
    unit = x * inv
    n1 = (unit * gain).astype(BF16)
    dwv_ref[...] += dot_tn(n1, vg[...])
    dwg_ref[...] += dot_tn(n1, gpg[...])
    ngrad = dot(vg[...], wv_ref[...]) + dot(gpg[...], wg_ref[...])
    weighted = ngrad * gain
    inner = jnp.mean(weighted * unit, axis=1, keepdims=True)
    tg_ref[...] = rg_ref[...] + inv * (weighted - unit * inner)
    dgain_ref[...] += jnp.sum((ngrad * unit).reshape(BP, 8, -1), axis=0)


def whole(shape):
    return pl.BlockSpec(shape, lambda i: (0,) * len(shape))


def resident(shape):
    return pl.BlockSpec(shape, lambda i: (0,) * len(shape), pipeline_mode=pl.Buffered(1))


def per_device(tokens, lengths, cotangent, norm1_gain, value_proj, gate_proj, gate_bias, conv_taps, conv_bias, out_proj,
               norm2_gain, up_proj, down_proj):
    rows, span, dim = tokens.shape
    n_mp = lax.axis_size("mp")
    n_a = n_mp // 2
    me = lax.axis_index("mp")
    total = rows * span
    blocks = span // BP
    tile = BP * 8
    local_c, local_f = value_proj.shape[1], up_proj.shape[1]
    width, units = local_c * n_mp, local_f * n_mp

    bounds = [lengths[:, 0]]
    for s in range(1, lengths.shape[1]):
        bounds.append(bounds[-1] + lengths[:, s])
    bounds = jnp.broadcast_to(jnp.stack(bounds, 0).astype(F32)[:, :, None], (lengths.shape[1], rows, 128))

    def time_major(a):
        return jnp.transpose(a, (1, 0, 2)).reshape(-1, a.shape[2])

    def row_major(a):
        return jnp.transpose(a.reshape(span, rows, dim), (1, 0, 2))

    x_tm, cot_tm = time_major(tokens), time_major(cotangent)
    pad_c, pad_f = max(local_c, 128), max(local_f, 128)
    small = jnp.concatenate([conv_taps, gate_bias[None], conv_bias[None], jnp.zeros((2, local_c), F32)], axis=0)
    small = jnp.pad(small, ((0, 0), (0, pad_c - local_c)))
    gain1, gain2 = norm1_gain.astype(F32)[None], norm2_gain.astype(F32)[None]

    def late(w):
        return pl.BlockSpec((tile, w), lambda i: (jnp.maximum(i - n_a, 0), 0))

    def rblk(w):
        return pl.BlockSpec((tile, w), lambda i: (blocks - 1 - i, 0))

    def sds(shape, t=F32):
        return jax.ShapeDtypeStruct(shape, t)

    dma = pltpu.SemaphoreType.DMA
    vmem = pltpu.VMEM
    tile_c = 2 * local_c
    out_tm, sg, rg, dgain2, acc, c2, a_end, s_end, gate, z, vals, wv, wg, dwu, dwd, dwo = pl.pallas_call(
        functools.partial(front_kernel, span),
        grid=(n_a + blocks,),
        in_specs=[resident((total, dim)), late(dim), resident(value_proj.shape), resident(gate_proj.shape), resident(out_proj.shape),
                  resident(up_proj.shape), resident(down_proj.shape), resident(small.shape), resident((1, dim)), resident((1, dim)),
                  resident(bounds.shape)],
        out_specs=[late(dim), late(width), late(dim), resident((8, dim)), resident((8, width)), resident((8, width)),
                   resident((8, width)), resident((8, width)), ANY, ANY, ANY, ANY, ANY, ANY, ANY, ANY],
        out_shape=[sds((total, dim), BF16), sds((total, width)), sds((total, dim)), sds((8, dim)), sds((8, width)), sds((8, width)),
                   sds((8, width)), sds((8, width)), sds((total, width)), sds((total, width)), sds((total, width), BF16),
                   sds((width, dim), BF16), sds((width, dim), BF16), sds((n_mp, dim, pad_f), BF16), sds((n_mp, dim, pad_f), BF16),
                   sds((n_mp, dim, pad_c), BF16)],
        scratch_shapes=[
            vmem((3 * width + 2 * units, dim), BF16), vmem((total + 32, dim), BF16), vmem((total, width), F32), vmem((total, width), F32),
            vmem((total, width), BF16), vmem((tile + 32, tile_c), F32), vmem((tile, tile_c), F32), vmem((tile, 128), F32),
            vmem((n_mp, 8, pad_c), F32), vmem((32, dim), BF16), vmem((n_mp, 16, width), F32), vmem((8, width), F32),
            vmem((tile, width), BF16), vmem((tile, FT), F32), vmem((tile, FT), F32), vmem((tile, units), BF16), vmem((tile, units), BF16),
            vmem((dim, width), F32), vmem((dim, units), F32), vmem((dim, units), F32), vmem((2, dim, pad_f), BF16),
            dma((5, 8 * n_a)), dma((5, 8 * n_a)), dma((n_mp,)), dma((n_mp,)), dma((2,)), dma((n_mp, n_a)), dma((n_mp, n_a)), dma((4,)),
            dma((blocks,)), dma((2,)),
        ],
        compiler_params=pltpu.CompilerParams(collective_id=0, has_side_effects=True, vmem_limit_bytes=60 * MIB),
        name="front",
    )(x_tm, cot_tm, value_proj, gate_proj, out_proj, up_proj, down_proj, small, gain1, gain2, bounds)

    a_all = lax.all_gather(a_end, "mp")
    taps = lax.all_gather(conv_taps, "mp", axis=1, tiled=True)
    first = me * span
    place = (first + jnp.arange(3)).astype(F32)[:, None]
    starts = jnp.concatenate([jnp.zeros_like(bounds[:1, :, 0]), bounds[:, :, 0]], 0)
    link = ~jnp.any(starts[None] == place[:, None], axis=1)
    g3 = gate[: 3 * 8].reshape(3, 8, width)
    k3 = jnp.where(link[:, :, None], 1.0 - g3, 0.0)
    sg2 = sg[: 2 * 8].reshape(2, 8, width)
    acc1 = sg2[1] + k3[2] * acc
    acc0 = sg2[0] + k3[1] * acc1
    c1 = k3[2] * c2
    c0 = k3[1] * c1
    b_all = lax.all_gather(k3[0] * acc0, "mp")
    u = jnp.zeros_like(s_end)
    u0, u_next = u, u
    for i in range(n_mp - 1, 0, -1):
        u_next = jnp.where(me == i - 1, u, u_next)
        u = b_all[i] + a_all[i] * u
        u0 = jnp.where(me == i - 1, u, u0)
    message = jnp.stack([g3[0] * acc0, g3[1] * acc1, g3[2] * acc, g3[0] * c0, g3[1] * c1, g3[2] * c2])
    message = lax.ppermute(message, "mp", [(i + 1, i) for i in range(n_mp - 1)])
    g_next = (message[:3] + message[3:] * u_next).reshape(24, width)

    tg_tm, dwv, dwg, dgain1, sums = pl.pallas_call(
        functools.partial(back_kernel, span, blocks),
        grid=(blocks,),
        in_specs=[rblk(dim), rblk(width), rblk(width), rblk(width), rblk(width), rblk(dim), whole((8, width)), whole((24, width)),
                  whole((width, dim)), whole((width, dim)), whole((1, dim)), whole((KW, width)), whole(bounds.shape)],
        out_specs=[rblk(dim), whole((dim, width)), whole((dim, width)), whole((8, dim)), whole((8 * (KW + 2), width))],
        out_shape=[sds((total, dim)), sds((dim, width)), sds((dim, width)), sds((8, dim)), sds((8 * (KW + 2), width))],
        scratch_shapes=[pltpu.VMEM((8, width), F32), pltpu.VMEM((24, width), F32), pltpu.VMEM((tile + 32, 128), F32),
                        pltpu.VMEM((tile, width), BF16), pltpu.VMEM((tile, width), BF16)],
        compiler_params=pltpu.CompilerParams(vmem_limit_bytes=58 * MIB),
        name="back",
    )(x_tm, sg, gate, z, vals, rg, u0, g_next, wv, wg, gain1, taps, bounds)

    def total_cols(g):
        return lax.psum(lax.psum_scatter(g.astype(BF16), "mp", scatter_dimension=1, tiled=True).astype(F32), "dp")

    def total_first(g):
        return lax.psum(lax.psum_scatter(g, "mp", scatter_dimension=0, tiled=False).astype(F32), "dp")

    sums = jnp.sum(sums.reshape(KW + 2, 8, width), axis=1)
    sums = lax.psum(lax.psum_scatter(sums, "mp", scatter_dimension=1, tiled=True), "dp")
    gains = lax.psum(jnp.stack([dgain1.sum(0), dgain2.sum(0)]), ("dp", "mp"))
    return (
        row_major(out_tm),
        row_major(tg_tm),
        gains[0],
        total_cols(dwv),
        total_cols(dwg),
        sums[KW + 1],
        sums[:KW],
        sums[KW],
        total_first(dwo)[:, :local_c].T,
        gains[1],
        total_first(dwu)[:, :local_f],
        total_first(dwd)[:, :local_f].T,
    )


def solution(mesh):
    in_specs = (
        P("dp", "mp", None),
        P("dp", None),
        P("dp", "mp", None),
        P(),
        P(None, "mp"),
        P(None, "mp"),
        P("mp"),
        P(None, "mp"),
        P("mp"),
        P("mp", None),
        P(),
        P(None, "mp"),
        P("mp", None),
    )
    out_specs = (
        P("dp", "mp", None),
        P("dp", "mp", None),
        P(),
        P(None, "mp"),
        P(None, "mp"),
        P("mp"),
        P(None, "mp"),
        P("mp"),
        P("mp", None),
        P(),
        P(None, "mp"),
        P("mp", None),
    )
    return jax.shard_map(per_device, mesh=mesh, in_specs=in_specs, out_specs=out_specs, check_vma=False)
```

time: 744 us -> 603 us (0.81)
  waiting for transfers between devices: 338 us -> 225 us
  blocking collectives: 232 us -> 156 us
  Pallas kernels: 96.7 us -> 156 us
    all_gather x5 -> x0, waiting for transfers between devices: 70.9 us -> none  [gather(): return lax.all_gather(w, 'mp', axis=axis, tiled=True)]
    all_gather x5 -> x2, blocking collectives: 126 us -> 62.2 us  [the longest x1 31.3 us: per_device(): a_all = lax.all_gather(a_end, 'mp')]
    pallas_call x2 -> x1, Pallas kernels: 70.5 us -> 130 us  [per_device(): pl.pallas_call(functools.partial(front_kernel, span), grid=(n_a + blocks,...]
    unnamed x15 -> x9, waiting for transfers between devices: 125 us -> 89.9 us
    reduce_scatter x2 -> x3, waiting for transfers between devices: 80 us -> 57.5 us  [total_first(): lax.psum_scatter(g, 'mp', scatter_dimension=0, tiled=False).astype(F32)]
    psum x1, waiting for transfers between devices: 5.12 us -> 22.4 us  [total_first(): lax.psum(lax.psum_scatter(g, 'mp', scatter_dimension=0, tiled=False).asty...]
    psum x1, blocking collectives: 34.5 us -> 22.2 us  [total_cols(): lax.psum(lax.psum_scatter(g.astype(BF16), 'mp', scatter_dimension=1, tile...]
    convert_element_type x5 -> x2, other arithmetic: 11.6 us -> 2.08 us  [total_cols(): g.astype(BF16)]
  transfers between devices with their start and end apart: 14 -> 8, of which waited for: 9 -> 5; matrix products, arithmetic and copies ran while one was open for 7% -> 5% of each run, Pallas kernels for 5% -> 4%
where the time goes in v2:
time: 603 us; the launch traced here: 602 us
  waiting for transfers between devices  225 us (37%)
  Pallas kernels  156 us (26%)
  blocking collectives  156 us (26%)
  local copies, waits for them, and re-layouts  29.5 us (5%)
  other arithmetic  19.1 us (3%)
  between operations  14.4 us (2%)
    pallas_call x1, Pallas kernels, per_device(): pl.pallas_call(functools.partial(front_kernel, span), grid=(n_a + blocks,...  130 us
    unnamed x9, waiting for transfers between devices  89.9 us
    reduce_scatter x3, waiting for transfers between devices, total_first(): lax.psum_scatter(g, 'mp', scatter_dimension=0, tiled=False).astype(F32)  57.5 us
    reduce_scatter x1, waiting for transfers between devices, per_device(): lax.psum_scatter(sums, 'mp', scatter_dimension=1, tiled=True)  55.4 us
    psum x1, blocking collectives, per_device(): gains = lax.psum(jnp.stack([dgain1.sum(0), dgain2.sum(0)]), ('dp', 'mp'))  40.1 us
    all_gather x1, blocking collectives, per_device(): a_all = lax.all_gather(a_end, 'mp')  31.3 us
    all_gather x1, blocking collectives, per_device(): b_all = lax.all_gather(k3[0] * acc0, 'mp')  31.1 us
    all_gather x1, blocking collectives, per_device(): taps = lax.all_gather(conv_taps, 'mp', axis=1, tiled=True)  31 us
  transfers between devices with their start and end apart: 8, of which 5 were waited for; matrix products, arithmetic and copies ran while one was open for 5% of the time, Pallas kernels for 4%

profile of v2, /device:TPU:0, one launch (start us, length us, event | category | flops | bytes accessed | tf_op | source)
XLA Modules:
  0.0 601.8 jit_solution(16175620834555097836)
XLA Ops:
  8.1 0.8 bitcast_add_fusion.2
  8.9 1.3 broadcast_in_dim.54
  10.2 1.3 broadcast_in_dim.55
  11.4 4.1 copy.54
  15.5 2.5 copy.53
  19.5 129.8 %front.1 = (bf16[2048,512]{1,0:T(8,128)(2,1)}, f32[2048,1024]{1,0:T(8,128)}, f32[2048,512]{1,0:T(8,128)}, f32[8,512]{1,0:T(8,128)}, f32[8,1024]{1,0:T(8,128)}, /...) custom-call(bf16[2048,512]{1,0:T(8,128)(2,1)} %bitcast.162, ...), custom_call_target="tpu_custom_call" | custom-call | tf_op jit(solution)/shard_map/front/pallas_call | solution.py:613
  151.0 1.0 bitcast_select_fusion
  156.7 1.3 collective-permute-start
  158.0 31.0 %all_gather.19.taps_ref = f32[4,1024]{1,0:T(4,128)} all-gather(f32[4,128]{1,0:T(4,128)S(1)} %copy-done.9), channel_id=1, replica_groups=mesh['dp'=4,'mp'=8] {'mp'}, dimensions={1}, use_global_device_ids=true | all-gather | bytes 18432 | tf_op jit(solution)/shard_map/all_gather | solution.py:639
  189.0 31.1 %all-gather = f32[64,1024]{1,0:T(8,128)S(1)} all-gather(f32[8,1024]{1,0:T(8,128)S(1)} %fusion.10), channel_id=2, replica_groups=mesh['dp'=4,'mp'=8] {'mp'}, dimensions={0}, use_global_device_ids=true | all-gather | bytes 294912 | tf_op jit(solution)/shard_map/all_gather | solution.py:651
  220.0 31.3 %all-gather.1 = f32[64,1024]{1,0:T(8,128)S(1)} all-gather(f32[8,1024]{1,0:T(8,128)S(1)} %copy-done.6), channel_id=3, replica_groups=mesh['dp'=4,'mp'=8] {'mp'}, dimensions={0}, use_global_device_ids=true | all-gather | bytes 294912 | tf_op jit(solution)/shard_map/all_gather | solution.py:638
  252.6 26.5 %back.1 = (f32[2048,512]{1,0:T(8,128)}, f32[512,1024]{1,0:T(8,128)}, f32[512,1024]{1,0:T(8,128)}, f32[8,512]{1,0:T(8,128)}, f32[48,1024]{1,0:T(8,128)}) custom-call(bf16[2048,512]{1,0:T(8,128)(2,1)} %bitcast.163, f32[2048,1024]{1,0:T(8,128)} %get-tuple-element.33.sg_ref, f32[2048,1024]{1,0:T(8,128)} %get-tuple-element.34.g_ref, ...), custom_call_target="tpu_custom_call" | custom-call | tf_op jit(solution)/shard_map/back/pallas_call | solution.py:662
  279.2 1.9 convert_element_type.48
  281.1 1.3 copy.43
  282.7 1.3 copy.45
  284.7 2.0 copy.52
  286.7 6.7 %copy.51 = f32[256,8,512]{2,0,1:T(8,128)} copy(f32[256,8,512]{2,1,0:T(8,128)} %bitcast.166) | data formatting | bytes 8388608 | tf_op jit(solution)/shard_map/reshape | solution.py:593
  294.2 1.6 convert_bitcast_fusion.1
  295.8 1.8 convert_bitcast_fusion
  297.6 57.5 %reduce-scatter.15.cloned.1.call-done = bf16[1,512,256]{2,1,0:T(8,128)(2,1)} async-done(((bf16[8,512,256]{2,1,0:T(8,128)(2,1)}), bf16[1,512,256]{2,1,0:T(8,128)(2,1)}) %reduce-scatter.15.cloned.1.call-update) | async-done | bytes 262160 | tf_op jit(solution)/shard_map/reduce_scatter | solution.py:679
  355.1 1.8 bitcast_convert_fusion
  356.9 40.1 %psum.49 = f32[2,512]{1,0:T(2,128)S(1)} all-reduce(f32[2,512]{1,0:T(2,128)S(1)} %pad_maximum_fusion), channel_id=1, replica_groups=mesh['dp'=4,'mp'=8] {'dp','mp'}, use_global_device_ids=true, to_apply=%region_3.4 | all-reduce | flops 1024 | bytes 8192 | tf_op jit(solution)/shard_map/psum | solution.py:683
  397.6 23.9 %reduce-scatter.19.cloned.1.call-done = bf16[128,512]{1,0:T(8,128)(2,1)} async-done(((bf16[1024,512]{1,0:T(8,128)(2,1)}), bf16[128,512]{1,0:T(8,128)(2,1)}) %reduce-scatter.19.cloned.1.call-update) | async-done | bytes 131088
  421.5 1.0 copy.44
  422.5 64.6 %reduce-scatter.21.cloned.1.call-done = bf16[128,512]{1,0:T(8,128)(2,1)} async-done(((bf16[1024,512]{1,0:T(8,128)(2,1)}), bf16[128,512]{1,0:T(8,128)(2,1)}) %reduce-scatter.21.cloned.1.call-update) | async-done | bytes 131088
  487.1 1.0 copy.46
  488.1 55.4 %reduce-scatter.11.cloned.1.call-done = f32[6,128]{1,0:T(8,128)} async-done(((f32[6,1024]{1,0:T(8,128)}), f32[6,128]{1,0:T(8,128)}) %reduce-scatter.11.cloned.1.call-update) | async-done | bytes 3088 | tf_op jit(solution)/shard_map/reduce_scatter | solution.py:682
  543.5 22.2 %all-reduce.7 = (f32[512,128]{1,0:T(8,128)}, f32[512,128]{1,0:T(8,128)}, f32[6,128]{1,0:T(8,128)S(1)}) all-reduce(bf16[512,128]{1,0:T(8,128)(2,1)S(1)} %copy.44, bf16[512,128]{1,0:T(8,128)(2,1)S(1)} %copy.46, f32[6,128]{1,0:T(8,128)} %reduce-scatter.11.cloned.1.call-done), channel_id=1, replica_groups=mesh['dp'=4,'mp'=8] {'dp'}, use_global_device_ids=true, to_apply=%region_5.6 | all-reduce | flops 131840 | bytes 792576 | tf_op jit(solution)/shard_map/psum | solution.py:676
  566.8 22.4 %all-reduce.6.cloned.1.call-done = (f32[128,512]{0,1:T(8,128)}, f32[512,256]{1,0:T(8,128)}, f32[256,512]{0,1:T(8,128)}) async-done(((f32[128,512]{0,1:T(8,128)}, f32[512,256]{1,0:T(8,128)}, f32[256,512]{0,1:T(8,128)}), (f32[128,512]{0,1:T(8,128)}, f32[512,256]{1,0:T(8,128)}, f32[256,512]{0,1:T(8,128)})) %all-reduce.6.cloned.1.call-update) | async-done | bytes 1310736 | tf_op jit(solution)/shard_map/psum | solution.py:679
  589.2 1.8 copy.41
  591.0 2.0 copy.42
  593.1 1.9 copy.68
  (69 shorter events, 13.3 us)
Async XLA Ops:
  7.2 8.4 %copy-start.1 = (bf16[8,256,512]{2,1,0:T(8,128)(2,1)S(1)}, bf16[8,256,512]{2,1,0:T(8,128)(2,1)}, u32[]{:S(2)}) copy-start(bf16[8,256,512]{2,1,0:T(8,128)(2,1)} %param.15) | copy-start | bytes 6291460
  7.2 287.0 %reduce-scatter.13.cloned.1.call-start = ((), (), s32[]{:S(2)}) async-start(), calls=%async_computation.7 | async-start | bytes 1179648 | tf_op jit(solution)/shard_map/reduce_scatter | solution.py:679
  11.4 6.7 %copy-start.9 = (f32[4,128]{1,0:T(4,128)S(1)}, f32[4,128]{1,0:T(4,128)}, u32[]{:S(2)}) copy-start(f32[4,128]{1,0:T(4,128)} %param.20) | copy-start | bytes 6148
  11.4 6.7 %copy-start.10 = (f32[128]{0:T(128)S(1)}, f32[128]{0:T(128)}, u32[]{:S(2)}) copy-start(f32[128]{0:T(128)} %param.21) | copy-start | bytes 1540
  11.4 6.7 %copy-start.11 = (f32[128]{0:T(128)S(1)}, f32[128]{0:T(128)}, u32[]{:S(2)}) copy-start(f32[128]{0:T(128)} %param.19) | copy-start | bytes 1540
  149.3 2.7 copy-start.4
  149.3 5.0 copy-start.3
  149.3 70.7 %copy-start.6 = (f32[8,1024]{1,0:T(8,128)S(1)}, f32[8,1024]{1,0:T(8,128)}, u32[]{:S(2)}) copy-start(f32[8,1024]{1,0:T(8,128)} %get-tuple-element.39) | copy-start | bytes 98308
  149.4 146.4 %reduce-scatter.17.cloned.1.call-start = ((), (), s32[]{:S(2)}) async-start(), calls=%async_computation.9 | async-start | bytes 2359296 | tf_op jit(solution)/shard_map/reduce_scatter | solution.py:679
  150.1 204.9 %reduce-scatter.15.cloned.1.call-start = ((), (), s32[]{:S(2)}) async-start(), calls=%async_computation.8 | async-start | bytes 2359296 | tf_op jit(solution)/shard_map/reduce_scatter | solution.py:679
  150.9 270.6 %reduce-scatter.19.cloned.1.call-start = ((), (), s32[]{:S(2)}) async-start(), calls=%async_computation.10 | async-start | bytes 1179648
  156.7 95.3 %collective-permute-start = (f32[6,8,1024]{2,1,0:T(8,128)S(1)}, f32[6,8,1024]{2,1,0:T(8,128)S(1)}, u32[]{:S(2)}, u32[]{:S(2)}) collective-permute-start(f32[6,8,1024]{2,1,0:T(8,128)S(1)} %bitcast_dynamic-update-slice_fusion), channel_id=1, source_target_pairs={{1,0},{2,1},{3,2},{4,3},{5,4},{6,5},{7,6},{9,8},{10,9},{11,10},{12... | collective-permute-start | bytes 589832 | tf_op jit(solution)/shard_map/ppermute | solution.py:659
  279.2 3.3 copy-start
  282.5 204.6 %reduce-scatter.21.cloned.1.call-start = ((), (), s32[]{:S(2)}) async-start(), calls=%async_computation.11 | async-start | bytes 1179648
  282.7 2.0 copy-start.2
  282.7 4.0 copy-start.7
  284.1 259.4 %reduce-scatter.11.cloned.1.call-start = ((), (), s32[]{:S(2)}) async-start(), calls=%async_computation.6 | async-start | bytes 36864 | tf_op jit(solution)/shard_map/reduce_scatter | solution.py:682
  286.7 6.7 %copy-start.8 = (f32[8,512]{1,0:T(8,128)S(1)}, f32[8,512]{1,0:T(8,128)}, u32[]{:S(2)}) copy-start(f32[8,512]{1,0:T(8,128)} %get-tuple-element.44) | copy-start | bytes 49156
  286.7 6.7 %copy-start.5 = (f32[48,1024]{1,0:T(8,128)S(1)}, f32[48,1024]{1,0:T(8,128)}, u32[]{:S(2)}) copy-start(f32[48,1024]{1,0:T(8,128)} %get-tuple-element.48) | copy-start | bytes 589828
  294.1 295.1 %all-reduce.6.cloned.1.call-start = ((), (), s32[]{:S(2)}) async-start(), calls=%async_computation.12 | async-start | bytes 2621440 | tf_op jit(solution)/shard_map/psum | solution.py:679
Sparse Core Ops, SparseCore 0:
  149.5 63.6 reduce-scatter.12
  217.2 67.0 reduce-scatter.16
  288.2 66.8 reduce-scatter.14
  358.7 62.6 reduce-scatter.18
  424.7 62.3 reduce-scatter.20
  490.9 52.5 reduce-scatter.10
  546.8 42.3 all-reduce.5

commit v3 on v2

--- a/solution.py
+++ b/solution.py
@@ -67,7 +67,7 @@
         self.a, self.b = self.mp // 2, self.mp % 2
         self.y, self.c = (self.dp // 2) % 2, self.dp % 2
         self.base = self.dp - self.y * 2 - self.c
-        self.q = self.y * 2 + self.c
+        self.q = self.c * 2 + self.y
 
     def line(self, da):
         return (self.dp, lax.rem(self.a + da + self.n_a, self.n_a) * 2 + self.b)
@@ -88,7 +88,8 @@
         return (self.dp, lax.rem(self.mp + dm, self.n_mp))
 
     def partners(self):
-        return [self.twin(), self.beside(), self.across()] + [self.other(dm) for dm in range(1, self.n_mp)]
+        group = [(lax.rem(self.dp + k, self.n_dp), self.mp) for k in range(1, self.n_dp)]
+        return group + [self.other(dm) for dm in range(1, self.n_mp)]
 
     def barrier(self):
         bar = pltpu.get_barrier_semaphore()
@@ -152,14 +153,14 @@
 
     def from_beside(self, da, other):
         h, s = self.h, self.shard(da, other)
-        q = (1 - h.y) * 2 + h.c
+        q = h.c * 2 + 1 - h.y
         self.landed(self.y0 + self.slot(da, other), s, q)
         self.move(self.t0 + 2 * self.slot(da, other) + 1, s, q, h.twin())
 
     def from_twin(self, da, other):
         h, s = self.h, self.shard(da, other)
-        self.landed(self.t0 + 2 * self.slot(da, other), s, h.y * 2 + 1 - h.c)
-        self.landed(self.t0 + 2 * self.slot(da, other) + 1, s, (1 - h.y) * 2 + 1 - h.c)
+        self.landed(self.t0 + 2 * self.slot(da, other), s, (1 - h.c) * 2 + h.y)
+        self.landed(self.t0 + 2 * self.slot(da, other) + 1, s, (1 - h.c) * 2 + 1 - h.y)
 
     def close(self):
         s = self.wall.at[pl.ds(self.first, self.rows // 4)]
@@ -168,9 +169,8 @@
 
 
 def front_kernel(span, x_ref, cot_ref, wv_in, wg_in, wo_in, wu_in, wd_in, small_in, gain1_ref, gain2_ref, bounds_ref,
-                 out_ref, sg_ref, rg_ref, dgain_ref, acc_ref, c2_ref, aend_ref, send_ref, g_out, z_out, v_out, wv_out, wg_out,
-                 du_out, dd_out, do_out,
-                 wall, nbuf, gsc, msc, vsc, vbuf, gbuf, dbuf, smalls, halo, carry, state_ref, stb, hp, dh, hb, hg,
+                 out_ref, sg_ref, rg_ref, dgain_ref, ba_ref, msg_ref, small_out, g_out, z_out, v_out, wv_out, wg_out, f_out,
+                 wall, nbuf, gsc, msc, vsc, vbuf, gbuf, dbuf, smalls, halo, carry, state_ref, acc_ref, c2_ref, sg_head, stb, hp, dh, hb, hg,
                  dwo, dwu, dwd, stage, w_send, w_recv, s_send, s_recv, h_sem, c_send, c_recv, l_sem, z_sem, st_sem):
     here = Place()
     n_mp, n_a = here.n_mp, here.n_a
@@ -382,8 +382,7 @@
         dgain_ref[...] = jnp.zeros_like(dgain_ref)
         acc_ref[...] = jnp.zeros_like(acc_ref)
         c2_ref[...] = jnp.ones_like(c2_ref)
-        aend_ref[...] = carry[here.mp, 8:16]
-        send_ref[...] = carry[here.mp, 0:8]
+        small_out[...] = smalls[...]
 
     @pl.when(step >= n_a)
     def _():
@@ -443,6 +442,10 @@
         mix = rgrad.astype(BF16)
         dwo[...] += dot_tn(mix, stb[...])
         sg_ref[...] = dot_nt(mix, part(wo))
+        @pl.when(i == 0)
+        def _():
+            sg_head[...] = sg_ref[0:16]
+
         for c in range(0, width, CT):
             lanes = slice(c, c + CT)
             acc, decay = acc_ref[:, lanes], c2_ref[:, lanes]
@@ -476,89 +479,425 @@
                 for t in range(n_a):
                     carry_copy(dm, t).wait_send()
 
-        k = 0
-        for acc, out, local in ((dwu, du_out, local_f), (dwd, dd_out, local_f), (dwo, do_out, local_c)):
-            for s in range(n_mp):
-                def move(j, ref, out=out, local=local, s=s):
-                    return pltpu.make_async_copy(ref.at[:, 0 : out.shape[2]], out.at[s], st_sem.at[j])
-                if k >= 2:
-                    st_prev[k % 2]().wait()
-                else:
-                    st_prev = [None, None] if k == 0 else st_prev
-                stage[k % 2, :, 0:local] = acc[:, s * local : (s + 1) * local].astype(BF16)
-                copy = functools.partial(move, k % 2, stage.at[k % 2])
-                copy().start()
-                st_prev[k % 2] = copy
-                k += 1
-        for copy in st_prev:
-            copy().wait()
-
-
-def back_kernel(span, blocks, x_ref, sg_ref, g_ref, z_ref, v_ref, rg_ref, u0_ref, gn_ref, wv_ref, wg_ref, gain_ref, taps_ref,
-                bounds_ref, tg_ref, dwv_ref, dwg_ref, dgain_ref, sums_ref, u_ref, gdel, dbuf, vg, gpg):
-    step = pl.program_id(0)
+        d3 = dist_of(bounds_ref, here.mp * span, 3)
+        for c in range(0, width, CT):
+            lanes = slice(c, c + CT)
+            g3 = [gsc[8 * j : 8 * j + 8, lanes] for j in range(3)]
+            k3 = [jnp.where(wide(d3[8 * j : 8 * j + 8]) >= 1.0, 1.0 - g3[j], 0.0) for j in range(3)]
+            acc2, c2 = acc_ref[:, lanes], c2_ref[:, lanes]
+            acc1, c1 = sg_head[8:16, lanes] + k3[2] * acc2, k3[2] * c2
+            acc0, c0 = sg_head[0:8, lanes] + k3[1] * acc1, k3[1] * c1
+            ba_ref[0:8, lanes] = k3[0] * acc0
+            ba_ref[8:16, lanes] = carry[here.mp, 8:16, lanes]
+            parts = [g3[0] * acc0, g3[1] * acc1, g3[2] * acc2, g3[0] * c0, g3[1] * c1, g3[2] * c2]
+            for j in range(0, 6, 2):
+                msg_ref[8 * j : 8 * j + 16, lanes] = jnp.concatenate(parts[j : j + 2], axis=0).astype(BF16)
+
+        def out_copy(s):
+            return pltpu.make_async_copy(stage.at[s % 2], f_out.at[s], st_sem.at[s % 2])
+
+        for s in range(n_mp):
+            if s >= 2:
+                out_copy(s - 2).wait()
+            for k, (acc, local) in enumerate(((dwu, local_f), (dwd, local_f), (dwo, local_c))):
+                stage[s % 2, :, k * local_f : k * local_f + local] = acc[:, s * local : (s + 1) * local].astype(BF16)
+
+            out_copy(s).start()
+        for s in (n_mp - 2, n_mp - 1):
+            out_copy(s).wait()
+
+
+class Reduce:
+    def __init__(self, here, other_half, own_half, r1, r2, r3, line_slot, da, send, recv):
+        self.h, self.other_half, self.own_half = here, other_half, own_half
+        self.r1, self.r2, self.r3, self.line_slot, self.da, self.send, self.recv = r1, r2, r3, line_slot, da, send, recv
+        self.quarter = r2.shape[1]
+
+    def copy(self, k):
+        h, n = self.h, self.quarter
+        if k == 0:
+            src, dst, device = self.other_half(), self.r1, h.twin()
+        elif k == 1:
+            src, dst, device = self.r1.at[:, pl.ds(pl.multiple_of((1 - h.y) * n, n), n)], self.r2, h.beside()
+        elif k == 2:
+            src, dst, device = self.r2.at[1 - h.b], self.r3, h.pair()
+        else:
+            src, dst, device = self.r3, self.line_slot, h.line(self.da)
+        return remote(src, dst, self.send.at[k], self.recv.at[k], device)
+
+    def add(self, dst, src, rows, shift=0):
+        step = 32
+
+        @pl.loop(0, rows // step)
+        def _(i):
+            at = pl.ds(pl.multiple_of(i * step, step), step)
+            dst[at] = (dst[at].astype(F32) + src[pl.ds(pl.multiple_of(shift + i * step, step), step)].astype(F32)).astype(BF16)
+
+    def step1(self):
+        self.copy(0).start()
+
+    def step2(self):
+        self.copy(0).wait_recv()
+        for s in range(2):
+            self.add(self.r1.at[s], self.own_half().at[s], 2 * self.quarter)
+        self.copy(1).start()
+
+    def step3(self):
+        self.copy(1).wait_recv()
+        for s in range(2):
+            self.add(self.r2.at[s], self.r1.at[s], self.quarter, self.h.y * self.quarter)
+        self.copy(2).start()
+
+    def step4(self):
+        self.copy(2).wait_recv()
+        self.add(self.r3, self.r2.at[self.h.b], self.quarter)
+        if self.da:
+            self.copy(3).start()
+
+    def close(self):
+        for k in range(4 if self.da else 3):
+            self.copy(k).wait_send()
+
+
+class Finish:
+    def __init__(self, here, units, slots, groups, whole_sum, send, recv):
+        self.h, self.units, self.slots, self.groups, self.whole, self.send, self.recv = here, units, slots, groups, whole_sum, send, recv
+        self.n = units[0].quarter
+
+    def rows(self, q):
+        return self.whole.at[pl.ds(pl.multiple_of(q * self.n, self.n), self.n)]
+
+    def copy(self, k):
+        h = self.h
+        part = self.rows(h.q)
+        return remote(part, part, self.send.at[k], self.recv.at[k], (h.twin(), h.beside(), h.across())[k])
+
+    def group_copy(self, k):
+        h = self.h
+        mine = h.dp // 4
+        block = self.groups.at[mine]
+        device = (lax.rem(h.dp + 4 * k, h.n_dp), h.mp)
+        return remote(block, block, self.send.at[2 + k], self.recv.at[2 + k], device)
+
+    def sum_line(self):
+        h = self.h
+        n_groups = h.n_dp // 4
+        for unit in self.units:
+            if unit.da:
+                unit.copy(3).wait_recv()
+        step = 32
+        dst = self.rows(h.q) if n_groups == 1 else self.groups.at[h.dp // 4]
+        own = self.units[-1].r3
+
+        @pl.loop(0, self.n // step)
+        def _(i):
+            at = pl.ds(pl.multiple_of(i * step, step), step)
+            total = own[at].astype(F32)
+            for k in range(h.n_a - 1):
+                total = total + self.slots[k, at].astype(F32)
+            dst[at] = total.astype(BF16)
+
+        if n_groups > 1:
+            for k in range(1, n_groups):
+                self.group_copy(k).start()
+            for k in range(1, n_groups):
+                self.group_copy(k).wait_recv()
+            mine = self.rows(h.q)
+
+            @pl.loop(0, self.n // step)
+            def _(i):
+                at = pl.ds(pl.multiple_of(i * step, step), step)
+                total = self.groups[0, at].astype(F32)
+                for k in range(1, n_groups):
+                    total = total + self.groups[k, at].astype(F32)
+                mine[at] = total.astype(BF16)
+
+        for k in range(3):
+            self.copy(k).start()
+
+    def write(self, out):
+        for k in range(3):
+            self.copy(k).wait_recv()
+        step = 32
+
+        @pl.loop(0, 4 * self.n // step)
+        def _(i):
+            at = pl.ds(pl.multiple_of(i * step, step), step)
+            out[at] = self.whole[at].astype(F32)
+
+    def close(self):
+        for k in range(3):
+            self.copy(k).wait_send()
+        for k in range(1, self.h.n_dp // 4):
+            self.group_copy(k).wait_send()
+
+
+def back_kernel(span, x_ref, small_ref, dgain2_ref, ba_ref, msg_ref, gain_ref, bounds_ref, wv_ref, wg_ref,
+                sg_in, g_in, z_in, v_in, rg_in, f_in,
+                tg_ref, vg_grad, f_grad, small_grad, gain_grad,
+                sgb, gb, zb, vb, vg, gpg, n1t, ngr, dbuf, bar_buf, msg_buf, u0_ref, gn_ref, sm, smr, sm2,
+                st, v1, v2, v3, v4, vw, fown, f1, f2, f3, f4, fw, vgroups, fgroups,
+                e_send, e_recv, in_sem, own_sem, rg_sem, f_send, f_recv, v_send, v_recv, ff_send, ff_recv, vf_send, vf_recv,
+                m_send, m_recv, k_send, k_recv):
+    here = Place()
+    n_mp, n_a, n_dp = here.n_mp, here.n_a, here.n_dp
+    total, dim = x_ref.shape
+    width = wv_ref.shape[0]
+    local_c = width // n_mp
+    tile_c = 2 * local_c
     rows = BP * 8
-    width = wv_ref.shape[0]
-
-    @pl.when(step == 0)
-    def _():
-        u_ref[...] = u0_ref[...]
-        gdel[...] = gn_ref[...]
-        dwv_ref[...] = jnp.zeros_like(dwv_ref)
-        dwg_ref[...] = jnp.zeros_like(dwg_ref)
-        dgain_ref[...] = jnp.zeros_like(dgain_ref)
-        sums_ref[...] = jnp.zeros_like(sums_ref)
-
-    first = lax.axis_index("mp") * span + (blocks - 1 - step) * BP
-    dbuf[...] = dist_of(bounds_ref, first, BP + 4)
-    for c in range(0, width, CT):
-        lanes = slice(c, c + CT)
-        taps = [jnp.broadcast_to(taps_ref[j : j + 1, lanes], (8, CT)) for j in range(KW)]
-        u = u_ref[:, lanes]
-        g1, g2, g3 = (gdel[8 * i : 8 * i + 8, lanes] for i in range(3))
-        sums = [sums_ref[8 * i : 8 * i + 8, lanes] for i in range(KW + 2)]
-        for p in range(BP - 2, -2, -2):
-            vals = v_ref[8 * p : 8 * p + 16, lanes].astype(F32)
-            vgs, gpgs = [None, None], [None, None]
-            for k in (1, 0):
-                q = p + k
-                at = slice(8 * q, 8 * q + 8)
-                gate = g_ref[at, lanes]
-                carried = sg_ref[at, lanes] + u
-                g0 = carried * gate
-                gp = g0 * z_ref[at, lanes] * (1.0 - gate)
-                u = jnp.where(wide(dbuf[at]) >= 1.0, carried - g0, 0.0)
-                h1 = jnp.where(wide(dbuf[8 * q + 8 : 8 * q + 16]) >= 1.0, g1, 0.0)
-                h2 = jnp.where(wide(dbuf[8 * q + 16 : 8 * q + 24]) >= 2.0, g2, 0.0)
-                h3 = jnp.where(wide(dbuf[8 * q + 24 : 8 * q + 32]) >= 3.0, g3, 0.0)
-                v = vals[8 * k : 8 * k + 8]
-                vgs[k] = taps[0] * g0 + taps[1] * h1 + taps[2] * h2 + taps[3] * h3
-                gpgs[k] = gp
-                for j, h in enumerate((g0, h1, h2, h3)):
-                    sums[j] = sums[j] + v * h
-                sums[KW] = sums[KW] + g0
-                sums[KW + 1] = sums[KW + 1] + gp.astype(BF16).astype(F32)
-                g1, g2, g3 = g0, g1, g2
-            vg[8 * p : 8 * p + 16, lanes] = jnp.concatenate(vgs, axis=0).astype(BF16)
-            gpg[8 * p : 8 * p + 16, lanes] = jnp.concatenate(gpgs, axis=0).astype(BF16)
-        u_ref[:, lanes] = u
-        for i, g in enumerate((g1, g2, g3)):
-            gdel[8 * i : 8 * i + 8, lanes] = g
-        for i in range(KW + 2):
-            sums_ref[8 * i : 8 * i + 8, lanes] = sums[i]
-
+    blocks = span // BP
+    half = dim // 2
+    own_rows = pl.ds(pl.multiple_of(here.c * half, half), half)
+    other_rows = pl.ds(pl.multiple_of((1 - here.c) * half, half), half)
+
+    def tile_of(t):
+        return lax.rem(here.a + 1 + t, n_a)
+
+    def lanes_of(t):
+        return pl.ds(pl.multiple_of(tile_of(t) * tile_c, tile_c), tile_c)
+
+    def ba_copy(dm):
+        return remote(ba_ref, bar_buf.at[here.mp], e_send.at[dm], e_recv.at[dm], (here.dp, here.mp - dm))
+
+    def msg_copy():
+        return remote(msg_ref, msg_buf, e_send.at[0], e_recv.at[0], (here.dp, here.mp - 1))
+
+    def inputs(t):
+        slot, lanes = t % 2, lanes_of(t)
+        pairs = ((sg_in, sgb), (g_in, gb), (z_in, zb), (v_in, vb))
+        return [pltpu.make_async_copy(src.at[:, lanes], dst.at[slot], in_sem.at[slot, k]) for k, (src, dst) in enumerate(pairs)]
+
+    def own_copy(t):
+        return pltpu.make_async_copy(f_in.at[pl.ds(pl.multiple_of(2 * tile_of(t), 2), 2), own_rows], fown.at[t], own_sem.at[t])
+
+    rg_copy = pltpu.make_async_copy(rg_in, tg_ref, rg_sem)
+
+    def far(t):
+        return (t + 1) % n_a
+
+    f_units = [
+        Reduce(here, (lambda t=t: f_in.at[pl.ds(pl.multiple_of(2 * tile_of(t), 2), 2), other_rows]), (lambda t=t: fown.at[t]),
+               f1.at[t], f2.at[t], f3.at[t], f4.at[far(t) - 1] if far(t) else None, far(t), f_send.at[t], f_recv.at[t])
+        for t in range(n_a)
+    ]
+    v_units = [
+        Reduce(here, (lambda t=t: st.at[t, :, other_rows]), (lambda t=t: st.at[t, :, own_rows]),
+               v1.at[t], v2.at[t], v3.at[t], v4.at[far(t) - 1] if far(t) else None, far(t), v_send.at[t], v_recv.at[t])
+        for t in range(n_a)
+    ]
+    f_end = Finish(here, f_units, f4, fgroups, fw, ff_send, ff_recv)
+    v_end = Finish(here, v_units, v4, vgroups, vw, vf_send, vf_recv)
+
+    here.barrier()
+    for dm in range(1, n_mp):
+
+        @pl.when(here.mp - dm >= 0)
+        def _():
+            if dm == 1:
+                msg_copy().start()
+            ba_copy(dm).start()
+
+    for copy in inputs(0):
+        copy.start()
+    for unit in f_units:
+        unit.step1()
+    for t in range(n_a):
+        own_copy(t).start()
+    rg_copy.start()
+
+    sm[...] = jnp.zeros_like(sm)
     gain = gain_ref[...]
-    x = x_ref[...].astype(F32)
-    inv = lax.rsqrt(jnp.mean(x * x, axis=1, keepdims=True) + NORM_EPS)
-    unit = x * inv
-    n1 = (unit * gain).astype(BF16)
-    dwv_ref[...] += dot_tn(n1, vg[...])
-    dwg_ref[...] += dot_tn(n1, gpg[...])
-    ngrad = dot(vg[...], wv_ref[...]) + dot(gpg[...], wg_ref[...])
-    weighted = ngrad * gain
-    inner = jnp.mean(weighted * unit, axis=1, keepdims=True)
-    tg_ref[...] = rg_ref[...] + inv * (weighted - unit * inner)
-    dgain_ref[...] += jnp.sum((ngrad * unit).reshape(BP, 8, -1), axis=0)
+    dbuf[...] = dist_of(bounds_ref, here.mp * span, span + 4)
+
+    def unit_of(i):
+        x = x_ref[pl.ds(pl.multiple_of(i * rows, rows), rows)].astype(F32)
+        inv = lax.rsqrt(jnp.mean(x * x, axis=1, keepdims=True) + NORM_EPS)
+        return x * inv, inv
+
+    for i in range(blocks):
+        unit, _ = unit_of(i)
+        n1t[:, i * rows : (i + 1) * rows] = (unit * gain).astype(BF16).astype(F32).T.astype(BF16)
+
+    for t, unit in enumerate(f_units):
+        own_copy(t).wait()
+        unit.step2()
+
+    for dm in range(1, n_mp):
+
+        @pl.when(here.mp + dm < n_mp)
+        def _():
+            if dm == 1:
+                msg_copy().wait_recv()
+            ba_copy(dm).wait_recv()
+
+    zero = jnp.zeros((8, width), F32)
+    last = here.mp >= n_mp - 1
+    u_next = lax.fori_loop(0, n_mp - 2 - here.mp, lambda j, u: bar_buf[n_mp - 1 - j, 0:8] + bar_buf[n_mp - 1 - j, 8:16] * u, zero)
+    right = jnp.minimum(here.mp + 1, n_mp - 1)
+    u0_ref[...] = jnp.where(last, 0.0, bar_buf[right, 0:8] + bar_buf[right, 8:16] * u_next)
+    msg = msg_buf[...].astype(F32)
+    for j in range(3):
+        gn_ref[8 * j : 8 * j + 8] = jnp.where(last, 0.0, msg[8 * j : 8 * j + 8] + msg[24 + 8 * j : 32 + 8 * j] * u_next)
+
+    def tile_pass(t, hook):
+        slot, tile, lanes = t % 2, tile_of(t), lanes_of(t)
+        for copy in inputs(t):
+            copy.wait()
+        if t + 1 < n_a:
+            for copy in inputs(t + 1):
+                copy.start()
+        small = jnp.concatenate([small_ref[2 * tile, :, 0:local_c], small_ref[2 * tile + 1, :, 0:local_c]], axis=1)
+        taps = [jnp.broadcast_to(small[j : j + 1], (8, tile_c)) for j in range(KW)]
+
+        def body(i, held):
+            u, g1, g2, g3 = held[:4]
+            sums = list(held[4:])
+            base = pl.multiple_of((blocks - 1 - i) * rows, rows)
+
+            @pl.when(i == blocks // 2)
+            def _():
+                hook()
+
+            def dist(q, least):
+                return wide(dbuf[pl.ds(pl.multiple_of(base + 8 * q, 8), 8)], tile_c) >= least
+
+            for p in range(BP - 2, -2, -2):
+                pair_at = pl.ds(pl.multiple_of(base + 8 * p, 16), 16)
+                vals = vb[slot, pair_at].astype(F32)
+                vgs, gpgs = [None, None], [None, None]
+                for k in (1, 0):
+                    q = p + k
+                    at = pl.ds(pl.multiple_of(base + 8 * q, 8), 8)
+                    gate = gb[slot, at]
+                    carried = sgb[slot, at] + u
+                    g0 = carried * gate
+                    gp = g0 * zb[slot, at] * (1.0 - gate)
+                    u = jnp.where(dist(q, 1.0), carried - g0, 0.0)
+                    h1 = jnp.where(dist(q + 1, 1.0), g1, 0.0)
+                    h2 = jnp.where(dist(q + 2, 2.0), g2, 0.0)
+                    h3 = jnp.where(dist(q + 3, 3.0), g3, 0.0)
+                    v = vals[8 * k : 8 * k + 8]
+                    vgs[k] = taps[0] * g0 + taps[1] * h1 + taps[2] * h2 + taps[3] * h3
+                    gpgs[k] = gp
+                    for j, h in enumerate((g0, h1, h2, h3)):
+                        sums[j] = sums[j] + v * h
+                    sums[KW + 1] = sums[KW + 1] + g0
+                    sums[KW] = sums[KW] + gp.astype(BF16).astype(F32)
+                    g1, g2, g3 = g0, g1, g2
+                vg[pair_at] = jnp.concatenate(vgs, axis=0).astype(BF16)
+                gpg[pair_at] = jnp.concatenate(gpgs, axis=0).astype(BF16)
+            return (u, g1, g2, g3, *sums)
+
+        start = [u0_ref[:, lanes]] + [gn_ref[8 * j : 8 * j + 8, lanes] for j in range(3)]
+        held = lax.fori_loop(0, blocks, body, (*start, *[jnp.zeros((8, tile_c), F32)] * (KW + 2)))
+        for j in range(KW + 2):
+            sm[j : j + 1, lanes] = jnp.sum(held[4 + j], axis=0, keepdims=True)
+        dv = dot(n1t[...], vg[...]).astype(BF16)
+        dg = dot(n1t[...], gpg[...]).astype(BF16)
+        for s in range(2):
+            cols = slice(s * local_c, (s + 1) * local_c)
+            st[t, s] = jnp.concatenate([dv[:, cols], dg[:, cols]], axis=1)
+        v_units[t].step1()
+        wv_t = wv_ref[pl.ds(pl.multiple_of(tile * tile_c, tile_c), tile_c)]
+        wg_t = wg_ref[pl.ds(pl.multiple_of(tile * tile_c, tile_c), tile_c)]
+
+        @pl.loop(0, blocks)
+        def _(i):
+            at = pl.ds(pl.multiple_of(i * rows, rows), rows)
+            ngrad = dot(vg[at], wv_t) + dot(gpg[at], wg_t)
+            if t > 0:
+                ngrad = ngrad + ngr[at]
+            if t < n_a - 1:
+                ngr[at] = ngrad
+            else:
+                unit, inv = unit_of(i)
+                weighted = ngrad * gain
+                inner = jnp.mean(weighted * unit, axis=1, keepdims=True)
+                tg_ref[at] = tg_ref[at] + inv * (weighted - unit * inner)
+                part = jnp.sum((ngrad * unit).reshape(BP, 8, -1), axis=0)
+                ngr[0:8] = jnp.where(i == 0, part, ngr[0:8] + part)
+
+    stages = [[] for _ in range(2 * n_a)]
+    def later(at, action):
+        stages[min(at, 2 * n_a - 1)].append(action)
+
+    for t in range(n_a):
+        later(2 * t, f_units[t].step3)
+        later(2 * t + 2, f_units[t].step4)
+        later(2 * t + 2, v_units[t].step2)
+        later(2 * t + 3, v_units[t].step3)
+        later(2 * t + 4, v_units[t].step4)
+
+    def run(k):
+        for action in stages[k]:
+            action()
+
+    for t in range(n_a):
+        if t == n_a - 1:
+            rg_copy.wait()
+        tile_pass(t, functools.partial(run, 2 * t))
+        if t < n_a - 1:
+            run(2 * t + 1)
+
+    for k, g in enumerate((ngr[0:8], dgain2_ref[...])):
+        row = jnp.sum(g, axis=0, keepdims=True)
+        for j in range(dim // 128):
+            at = k * (dim // 128) + j
+            sm[at : at + 1, width : width + 128] = row[:, j * 128 : (j + 1) * 128]
+
+    def sm_copy(k):
+        return remote(sm, smr.at[here.dp], m_send.at[k], m_recv.at[k], (lax.rem(here.dp + k, n_dp), here.mp))
+
+    for k in range(1, n_dp):
+        sm_copy(k).start()
+    smr[here.dp] = sm[...]
+    for action in stages[2 * n_a - 1][:-1]:
+        action()
+    for k in range(1, n_dp):
+        sm_copy(k).wait()
+    sm_sum = smr[0]
+    for k in range(1, n_dp):
+        sm_sum = sm_sum + smr[k]
+    sm[...] = sm_sum
+
+    def tile_copies(dm):
+        tile = lax.rem(here.mp + dm, n_mp) // 2
+        lanes = pl.ds(pl.multiple_of(tile * tile_c, tile_c), tile_c)
+        device = here.other(dm)
+        return [remote(sm.at[:, lanes], sm2.at[here.mp, :, pl.ds(0, tile_c)], k_send.at[0, dm], k_recv.at[0, dm], device),
+                remote(sm.at[:, pl.ds(width, 128)], sm2.at[here.mp, :, pl.ds(tile_c, 128)], k_send.at[1, dm], k_recv.at[1, dm], device)]
+
+    for dm in range(1, n_mp):
+        for copy in tile_copies(dm):
+            copy.start()
+    f_end.sum_line()
+    stages[2 * n_a - 1][-1]()
+    v_end.sum_line()
+    own_lanes = pl.ds(pl.multiple_of(here.a * tile_c, tile_c), tile_c)
+    sm2[here.mp] = jnp.concatenate([sm[:, own_lanes], sm[:, width : width + 128]], axis=1)
+    for dm in range(1, n_mp):
+        for copy in tile_copies(dm):
+            copy.wait_recv()
+    last_sum = sm2[0]
+    for m in range(1, n_mp):
+        last_sum = last_sum + sm2[m]
+    small_grad[...] = last_sum[:, 0:tile_c]
+    gain_grad[...] = last_sum[:, tile_c : tile_c + 128]
+    f_end.write(f_grad)
+    v_end.write(vg_grad)
+
+    for unit in f_units + v_units + [f_end, v_end]:
+        unit.close()
+    for dm in range(1, n_mp):
+        for copy in tile_copies(dm):
+            copy.wait_send()
+
+        @pl.when(here.mp - dm >= 0)
+        def _():
+            if dm == 1:
+                msg_copy().wait_send()
+            ba_copy(dm).wait_send()
 
 
 def whole(shape):
@@ -610,24 +949,25 @@
     dma = pltpu.SemaphoreType.DMA
     vmem = pltpu.VMEM
     tile_c = 2 * local_c
-    out_tm, sg, rg, dgain2, acc, c2, a_end, s_end, gate, z, vals, wv, wg, dwu, dwd, dwo = pl.pallas_call(
+    pad = -(-(2 * local_f + local_c) // 128) * 128
+    out_tm, sg, rg, dgain2, ba, msg, smalls, gate, z, vals, wv, wg, f_grads = pl.pallas_call(
         functools.partial(front_kernel, span),
         grid=(n_a + blocks,),
         in_specs=[resident((total, dim)), late(dim), resident(value_proj.shape), resident(gate_proj.shape), resident(out_proj.shape),
                   resident(up_proj.shape), resident(down_proj.shape), resident(small.shape), resident((1, dim)), resident((1, dim)),
                   resident(bounds.shape)],
-        out_specs=[late(dim), late(width), late(dim), resident((8, dim)), resident((8, width)), resident((8, width)),
-                   resident((8, width)), resident((8, width)), ANY, ANY, ANY, ANY, ANY, ANY, ANY, ANY],
-        out_shape=[sds((total, dim), BF16), sds((total, width)), sds((total, dim)), sds((8, dim)), sds((8, width)), sds((8, width)),
-                   sds((8, width)), sds((8, width)), sds((total, width)), sds((total, width)), sds((total, width), BF16),
-                   sds((width, dim), BF16), sds((width, dim), BF16), sds((n_mp, dim, pad_f), BF16), sds((n_mp, dim, pad_f), BF16),
-                   sds((n_mp, dim, pad_c), BF16)],
+        out_specs=[late(dim), late(width), late(dim), resident((8, dim)), resident((16, width)), resident((48, width)),
+                   resident((n_mp, 8, pad_c)), ANY, ANY, ANY, ANY, ANY, ANY],
+        out_shape=[sds((total, dim), BF16), sds((total, width)), sds((total, dim)), sds((8, dim)), sds((16, width)), sds((48, width), BF16),
+                   sds((n_mp, 8, pad_c)), sds((total, width)), sds((total, width)), sds((total, width), BF16),
+                   sds((width, dim), BF16), sds((width, dim), BF16), sds((n_mp, dim, pad), BF16)],
         scratch_shapes=[
             vmem((3 * width + 2 * units, dim), BF16), vmem((total + 32, dim), BF16), vmem((total, width), F32), vmem((total, width), F32),
             vmem((total, width), BF16), vmem((tile + 32, tile_c), F32), vmem((tile, tile_c), F32), vmem((tile, 128), F32),
             vmem((n_mp, 8, pad_c), F32), vmem((32, dim), BF16), vmem((n_mp, 16, width), F32), vmem((8, width), F32),
+            vmem((8, width), F32), vmem((8, width), F32), vmem((16, width), F32),
             vmem((tile, width), BF16), vmem((tile, FT), F32), vmem((tile, FT), F32), vmem((tile, units), BF16), vmem((tile, units), BF16),
-            vmem((dim, width), F32), vmem((dim, units), F32), vmem((dim, units), F32), vmem((2, dim, pad_f), BF16),
+            vmem((dim, width), F32), vmem((dim, units), F32), vmem((dim, units), F32), vmem((2, dim, pad), BF16),
             dma((5, 8 * n_a)), dma((5, 8 * n_a)), dma((n_mp,)), dma((n_mp,)), dma((2,)), dma((n_mp, n_a)), dma((n_mp, n_a)), dma((4,)),
             dma((blocks,)), dma((2,)),
         ],
@@ -635,65 +975,50 @@
         name="front",
     )(x_tm, cot_tm, value_proj, gate_proj, out_proj, up_proj, down_proj, small, gain1, gain2, bounds)
 
-    a_all = lax.all_gather(a_end, "mp")
-    taps = lax.all_gather(conv_taps, "mp", axis=1, tiled=True)
-    first = me * span
-    place = (first + jnp.arange(3)).astype(F32)[:, None]
-    starts = jnp.concatenate([jnp.zeros_like(bounds[:1, :, 0]), bounds[:, :, 0]], 0)
-    link = ~jnp.any(starts[None] == place[:, None], axis=1)
-    g3 = gate[: 3 * 8].reshape(3, 8, width)
-    k3 = jnp.where(link[:, :, None], 1.0 - g3, 0.0)
-    sg2 = sg[: 2 * 8].reshape(2, 8, width)
-    acc1 = sg2[1] + k3[2] * acc
-    acc0 = sg2[0] + k3[1] * acc1
-    c1 = k3[2] * c2
-    c0 = k3[1] * c1
-    b_all = lax.all_gather(k3[0] * acc0, "mp")
-    u = jnp.zeros_like(s_end)
-    u0, u_next = u, u
-    for i in range(n_mp - 1, 0, -1):
-        u_next = jnp.where(me == i - 1, u, u_next)
-        u = b_all[i] + a_all[i] * u
-        u0 = jnp.where(me == i - 1, u, u0)
-    message = jnp.stack([g3[0] * acc0, g3[1] * acc1, g3[2] * acc, g3[0] * c0, g3[1] * c1, g3[2] * c2])
-    message = lax.ppermute(message, "mp", [(i + 1, i) for i in range(n_mp - 1)])
-    g_next = (message[:3] + message[3:] * u_next).reshape(24, width)
-
-    tg_tm, dwv, dwg, dgain1, sums = pl.pallas_call(
-        functools.partial(back_kernel, span, blocks),
-        grid=(blocks,),
-        in_specs=[rblk(dim), rblk(width), rblk(width), rblk(width), rblk(width), rblk(dim), whole((8, width)), whole((24, width)),
-                  whole((width, dim)), whole((width, dim)), whole((1, dim)), whole((KW, width)), whole(bounds.shape)],
-        out_specs=[rblk(dim), whole((dim, width)), whole((dim, width)), whole((8, dim)), whole((8 * (KW + 2), width))],
-        out_shape=[sds((total, dim)), sds((dim, width)), sds((dim, width)), sds((8, dim)), sds((8 * (KW + 2), width))],
-        scratch_shapes=[pltpu.VMEM((8, width), F32), pltpu.VMEM((24, width), F32), pltpu.VMEM((tile + 32, 128), F32),
-                        pltpu.VMEM((tile, width), BF16), pltpu.VMEM((tile, width), BF16)],
-        compiler_params=pltpu.CompilerParams(vmem_limit_bytes=58 * MIB),
+    n_dp = lax.axis_size("dp")
+    groups = n_dp // 4
+    full = pl.BlockSpec(memory_space=pltpu.VMEM)
+    half, quarter = dim // 2, dim // 4
+
+    def buffers(w):
+        return [vmem((n_a, 2, half, w), BF16), vmem((n_a, 2, quarter, w), BF16), vmem((n_a, quarter, w), BF16),
+                vmem((n_a - 1, quarter, w), BF16), vmem((dim, w), BF16)]
+
+    tg_tm, vg_grad, f_grad, small_grad, gain_grad = pl.pallas_call(
+        functools.partial(back_kernel, span),
+        in_specs=[full] * 9 + [ANY] * 6,
+        out_specs=[full] * 5,
+        out_shape=[sds((total, dim)), sds((dim, tile_c)), sds((dim, pad)), sds((8, tile_c)), sds((8, 128))],
+        scratch_shapes=[
+            vmem((2, total, tile_c), F32), vmem((2, total, tile_c), F32), vmem((2, total, tile_c), F32), vmem((2, total, tile_c), BF16),
+            vmem((total, tile_c), BF16), vmem((total, tile_c), BF16), vmem((dim, total), BF16), vmem((total, dim), F32),
+            vmem((total + 32, 128), F32), vmem((n_mp, 16, width), F32), vmem((48, width), BF16), vmem((8, width), F32),
+            vmem((24, width), F32), vmem((8, width + 128), F32), vmem((n_dp, 8, width + 128), F32), vmem((n_mp, 8, tile_c + 128), F32),
+            vmem((n_a, 2, dim, tile_c), BF16), *buffers(tile_c), vmem((n_a, 2, half, pad), BF16), *buffers(pad),
+            vmem((groups, quarter, tile_c), BF16), vmem((groups, quarter, pad), BF16),
+            dma((n_mp,)), dma((n_mp,)), dma((2, 4)), dma((n_a,)), dma, dma((n_a, 4)), dma((n_a, 4)), dma((n_a, 4)), dma((n_a, 4)),
+            dma((2 + groups,)), dma((2 + groups,)), dma((2 + groups,)), dma((2 + groups,)), dma((n_dp,)), dma((n_dp,)),
+            dma((2, n_mp)), dma((2, n_mp)),
+        ],
+        compiler_params=pltpu.CompilerParams(collective_id=1, has_side_effects=True, vmem_limit_bytes=60 * MIB),
         name="back",
-    )(x_tm, sg, gate, z, vals, rg, u0, g_next, wv, wg, gain1, taps, bounds)
-
-    def total_cols(g):
-        return lax.psum(lax.psum_scatter(g.astype(BF16), "mp", scatter_dimension=1, tiled=True).astype(F32), "dp")
-
-    def total_first(g):
-        return lax.psum(lax.psum_scatter(g, "mp", scatter_dimension=0, tiled=False).astype(F32), "dp")
-
-    sums = jnp.sum(sums.reshape(KW + 2, 8, width), axis=1)
-    sums = lax.psum(lax.psum_scatter(sums, "mp", scatter_dimension=1, tiled=True), "dp")
-    gains = lax.psum(jnp.stack([dgain1.sum(0), dgain2.sum(0)]), ("dp", "mp"))
+    )(x_tm, smalls, dgain2, ba, msg, gain1, bounds, wv, wg, sg, gate, z, vals, rg, f_grads)
+
+    gains = gain_grad.reshape(2, dim)
+    mine = lax.dynamic_slice_in_dim(small_grad, (me % 2) * local_c, local_c, 1)
     return (
         row_major(out_tm),
         row_major(tg_tm),
         gains[0],
-        total_cols(dwv),
-        total_cols(dwg),
-        sums[KW + 1],
-        sums[:KW],
-        sums[KW],
-        total_first(dwo)[:, :local_c].T,
+        vg_grad[:, :local_c],
+        vg_grad[:, local_c : 2 * local_c],
+        mine[KW],
+        mine[:KW],
+        mine[KW + 1],
+        f_grad[:, 2 * local_f : 2 * local_f + local_c].T,
         gains[1],
-        total_first(dwu)[:, :local_f],
-        total_first(dwd)[:, :local_f].T,
+        f_grad[:, :local_f],
+        f_grad[:, local_f : 2 * local_f].T,
     )
 
 

time: 603 us -> 234 us (0.39)
  waiting for transfers between devices: 225 us -> 0 us
  blocking collectives: 156 us -> 0 us
  Pallas kernels: 156 us -> 208 us
  other arithmetic: 19.1 us -> 1.84 us
  between operations: 14.4 us -> 0.77 us
  local copies, waits for them, and re-layouts: 29.5 us -> 23 us
    reduce_scatter x4 -> x0, waiting for transfers between devices: 113 us -> none  [the longest x3 57.5 us: total_first(): lax.psum_scatter(g, 'mp', scatter_dimension=0, tiled=False).astype(F32)]
    all_gather x3 -> x0, blocking collectives: 93.3 us -> none  [the longest x1 31.3 us: per_device(): a_all = lax.all_gather(a_end, 'mp')]
    unnamed x9 -> x0, waiting for transfers between devices: 89.9 us -> none
    psum x2 -> x0, blocking collectives: 62.3 us -> none  [the longest x1 40.1 us: per_device(): gains = lax.psum(jnp.stack([dgain1.sum(0), dgain2.sum(0)]), ('dp', 'mp'))]
    pallas_call x1, Pallas kernels: 26.5 us -> 81.7 us  [per_device(): pl.pallas_call(functools.partial(back_kernel, span), in_specs=[full] * 9...]
    psum x1 -> x0, waiting for transfers between devices: 22.4 us -> none  [total_first(): lax.psum(lax.psum_scatter(g, 'mp', scatter_dimension=0, tiled=False).asty...]
    unnamed x31 -> x22, local copies, waits for them, and re-layouts: 11 us -> 1.87 us
    reshape x0 -> x1, local copies, waits for them, and re-layouts: none -> 6.61 us  [time_major(): return jnp.transpose(a, (1, 0, 2)).reshape(-1, a.shape[2])]
  transfers between devices with their start and end apart: 8 -> 0, of which waited for: 5 -> 0; matrix products, arithmetic and copies ran while one was open for 5% -> 0% of each run, Pallas kernels for 4% -> 0%
where the time goes in v3:
time: 234 us
  Pallas kernels  208 us (89%)
  local copies, waits for them, and re-layouts  23 us (10%)
    pallas_call x1, Pallas kernels, per_device(): pl.pallas_call(functools.partial(front_kernel, span), grid=(n_a + blocks,...  126 us
    pallas_call x1, Pallas kernels, per_device(): pl.pallas_call(functools.partial(back_kernel, span), in_specs=[full] * 9...  81.7 us
    reshape x2, local copies, waits for them, and re-layouts, row_major(): return jnp.transpose(a.reshape(span, rows, dim), (1, 0, 2))  10.3 us
    reshape x1, local copies, waits for them, and re-layouts, time_major(): return jnp.transpose(a, (1, 0, 2)).reshape(-1, a.shape[2])  6.61 us

profile of v3, /device:TPU:0, one launch (start us, length us, event | category | flops | bytes accessed | tf_op | source)
XLA Modules:
  0.0 233.8 jit_solution(13531338042505258228)
XLA Ops:
  0.6 0.0 copy-start.5
  0.7 0.0 copy-start.8
  0.7 0.0 copy-start.9
  0.7 0.0 copy-start.6
  0.7 0.0 copy-start.7
  0.7 0.0 copy-start.3
  0.7 6.6 %copy_bitcast_fusion.2 = (bf16[2048,512]{1,0:T(8,128)(2,1)}, bf16[2048,512]{1,0:T(8,128)(2,1)}) fusion(bf16[256,8,512]{2,0,1:T(8,128)(2,1)} %bitcast.47, bf16[256,8,512]{2,0,1:T(8,128)(2,1)} %bitcast.48), kind=kLoop, calls=%fused_computation.2 | loop fusion | bytes 8388608 | tf_op jit(solution)/shard_map/reshape | solution.py:929
  7.3 0.1 pad.7.clone
  7.4 0.0 copy-done.5
  7.4 0.0 copy-done.8
  7.4 0.0 copy-done.9
  7.4 0.7 maximum_maximum_fusion.small_in
  8.1 0.0 copy-done.6
  8.1 0.6 broadcast_in_dim.33
  8.7 0.0 copy-done.7
  8.7 0.6 broadcast_in_dim.34
  9.3 0.7 broadcast_in_dim.32.bounds_ref
  9.9 126.5 %front.1 = (bf16[2048,512]{1,0:T(8,128)(2,1)}, f32[2048,1024]{1,0:T(8,128)}, f32[2048,512]{1,0:T(8,128)}, f32[8,512]{1,0:T(8,128)}, f32[16,1024]{1,0:T(8,128)}, ...) custom-call(bf16[2048,512]{1,0:T(8,128)(2,1)} %get-tuple-element.72., ...), custom_call_target="tpu_custom_call" | custom-call | tf_op jit(solution)/shard_map/front/pallas_call | solution.py:953
  136.4 3.6 %copy.36 = bf16[256,8,512]{2,0,1:T(8,128)(2,1)} copy(bf16[256,8,512]{2,1,0:T(8,128)(2,1)} %bitcast.46) | data formatting | bytes 4194304 | tf_op jit(solution)/shard_map/reshape | solution.py:932
  140.0 81.7 %back.1 = (f32[2048,512]{1,0:T(8,128)}, f32[512,256]{1,0:T(8,128)}, f32[512,640]{1,0:T(8,128)}, f32[8,256]{1,0:T(8,128)}, f32[8,128]{1,0:T(8,128)}) custom-call(bf16[2048,512]{1,0:T(8,128)(2,1)} %get-tuple-element.72.x_ref, f32[8,8,128]{2,1,0:T(8,128)} %get-tuple-element.31.small_ref, f32[8,512]{1,0:T(8,128)} %get-tuple-element.32.dgain2_ref, ...), custom_call_target="tpu_custom_call" | custom-call | tf_op jit(solution)/shard_map/back/pallas_call | solution.py:987
  221.7 6.8 %copy.35 = f32[256,8,512]{2,0,1:T(8,128)} copy(f32[256,8,512]{2,1,0:T(8,128)} %bitcast.44) | data formatting | bytes 8388608 | tf_op jit(solution)/shard_map/reshape | solution.py:932
  228.5 0.0 copy-done.2
  228.5 0.6 slice_bitcast_fusion.2
  229.1 0.0 copy-done.1
  229.1 0.8 fusion
  229.9 0.0 copy-done.4
  229.9 0.5 slice_bitcast_fusion.4
  230.4 0.6 slice.52
  231.0 0.0 copy-done
  231.0 0.8 copy.29
  231.9 0.9 slice_bitcast_fusion
  232.8 1.0 copy.30
  (11 shorter events, 0.1 us)
Async XLA Ops:
  0.6 6.8 %copy-start.5 = (f32[4,128]{1,0:T(4,128)S(1)}, f32[4,128]{1,0:T(4,128)}, u32[]{:S(2)}) copy-start(f32[4,128]{1,0:T(4,128)} %param.20) | copy-start | bytes 6148
  0.7 6.7 %copy-start.8 = (f32[128]{0:T(128)S(1)}, f32[128]{0:T(128)}, u32[]{:S(2)}) copy-start(f32[128]{0:T(128)} %param.21) | copy-start | bytes 1540
  0.7 6.7 %copy-start.9 = (f32[128]{0:T(128)S(1)}, f32[128]{0:T(128)}, u32[]{:S(2)}) copy-start(f32[128]{0:T(128)} %param.19) | copy-start | bytes 1540
  0.7 7.4 %copy-start.6 = (bf16[512]{0:T(512)(128)(2,1)S(1)}, bf16[512]{0:T(512)(128)(2,1)}, u32[]{:S(2)}) copy-start(bf16[512]{0:T(512)(128)(2,1)} %param.16) | copy-start | bytes 3076
  0.7 8.0 %copy-start.7 = (bf16[512]{0:T(512)(128)(2,1)S(1)}, bf16[512]{0:T(512)(128)(2,1)}, u32[]{:S(2)}) copy-start(bf16[512]{0:T(512)(128)(2,1)} %param.23) | copy-start | bytes 3076
  0.7 8.5 %copy-start.3 = (s32[8,4]{0,1:T(4,128)S(1)}, s32[8,4]{0,1:T(4,128)}, u32[]{:S(2)}) copy-start(s32[8,4]{0,1:T(4,128)} %param.14) | copy-start | bytes 388
  221.7 6.8 %copy-start.2 = (f32[8,128]{1,0:T(8,128)S(1)}, f32[8,128]{1,0:T(8,128)}, u32[]{:S(2)}) copy-start(f32[8,128]{1,0:T(8,128)} %get-tuple-element.44) | copy-start | bytes 12292
  221.7 7.4 %copy-start.1 = (f32[512,256]{1,0:T(8,128)S(1)}, f32[512,256]{1,0:T(8,128)}, u32[]{:S(2)}) copy-start(f32[512,256]{1,0:T(8,128)} %get-tuple-element.45) | copy-start | bytes 1572868
  221.7 8.2 %copy-start.4 = (f32[8,256]{1,0:T(8,128)S(1)}, f32[8,256]{1,0:T(8,128)}, u32[]{:S(2)}) copy-start(f32[8,256]{1,0:T(8,128)} %get-tuple-element.46) | copy-start | bytes 24580
  221.7 9.3 %copy-start = (f32[512,640]{1,0:T(8,128)S(1)}, f32[512,640]{1,0:T(8,128)}, u32[]{:S(2)}) copy-start(f32[512,640]{1,0:T(8,128)} %get-tuple-element.47) | copy-start | bytes 3932164

commit v4 on v2

v4 whole, which is shorter than its diff:
```python
import functools

import jax
import jax.numpy as jnp
from jax import lax
from jax.experimental import pallas as pl
from jax.experimental.pallas import tpu as pltpu
from jax.sharding import PartitionSpec as P

KW = 4
NORM_EPS = 1e-06
BP = 32
CT = 256
FT = 512
MIB = 2**20
F32 = jnp.float32
BF16 = jnp.bfloat16
MESH = pl.DeviceIdType.MESH
ANY = pl.BlockSpec(memory_space=pl.ANY)

ERF_A = (0.254829592, -0.284496736, 1.421413741, -1.453152027, 1.061405429)
ERF_P = 0.3275911 * 0.7071067811865476
INV_ROOT_TWO_PI = 0.3989422804014327


def gelu_parts(x):
    t = 1.0 / (1.0 + ERF_P * jnp.abs(x))
    e = jnp.exp(-0.5 * (x * x))
    poly = 0.5 * ERF_A[4]
    for a in (ERF_A[3], ERF_A[2], ERF_A[1], ERF_A[0]):
        poly = poly * t + 0.5 * a
    tail = poly * t * e
    cdf = jnp.where(x >= 0, 1.0 - tail, tail)
    return x * cdf, cdf + x * (e * INV_ROOT_TWO_PI)


def dist_of(bounds_ref, first, count):
    place = (lax.broadcasted_iota(jnp.int32, (count, 8, 128), 0) + first).astype(F32)
    start = jnp.zeros((count, 8, 128), F32)
    for s in range(bounds_ref.shape[0]):
        b = bounds_ref[s][None]
        start = jnp.where(b <= place, jnp.maximum(start, b), start)
    return (place - start).reshape(count * 8, 128)


def wide(d, width=CT):
    return jnp.concatenate([d] * (width // 128), axis=1)


def dot(a, b):
    return jnp.dot(a, b, preferred_element_type=F32)


def dot_nt(a, b):
    return lax.dot_general(a, b, (((1,), (1,)), ((), ())), preferred_element_type=F32)


def dot_tn(a, b):
    return lax.dot_general(a, b, (((0,), (0,)), ((), ())), preferred_element_type=F32)


class Place:
    def __init__(self):
        self.n_mp, self.n_dp = lax.axis_size("mp"), lax.axis_size("dp")
        self.n_a = self.n_mp // 2
        self.dp, self.mp = lax.axis_index("dp"), lax.axis_index("mp")
        self.a, self.b = self.mp // 2, self.mp % 2
        self.y, self.c = (self.dp // 2) % 2, self.dp % 2
        self.base = self.dp - self.y * 2 - self.c
        self.q = self.c * 2 + self.y

    def line(self, da):
        return (self.dp, (self.a ^ da) * 2 + self.b)

    def diagonal(self, da):
        return (self.dp, (self.a ^ da) * 2 + 1 - self.b)

    def pair(self):
        return (self.dp, self.a * 2 + 1 - self.b)

    def beside(self):
        return (self.base + (1 - self.y) * 2 + self.c, self.mp)

    def twin(self):
        return (self.base + self.y * 2 + 1 - self.c, self.mp)

    def across(self):
        return (self.base + (1 - self.y) * 2 + 1 - self.c, self.mp)

    def other(self, dm):
        return (self.dp, lax.rem(self.mp + dm, self.n_mp))

    def partners(self):
        group = [(lax.rem(self.dp + k, self.n_dp), self.mp) for k in range(1, self.n_dp)]
        return group + [self.other(dm) for dm in range(1, self.n_mp)]

    def greet(self):
        for d in self.partners():
            pl.semaphore_signal(pltpu.get_barrier_semaphore(), inc=1, device_id=d, device_id_type=MESH)

    def await_all(self):
        pl.semaphore_wait(pltpu.get_barrier_semaphore(), len(self.partners()))


def remote(src, dst, send, recv, device):
    return pltpu.make_async_remote_copy(src_ref=src, dst_ref=dst, send_sem=send, recv_sem=recv, device_id=device, device_id_type=MESH)


class Gather:
    def __init__(self, here, wall, first, rows, send, recv, direct=False, routed=False):
        self.direct = direct
        self.routed = routed
        self.h, self.wall, self.first, self.rows, self.send, self.recv = here, wall, first, rows, send, recv
        n_a = here.n_a
        self.z0, self.x0, self.y0, self.t0 = 0, n_a, 2 * n_a, 4 * n_a
        self.used = []

    def span(self, shard, q, count=1):
        n = self.rows // 4
        return self.wall.at[pl.ds(pl.multiple_of(self.first + shard * self.rows + q * n, 16), count * n)]

    def move(self, sem, shard, q, device, count=1):
        s = self.span(shard, q, count)
        remote(s, s, self.send.at[sem], self.recv.at[sem], device).start()
        self.used.append((sem, count))

    def landed(self, sem, shard, q, count=1):
        s = self.span(shard, q, count)
        remote(s, s, self.send.at[sem], self.recv.at[sem], self.h.pair()).wait_recv()

    def shard(self, da, other):
        h = self.h
        return (h.a ^ da) * 2 + ((1 - h.b) if other else h.b)

    def slot(self, da, other):
        return 2 * da + (1 if other else 0)

    def open(self):
        h = self.h
        self.move(self.x0, h.mp, h.q, h.pair())
        for da in range(1, h.n_a):
            if self.direct:
                self.move(self.z0 + da, h.mp, 2 * h.c, h.line(da), 2)
            else:
                self.move(self.z0 + da, h.mp, h.q, h.line(da))
            if self.routed:
                self.move(self.x0 + da, h.mp, h.q, h.diagonal(da))

    def spread(self, da, other):
        h, s = self.h, self.shard(da, other)
        self.move(self.y0 + self.slot(da, other), s, h.q, h.beside())
        self.move(self.t0 + 2 * self.slot(da, other), s, h.q, h.twin())

    def from_line(self, da):
        h, s = self.h, self.shard(da, False)
        if self.direct:
            self.landed(self.z0 + da, s, 2 * h.c, 2)
            self.move(self.x0 + da, s, h.q, h.pair())
            self.move(self.t0 + 2 * self.slot(da, False), s, 2 * h.c, h.twin(), 2)
        else:
            self.landed(self.z0 + da, s, h.q)
            if not self.routed:
                self.move(self.x0 + da, s, h.q, h.pair())
            self.spread(da, False)

    def from_pair(self, da):
        self.landed(self.x0 + da, self.shard(da, True), self.h.q)
        self.spread(da, True)

    def from_beside(self, da, other):
        if self.direct and not other:
            return
        h, s = self.h, self.shard(da, other)
        q = h.c * 2 + 1 - h.y
        self.landed(self.y0 + self.slot(da, other), s, q)
        self.move(self.t0 + 2 * self.slot(da, other) + 1, s, q, h.twin())

    def from_twin(self, da, other):
        h, s = self.h, self.shard(da, other)
        if self.direct and not other:
            self.landed(self.t0 + 2 * self.slot(da, other), s, 2 * (1 - h.c), 2)
            return
        self.landed(self.t0 + 2 * self.slot(da, other), s, (1 - h.c) * 2 + h.y)
        self.landed(self.t0 + 2 * self.slot(da, other) + 1, s, (1 - h.c) * 2 + 1 - h.y)

    def close(self):
        for sem, count in self.used:
            s = self.wall.at[pl.ds(self.first, count * self.rows // 4)]
            remote(s, s, self.send.at[sem], self.recv.at[sem], self.h.pair()).wait_send()


class Reduce:
    def __init__(self, here, other_half, own_half, r1, r2, r3, line_slot, da, send, recv, pair_first=False):
        self.h, self.other_half, self.own_half, self.pair_first = here, other_half, own_half, pair_first
        self.r1, self.r2, self.r3, self.line_slot, self.da, self.send, self.recv = r1, r2, r3, line_slot, da, send, recv
        self.quarter = r2.shape[1]

    def copy(self, k):
        h = self.h
        if k == 0:
            src, dst, device = self.other_half(), self.r1, h.twin()
        elif k == 1 and self.pair_first:
            src, dst, device = self.r1.at[1 - h.b], self.r2, h.pair()
        elif k == 1:
            src, dst, device = self.r1.at[:, 1 - h.y], self.r2, h.beside()
        elif k == 2 and self.pair_first:
            src, dst, device = self.r2.at[1 - h.y], self.r3, h.beside()
        elif k == 2:
            src, dst, device = self.r2.at[1 - h.b], self.r3, h.pair()
        else:
            src, dst, device = self.r3, self.line_slot, h.line(self.da)
        return remote(src, dst, self.send.at[k], self.recv.at[k], device)

    def add(self, dst, src):
        step = 32

        @pl.loop(0, self.quarter // step)
        def _(i):
            at = pl.ds(pl.multiple_of(i * step, step), step)
            dst[at] = (dst[at].astype(F32) + src[at].astype(F32)).astype(BF16)

    def step1(self):
        self.copy(0).start()

    def step2(self):
        self.copy(0).wait_recv()
        own = self.own_half()
        for s in range(2):
            for y in range(2):
                self.add(self.r1.at[s, y], own.at[s, y])
        self.copy(1).start()

    def step3(self):
        self.copy(1).wait_recv()
        for s in range(2):
            self.add(self.r2.at[s], self.r1.at[self.h.b, s] if self.pair_first else self.r1.at[s, self.h.y])
        self.copy(2).start()

    def step4(self):
        self.copy(2).wait_recv()
        self.add(self.r3, self.r2.at[self.h.y if self.pair_first else self.h.b])
        if self.da:
            self.copy(3).start()

    def close(self):
        for k in range(4 if self.da else 3):
            self.copy(k).wait_send()


class Finish:
    def __init__(self, here, units, slots, groups, whole_sum, send, recv):
        self.h, self.units, self.slots, self.groups, self.whole, self.send, self.recv = here, units, slots, groups, whole_sum, send, recv
        self.n = units[0].quarter

    def rows(self, q):
        return self.whole.at[pl.ds(pl.multiple_of(q * self.n, self.n), self.n)]

    def copy(self, k):
        h = self.h
        part = self.rows(h.q)
        return remote(part, part, self.send.at[k], self.recv.at[k], (h.twin(), h.beside(), h.across())[k])

    def group_copy(self, k):
        h = self.h
        mine = h.dp // 4
        block = self.groups.at[mine]
        device = (lax.rem(h.dp + 4 * k, h.n_dp), h.mp)
        return remote(block, block, self.send.at[2 + k], self.recv.at[2 + k], device)

    def sum_line(self):
        h = self.h
        n_groups = h.n_dp // 4
        for unit in self.units:
            if unit.da:
                unit.copy(3).wait_recv()
        step = 32
        dst = self.rows(h.q) if n_groups == 1 else self.groups.at[h.dp // 4]
        own = self.units[-1].r3

        @pl.loop(0, self.n // step)
        def _(i):
            at = pl.ds(pl.multiple_of(i * step, step), step)
            total = own[at].astype(F32)
            for k in range(h.n_a - 1):
                total = total + self.slots[k, at].astype(F32)
            dst[at] = total.astype(BF16)

        if n_groups > 1:
            for k in range(1, n_groups):
                self.group_copy(k).start()
            for k in range(1, n_groups):
                self.group_copy(k).wait_recv()
            mine = self.rows(h.q)

            @pl.loop(0, self.n // step)
            def _(i):
                at = pl.ds(pl.multiple_of(i * step, step), step)
                total = self.groups[0, at].astype(F32)
                for k in range(1, n_groups):
                    total = total + self.groups[k, at].astype(F32)
                mine[at] = total.astype(BF16)

        for k in range(3):
            self.copy(k).start()

    def write(self, out):
        for k in range(3):
            self.copy(k).wait_recv()
        step = 32

        @pl.loop(0, 4 * self.n // step)
        def _(i):
            at = pl.ds(pl.multiple_of(i * step, step), step)
            out[at] = self.whole[at].astype(F32)

    def close(self):
        for k in range(3):
            self.copy(k).wait_send()
        for k in range(1, self.h.n_dp // 4):
            self.group_copy(k).wait_send()


def fill_bounds(bounds_ref, len_in):
    diagonal = lax.broadcasted_iota(jnp.int32, (8, 8), 0) == lax.broadcasted_iota(jnp.int32, (8, 8), 1)
    end = jnp.zeros((8, 1), F32)
    for s in range(bounds_ref.shape[0]):
        end = end + jnp.sum(jnp.where(diagonal, len_in[s : s + 1].astype(F32), 0.0), axis=1, keepdims=True)
        bounds_ref[s] = jnp.broadcast_to(end, (8, 128))


def to_time_major(parts):
    block = jnp.stack([p.astype(F32) for p in parts], axis=0)
    return jnp.swapaxes(block, 0, 1).reshape(-1, block.shape[-1])


def to_row_major(block):
    return jnp.swapaxes(block.reshape(-1, 8, block.shape[-1]), 0, 1)


def front_kernel(span, cot_ref, wv_in, wg_in, wo_in, wu_in, wd_in, taps_in, gb_in, cb_in, gain_in, len_in, x_in,
                 out_ref, dgain_ref, b_ref, msg_ref, a_out, small_out, h_grad, x_out, g_out, z_out, v_out, sg_out, rg_out, wv_out, wg_out,
                 f_out,
                 wall, x_tm, nbuf, gsc, msc, vsc, rbuf, ngp, vbuf, gbuf, dbuf, smalls, halo, carry, state_ref, acc_ref, c2_ref,
                 sg_head, bounds_ref, gain1_ref, gain2_ref, hp, dh, hb, hg, dwo, du, dd, stage, st, r1, r2, r3, r4, rw, rgroups,
                 w_send, w_recv, s_send, s_recv, h_sem, c_send, c_recv, l_sem, t_sem, z_sem, sg_sem, rg_sem, st_sem, x_sem,
                 r_send, r_recv, e_send, e_recv, d_send, d_recv):
    here = Place()
    n_mp, n_a = here.n_mp, here.n_a
    dim = x_tm.shape[1]
    local_c, local_h = wv_in.shape[1], wu_in.shape[1] // 2
    width, units = local_c * n_mp, local_h * n_mp
    tile_c = 2 * local_c
    rows = BP * 8
    blocks = span // BP
    step = pl.program_id(0)
    sections, first = {}, 0
    for k, (name, count) in enumerate((("wu1", local_h), ("wd1", local_h), ("wu2", local_h), ("wd2", local_h),
                                       ("wv", local_c), ("wg", local_c), ("wo", local_c))):
        sections[name] = Gather(here, wall, first, count, w_send.at[k], w_recv.at[k], routed=name == "wo")
        first += count * n_mp
    wv, wg, wo = (sections[name] for name in ("wv", "wg", "wo"))
    ffn1, ffn2 = [sections["wu1"], sections["wd1"]], [sections["wu2"], sections["wd2"]]
    far = range(1, n_a)

    def tile_of(da):
        return here.a ^ da

    def lanes_of(t):
        return pl.ds(pl.multiple_of(tile_of(t) * tile_c, tile_c), tile_c)

    def small_copy(dm):
        return remote(smalls.at[here.mp], smalls.at[here.mp], s_send.at[dm], s_recv.at[dm], here.other(dm))

    def halo_copy():
        return remote(x_tm.at[pl.ds(span * 8 - 32, 32)], halo, h_sem.at[0], h_sem.at[1], here.other(1))

    def carry_copy(dm, t):
        block = carry.at[here.mp, :, lanes_of(t)]
        return remote(block, block, c_send.at[dm, t], c_recv.at[dm, t], (here.dp, here.mp + dm))

    def decay_copy(dm):
        block = carry.at[here.mp, 8:16]
        return remote(block, block, d_send.at[dm], d_recv.at[dm], (here.dp, here.mp - dm))

    def raw_copies():
        return [pltpu.make_async_copy(x_in.at[r], vsc.at[pl.ds(r * span, span), pl.ds(0, dim)], x_sem.at[r]) for r in range(8)]

    def tile_copies(t):
        lanes = lanes_of(t)
        return [pltpu.make_async_copy(gsc.at[:, lanes], g_out.at[:, lanes], t_sem.at[0, t]),
                pltpu.make_async_copy(vsc.at[:, lanes], v_out.at[:, lanes], t_sem.at[1, t])]

    def weight_copies():
        return [pltpu.make_async_copy(wall.at[pl.ds(s.first, width)], o, l_sem.at[1 + i]) for i, (s, o) in enumerate(((wv, wv_out), (wg, wg_out)))]

    def x_copy():
        return pltpu.make_async_copy(x_tm, x_out, l_sem.at[0])

    def block_copy(src, dst, sem, i):
        at = pl.ds(pl.multiple_of(i * rows, rows), rows)
        return pltpu.make_async_copy(src.at[at], dst.at[at], sem.at[i])

    z_copy = functools.partial(block_copy, msc, z_out, z_sem)
    sg_copy = functools.partial(block_copy, msc, sg_out, sg_sem)
    rg_copy = functools.partial(block_copy, ngp, rg_out, rg_sem)

    own_rows, other_rows = pl.ds(2 * here.c, 2), pl.ds(2 * (1 - here.c), 2)

    def shards(t):
        return pl.ds(pl.multiple_of(2 * (here.a ^ further(t)), 2), 2)

    def further(t):
        return (t + 1) % n_a

    h_units = [
        Reduce(here, (lambda t=t: st.at[shards(t), other_rows]), (lambda t=t: st.at[shards(t), own_rows]),
               r1.at[t], r2.at[t], r3.at[t], r4.at[further(t) - 1] if further(t) else None, further(t), r_send.at[t], r_recv.at[t], t % 2 == 1)
        for t in range(n_a)
    ]
    h_end = Finish(here, h_units, r4, rgroups, rw, e_send, e_recv)

    parts = min(4, blocks)
    moves = [[[] for _ in range(n_a)] for _ in range(parts)]

    def plan(t, i, *actions):
        moves[min(i, parts - 1)][min(t, n_a - 1)].extend(actions)

    def each(group, method, *args):
        return [functools.partial(getattr(s, method), *args) for s in group]

    mixer = (wv, wg)
    for da in far:
        plan(0, da - 1, *each(mixer, "from_pair", da))
        plan(0, da, *each(mixer, "from_beside", da, False))
        plan(0 if da < 2 else 1, 3 if da < 2 else 2 * da - 4, *each(mixer, "from_beside", da, True))
        plan(1, 1, *each([wo], "from_line", da), *each([wo], "from_pair", da))
        plan(1, 3, *each(ffn1, "from_line", da))
        plan(2, 1, *each([wo], "from_beside", da, False), *each([wo], "from_beside", da, True))
        plan(2, 3, *each(ffn1, "from_pair", da))
        plan(3, 1, *each(ffn1, "from_beside", da, False))
        plan(3, 3, *each(ffn1, "from_beside", da, True))
    plan(0, 1, *each([wo], "open"))
    plan(0, 3, *each(ffn1, "open"))
    plan(1, 1, *each([wo], "from_pair", 0))
    plan(1, 3, *each(ffn1, "from_pair", 0))
    plan(2, 1, *each([wo], "from_beside", 0, True))
    plan(3, 1, *each(ffn1, "from_beside", 0, True))
    plan(3, 3, *each(ffn2, "open"))

    def advance(i):
        for t in range(n_a):
            if moves[i][t]:

                @pl.when(step == t)
                def _():
                    for action in moves[i][t]:
                        action()

    def normed(x):
        inv = lax.rsqrt(jnp.mean(x * x, axis=1, keepdims=True) + NORM_EPS)
        return (x * inv * gain1_ref[...]).astype(BF16)

    @pl.when(step == 0)
    def _():
        for copy in raw_copies():
            copy.start()
        here.greet()
        fill_bounds(bounds_ref, len_in)
        gain1_ref[...] = gain_in[0:1]
        gain2_ref[...] = gain_in[1:2]
        for s, w in ((wv, wv_in), (wg, wg_in)):
            wall[pl.ds(pl.multiple_of(s.first + here.mp * s.rows, 16), s.rows)] = w[...].astype(F32).T.astype(BF16)
        here.await_all()
        wv.open()
        wg.open()
        smalls[here.mp] = jnp.zeros(smalls.shape[1:], F32)
        smalls[here.mp, 0:KW, 0:local_c] = taps_in[...]
        smalls[here.mp, KW : KW + 1, 0:local_c] = gb_in[...]
        smalls[here.mp, KW + 1 : KW + 2, 0:local_c] = cb_in[...]
        for dm in range(1, n_mp):
            small_copy(dm).start()

        def put(s, block):
            wall[pl.ds(pl.multiple_of(s.first + here.mp * s.rows, 16), s.rows)] = block

        put(wo, wo_in[...])
        up = wu_in[...].astype(F32).T.astype(BF16)
        for k, both in enumerate((ffn1, ffn2)):
            put(both[0], up[k * local_h : (k + 1) * local_h])
            put(both[1], wd_in[k * local_h : (k + 1) * local_h])

        def take(i):
            block = to_time_major([vsc[pl.ds(pl.multiple_of(r * span + i * BP, BP), BP), 0:dim] for r in range(8)])
            x_tm[pl.ds(pl.multiple_of(i * rows, rows), rows)] = block.astype(BF16)
            nbuf[pl.ds(pl.multiple_of(32 + i * rows, 16), rows)] = normed(block)

        for copy in raw_copies():
            copy.wait()
        take(blocks - 1)
        halo_copy().start()

        @pl.loop(0, blocks - 1)
        def _(i):
            take(i)

            @pl.when(i == min(2, blocks - 2))
            def _():
                for action in each(mixer, "from_pair", 0):
                    action()

        for action in each(mixer, "from_beside", 0, True):
            action()
        for da in far:
            for action in each(mixer, "from_line", da):
                action()
        x_copy().start()
        halo_copy().wait_recv()
        nbuf[0:32] = normed(halo[...].astype(F32))
        for dm in range(1, n_mp):
            small_copy(dm).wait_recv()

    @pl.when(step < n_a)
    def _():
        for s in (wv, wg):
            s.from_twin(step, True)

            @pl.when(step > 0)
            def _():
                s.from_twin(step, False)

        tile, lanes = tile_of(step), lanes_of(step)
        wv_t = wall[pl.ds(pl.multiple_of(wv.first + tile * tile_c, tile_c), tile_c)]
        wg_t = wall[pl.ds(pl.multiple_of(wg.first + tile * tile_c, tile_c), tile_c)]
        small = jnp.concatenate([smalls[2 * tile, :, 0:local_c], smalls[2 * tile + 1, :, 0:local_c]], axis=1)
        taps = [jnp.broadcast_to(small[j : j + 1], (8, tile_c)) for j in range(KW)]
        bias = jnp.broadcast_to(small[KW : KW + 1], (8, tile_c))
        cb = jnp.broadcast_to(small[KW + 1 : KW + 2], (8, tile_c))
        vbuf[0:32] = dot_nt(nbuf[0:32], wv_t)

        def body(i, held):
            state, decay = held
            at = pl.ds(pl.multiple_of(32 + i * rows, 16), rows)
            vbuf[32 : 32 + rows] = dot_nt(nbuf[at], wv_t)
            gbuf[...] = dot_nt(nbuf[at], wg_t)
            dbuf[0:rows] = dist_of(bounds_ref, here.mp * span + i * BP, BP)
            v1, v2, v3 = vbuf[24:32], vbuf[16:24], vbuf[8:16]
            values = []
            for p in range(BP):
                at = slice(8 * p, 8 * p + 8)
                out_at = pl.ds(pl.multiple_of(i * rows + 8 * p, 8), 8)
                v0 = vbuf[32 + 8 * p : 40 + 8 * p]
                gate = jax.nn.sigmoid(gbuf[at] + bias)
                d = wide(dbuf[at], tile_c)
                mixed = cb + taps[0] * v0
                mixed = mixed + jnp.where(d >= 1.0, taps[1] * v1, 0.0)
                mixed = mixed + jnp.where(d >= 2.0, taps[2] * v2, 0.0)
                mixed = mixed + jnp.where(d >= 3.0, taps[3] * v3, 0.0)
                linked = jnp.where(d >= 1.0, state, 0.0)
                state = linked + gate * (mixed - linked)
                decay = jnp.where(d >= 1.0, decay * (1.0 - gate), 0.0)
                gsc[out_at, lanes] = gate
                msc[out_at, lanes] = mixed
                values.append(v0)
                if p % 2:
                    pair_at = pl.ds(pl.multiple_of(i * rows + 8 * p - 8, 16), 16)
                    vsc[pair_at, lanes] = jnp.concatenate(values, axis=0).astype(BF16)
                    values = []
                v1, v2, v3 = v0, v1, v2
            vbuf[0:32] = vbuf[rows : rows + 32]
            return state, decay

        held = (jnp.zeros((8, tile_c), F32), jnp.ones((8, tile_c), F32))
        for part_no in range(parts):
            held = lax.fori_loop(part_no * blocks // parts, (part_no + 1) * blocks // parts, body, held)
            if part_no < parts - 1:
                advance(part_no)
        state, decay = held
        carry[here.mp, 0:8, lanes] = state
        carry[here.mp, 8:16, lanes] = decay
        for dm in range(1, n_mp):

            @pl.when(here.mp + dm < n_mp)
            def _():
                carry_copy(dm, step).start()

        for copy in tile_copies(step):
            copy.start()
        advance(parts - 1)

        @pl.when(step == n_a - 1)
        def _():
            for dm in range(1, n_mp):

                @pl.when(here.mp - dm >= 0)
                def _():
                    decay_copy(dm).start()

    def from_twin(s):
        s.from_twin(0, True)
        for da in far:
            s.from_twin(da, True)
            s.from_twin(da, False)

    @pl.when(step == n_a)
    def _():
        for copy in weight_copies():
            copy.start()
        for dm in range(1, n_mp):

            @pl.when(here.mp - dm >= 0)
            def _():
                for t in range(n_a):
                    carry_copy(dm, t).wait_recv()

        start = jnp.zeros((8, width), F32)
        state_ref[...] = lax.fori_loop(0, here.mp, lambda i, s: carry[i, 0:8] + carry[i, 8:16] * s, start)
        for s in [wo] + ffn1:
            from_twin(s)
        for t in range(n_a):
            for copy in tile_copies(t):
                copy.wait()
        x_copy().wait()
        halo_copy().wait_send()
        dwo[...] = jnp.zeros_like(dwo)
        du[...] = jnp.zeros_like(du)
        dd[...] = jnp.zeros_like(dd)
        dgain_ref[...] = jnp.zeros_like(dgain_ref)
        acc_ref[...] = jnp.zeros_like(acc_ref)
        c2_ref[...] = jnp.ones_like(c2_ref)
        small_out[...] = smalls[...]

    def part(s, lo=0, hi=None):
        return wall[s.first + lo : s.first + (s.rows * n_mp if hi is None else hi)]

    def inside_of(i):
        place = (lax.broadcasted_iota(jnp.int32, (BP, 8, 128), 0) + (here.mp * span + i * BP)).astype(F32)
        last = bounds_ref.shape[0] - 1
        return jnp.where(place < bounds_ref[last][None], 1.0, 0.0).reshape(rows, 128)[:, 0:1]

    def feed(n2, fg, up, down):
        tile_f = min(FT, units)
        for f in range(0, units, tile_f):
            cols = slice(f, f + tile_f)
            hp[...] = dot_nt(n2, part(up, f, f + tile_f))
            dh[...] = dot_nt(fg, part(down, f, f + tile_f))
            for r in range(0, rows, 16):
                at = slice(r, r + 16)
                hidden, slope = gelu_parts(hp[at])
                hb[at, cols] = hidden.astype(BF16)
                hg[at, cols] = (dh[at] * slope).astype(BF16)
        out, ngrad = dot(hb[...], part(down)), dot(hg[...], part(up))
        dd[...] += dot_tn(fg, hb[...])
        du[...] += dot_tn(n2, hg[...])
        return out, ngrad

    @pl.when((step >= n_a) & (step < n_a + blocks))
    def _():
        i = step - n_a
        base = pl.multiple_of(i * rows, rows)
        dbuf[0:rows] = dist_of(bounds_ref, here.mp * span + i * BP, BP)
        for c in range(0, width, CT):
            lanes = slice(c, c + CT)
            state = state_ref[:, lanes]
            for p in range(0, BP, 2):
                pair = []
                for q in (p, p + 1):
                    at = pl.ds(pl.multiple_of(base + 8 * q, 8), 8)
                    linked = jnp.where(wide(dbuf[8 * q : 8 * q + 8]) >= 1.0, state, 0.0)
                    z = msc[at, lanes] - linked
                    state = linked + gsc[at, lanes] * z
                    msc[at, lanes] = z
                    pair.append(state)
                vsc[pl.ds(pl.multiple_of(base + 8 * p, 16), 16), lanes] = jnp.concatenate(pair, axis=0).astype(BF16)
            state_ref[:, lanes] = state
        z_copy(i).start()
        at = pl.ds(base, rows)
        residual = x_tm[at].astype(F32) + dot(vsc[at], part(wo))
        resid_b = residual.astype(BF16)
        x_tm[at] = resid_b
        resid = resid_b.astype(F32)
        inv = lax.rsqrt(jnp.mean(resid * resid, axis=1, keepdims=True) + NORM_EPS)
        n2 = (resid * inv * gain2_ref[...]).astype(BF16)
        nbuf[pl.ds(pl.multiple_of(32 + base, 16), rows)] = n2
        fg = (to_time_major([cot_ref[r] for r in range(8)]) * inside_of(i)).astype(BF16)
        out, ngrad = feed(n2, fg, *ffn1)
        rbuf[at] = residual + out
        ngp[at] = ngrad

        def when_a(k, *calls):
            @pl.when(i == min(k, blocks - 1))
            def _():
                for method, *args in calls:
                    for action in each(ffn2, method, *args):
                        action()

        when_a(2, ("from_pair", 0), *[("from_line", da) for da in far])
        when_a(4, *[("from_pair", da) for da in far])
        when_a(6, ("from_beside", 0, True), *[("from_beside", da, False) for da in far], *[("from_beside", da, True) for da in far])

    @pl.when(step == n_a + blocks - 1)
    def _():
        for s in range(n_mp):
            cols = slice(s * local_h, (s + 1) * local_h)
            both = jnp.concatenate([du[:, cols].astype(BF16), dd[:, cols].astype(BF16)], axis=1)
            st[s] = both.reshape(st.shape[1:])
        for unit in h_units:
            unit.step1()
        du[...] = jnp.zeros_like(du)
        dd[...] = jnp.zeros_like(dd)
        for s in ffn2:
            from_twin(s)

    @pl.when(step >= n_a + blocks)
    def _():
        i = step - n_a - blocks
        base = pl.multiple_of(i * rows, rows)
        at = pl.ds(base, rows)
        dbuf[0:rows] = dist_of(bounds_ref, here.mp * span + i * BP, BP)
        inside = inside_of(i)
        grad_out = to_time_major([cot_ref[r] for r in range(8)]) * inside
        fg = grad_out.astype(BF16)
        out, ngrad = feed(nbuf[pl.ds(pl.multiple_of(32 + base, 16), rows)], fg, *ffn2)
        out_ref[...] = to_row_major((rbuf[at] + out) * inside).astype(BF16)
        ngrad = ngp[at] + ngrad
        resid = x_tm[at].astype(F32)
        inv = lax.rsqrt(jnp.mean(resid * resid, axis=1, keepdims=True) + NORM_EPS)
        unit = resid * inv
        weighted = ngrad * gain2_ref[...]
        inner = jnp.mean(weighted * unit, axis=1, keepdims=True)
        rgrad = grad_out + inv * (weighted - unit * inner)
        ngp[at] = rgrad
        rg_copy(i).start()
        dgain_ref[...] += jnp.sum((ngrad * unit).reshape(BP, 8, -1), axis=0)
        mix = rgrad.astype(BF16)
        dwo[...] += dot_tn(mix, vsc[at])
        z_copy(i).wait()
        msc[at] = dot_nt(mix, part(wo))
        sg_copy(i).start()

        @pl.when(i == 0)
        def _():
            sg_head[...] = msc[0:16]

        for c in range(0, width, CT):
            lanes = slice(c, c + CT)
            acc, decay = acc_ref[:, lanes], c2_ref[:, lanes]
            for p in range(BP):
                one = pl.ds(pl.multiple_of(base + 8 * p, 8), 8)
                keep = jnp.where(wide(dbuf[8 * p : 8 * p + 8]) >= 1.0, 1.0 - gsc[one, lanes], 0.0)
                if p < 3:
                    keep = jnp.where(i == 0, 1.0, keep)
                decay = decay * keep
                term = decay * msc[one, lanes]
                if p < 2:
                    term = jnp.where(i == 0, 0.0, term)
                acc = acc + term
            acc_ref[:, lanes], c2_ref[:, lanes] = acc, decay

        def when(k, actions):
            @pl.when(i == min(k, blocks - 2))
            def _():
                for action in actions:
                    action()

        when(0, [unit.step2 for unit in h_units])
        when(2, [unit.step3 for unit in h_units[: n_a // 2]])
        when(3, [unit.step3 for unit in h_units[n_a // 2 :]] + [unit.step4 for unit in h_units[: n_a // 2]])
        when(4, [unit.step4 for unit in h_units[n_a // 2 :]])
        when(6, [h_end.sum_line])

    @pl.when(step == n_a + 2 * blocks - 1)
    def _():
        d3 = dist_of(bounds_ref, here.mp * span, 3)
        for c in range(0, width, CT):
            lanes = slice(c, c + CT)
            g3 = [gsc[8 * j : 8 * j + 8, lanes] for j in range(3)]
            k3 = [jnp.where(wide(d3[8 * j : 8 * j + 8]) >= 1.0, 1.0 - g3[j], 0.0) for j in range(3)]
            acc2, c2 = acc_ref[:, lanes], c2_ref[:, lanes]
            acc1, c1 = sg_head[8:16, lanes] + k3[2] * acc2, k3[2] * c2
            acc0, c0 = sg_head[0:8, lanes] + k3[1] * acc1, k3[1] * c1
            b_ref[0:16, lanes] = jnp.concatenate([k3[0] * acc0, jnp.zeros_like(acc0)], axis=0).astype(BF16)
            parts = [g3[0] * acc0, g3[1] * acc1, g3[2] * acc2, g3[0] * c0, g3[1] * c1, g3[2] * c2]
            for j in range(0, 6, 2):
                msg_ref[8 * j : 8 * j + 16, lanes] = jnp.concatenate(parts[j : j + 2], axis=0).astype(BF16)

        def out_copy(s):
            return pltpu.make_async_copy(stage.at[s % 2], f_out.at[s], st_sem.at[s % 2])

        for s in range(n_mp):
            if s >= 2:
                out_copy(s - 2).wait()
            for k, (acc, local) in enumerate(((du, local_h), (dd, local_h), (dwo, local_c))):
                block = acc[:, s * local : (s + 1) * local].astype(BF16)
                stage[s % 2, :, :, k * local_h : k * local_h + local] = block.reshape(4, dim // 4, local)
            out_copy(s).start()
        h_end.write(h_grad)
        for s in (n_mp - 2, n_mp - 1):
            out_copy(s).wait()
        for copy in weight_copies():
            copy.wait()
        for i in range(blocks):
            sg_copy(i).wait()
            rg_copy(i).wait()
        for s in [wv, wg, wo] + ffn1 + ffn2:
            s.close()
        for unit in h_units:
            unit.close()
        h_end.close()
        for dm in range(1, n_mp):
            small_copy(dm).wait_send()

            @pl.when(here.mp - dm >= 0)
            def _():
                decay_copy(dm).wait_send()

            @pl.when(here.mp + dm < n_mp)
            def _():
                decay_copy(dm).wait_recv()
                for t in range(n_a):
                    carry_copy(dm, t).wait_send()

        a_out[...] = carry[:, 8:16]


def back_kernel(span, small_ref, dgain2_ref, b_ref, msg_ref, a_ref, gain_in, len_in, x_in, wv_in, wg_in,
                sg_in, g_in, z_in, v_in, rg_in, f_in,
                tg_ref, vg_grad, f_grad, small_grad, gain_grad,
                sgb, gb, zb, vb, vg, gpg, n1t, rgb, dbuf, bar_buf, msg_buf, u0_ref, gn_ref, sm, smr, sm2,
                st, v1, v2, v3, v4, vw, vgroups, fown, f1, f2, f3, f4, fw, fgroups,
                dg1, ga, gar, gs, gbr, bounds_ref, gain_ref, x_ref, wv_ref, wg_ref, w_sem,
                e_send, e_recv, in_sem, own_sem, rg_sem, f_send, f_recv, v_send, v_recv, ff_send, ff_recv, vf_send, vf_recv,
                m_send, m_recv, k_send, k_recv, g_send, g_recv):
    here = Place()
    n_mp, n_a, n_dp = here.n_mp, here.n_a, here.n_dp
    total, dim = x_ref.shape
    width = wv_ref.shape[0]
    local_c = width // n_mp
    tile_c = 2 * local_c
    rows = BP * 8
    blocks = span // BP
    own_rows, other_rows = pl.ds(2 * here.c, 2), pl.ds(2 * (1 - here.c), 2)

    def tile_of(t):
        return here.a ^ far(t)

    def lanes_of(t):
        return pl.ds(pl.multiple_of(tile_of(t) * tile_c, tile_c), tile_c)

    def ba_copy(dm):
        return remote(b_ref, bar_buf.at[here.mp], e_send.at[dm], e_recv.at[dm], (here.dp, here.mp - dm))

    def msg_copy():
        return remote(msg_ref, msg_buf, e_send.at[0], e_recv.at[0], (here.dp, here.mp - 1))

    def inputs(t):
        slot, lanes = t % 2, lanes_of(t)
        pairs = ((sg_in, sgb), (g_in, gb), (z_in, zb), (v_in, vb))
        return [pltpu.make_async_copy(src.at[:, lanes], dst.at[slot], in_sem.at[slot, k]) for k, (src, dst) in enumerate(pairs)]

    def own_copy(t):
        return pltpu.make_async_copy(f_in.at[pl.ds(pl.multiple_of(2 * tile_of(t), 2), 2), own_rows], fown.at[t], own_sem.at[t])

    rg_copy = pltpu.make_async_copy(rg_in, rgb, rg_sem)

    def far(t):
        return (t + 1) % n_a

    f_units = [
        Reduce(here, (lambda t=t: f_in.at[pl.ds(pl.multiple_of(2 * tile_of(t), 2), 2), other_rows]), (lambda t=t: fown.at[t]),
               f1.at[t], f2.at[t], f3.at[t], f4.at[far(t) - 1] if far(t) else None, far(t), f_send.at[t], f_recv.at[t], t % 2 == 1)
        for t in range(n_a)
    ]
    v_units = [
        Reduce(here, (lambda t=t: st.at[t, :, other_rows]), (lambda t=t: st.at[t, :, own_rows]),
               v1.at[t], v2.at[t], v3.at[t], v4.at[far(t) - 1] if far(t) else None, far(t), v_send.at[t], v_recv.at[t], True)
        for t in range(n_a)
    ]
    f_end = Finish(here, f_units, f4, fgroups, fw, ff_send, ff_recv)
    v_end = Finish(here, v_units, v4, vgroups, vw, vf_send, vf_recv)

    here.greet()
    weight_copies = [pltpu.make_async_copy(src, dst, w_sem.at[k]) for k, (src, dst) in enumerate(((x_in, x_ref), (wv_in, wv_ref), (wg_in, wg_ref)))]
    for copy in weight_copies:
        copy.start()
    fill_bounds(bounds_ref, len_in)
    gain_ref[...] = gain_in[0:1]
    here.await_all()
    for dm in range(1, n_mp):

        @pl.when(here.mp - dm >= 0)
        def _():
            ba_copy(dm).start()
            if dm == 1:
                msg_copy().start()

    for copy in inputs(0):
        copy.start()
    for unit in f_units:
        unit.step1()
    for t in range(n_a):
        own_copy(t).start()
    rg_copy.start()

    sm[...] = jnp.zeros_like(sm)
    gain = gain_ref[...]
    dbuf[...] = dist_of(bounds_ref, here.mp * span, span + 4)

    def unit_of(i):
        x = x_ref[pl.ds(pl.multiple_of(i * rows, rows), rows)].astype(F32)
        inv = lax.rsqrt(jnp.mean(x * x, axis=1, keepdims=True) + NORM_EPS)
        return x * inv, inv

    for copy in weight_copies:
        copy.wait()
    for i in range(blocks):
        unit, _ = unit_of(i)
        n1t[:, i * rows : (i + 1) * rows] = (unit * gain).astype(BF16).astype(F32).T.astype(BF16)

    for t, unit in enumerate(f_units):
        own_copy(t).wait()
        unit.step2()

    for dm in range(1, n_mp):

        @pl.when(here.mp + dm < n_mp)
        def _():
            if dm == 1:
                msg_copy().wait_recv()
            ba_copy(dm).wait_recv()

    zero = jnp.zeros((8, width), F32)
    last = here.mp >= n_mp - 1
    def start_of(m):
        return bar_buf[m].astype(F32)[0:8]

    u_next = lax.fori_loop(0, n_mp - 2 - here.mp, lambda j, u: start_of(n_mp - 1 - j) + a_ref[n_mp - 1 - j] * u, zero)
    right = jnp.minimum(here.mp + 1, n_mp - 1)
    u0_ref[...] = jnp.where(last, 0.0, start_of(right) + a_ref[right] * u_next)
    msg = msg_buf[...].astype(F32)
    for j in range(3):
        gn_ref[8 * j : 8 * j + 8] = jnp.where(last, 0.0, msg[8 * j : 8 * j + 8] + msg[24 + 8 * j : 32 + 8 * j] * u_next)

    def tile_pass(t, hook):
        slot, tile, lanes = t % 2, tile_of(t), lanes_of(t)
        for copy in inputs(t):
            copy.wait()
        if t + 1 < n_a:
            for copy in inputs(t + 1):
                copy.start()
        small = jnp.concatenate([small_ref[2 * tile, :, 0:local_c], small_ref[2 * tile + 1, :, 0:local_c]], axis=1)
        taps = [jnp.broadcast_to(small[j : j + 1], (8, tile_c)) for j in range(KW)]

        def body(i, held):
            u, g1, g2, g3 = held[:4]
            sums = list(held[4:])
            base = pl.multiple_of((blocks - 1 - i) * rows, rows)

            @pl.when(i == blocks // 2)
            def _():
                hook()

            def dist(q, least):
                return wide(dbuf[pl.ds(pl.multiple_of(base + 8 * q, 8), 8)], tile_c) >= least

            for p in range(BP - 2, -2, -2):
                pair_at = pl.ds(pl.multiple_of(base + 8 * p, 16), 16)
                vals = vb[slot, pair_at].astype(F32)
                vgs, gpgs = [None, None], [None, None]
                for k in (1, 0):
                    q = p + k
                    at = pl.ds(pl.multiple_of(base + 8 * q, 8), 8)
                    gate = gb[slot, at]
                    carried = sgb[slot, at] + u
                    g0 = carried * gate
                    gp = g0 * zb[slot, at] * (1.0 - gate)
                    u = jnp.where(dist(q, 1.0), carried - g0, 0.0)
                    h1 = jnp.where(dist(q + 1, 1.0), g1, 0.0)
                    h2 = jnp.where(dist(q + 2, 2.0), g2, 0.0)
                    h3 = jnp.where(dist(q + 3, 3.0), g3, 0.0)
                    v = vals[8 * k : 8 * k + 8]
                    vgs[k] = taps[0] * g0 + taps[1] * h1 + taps[2] * h2 + taps[3] * h3
                    gpgs[k] = gp
                    for j, h in enumerate((g0, h1, h2, h3)):
                        sums[j] = sums[j] + v * h
                    sums[KW + 1] = sums[KW + 1] + g0
                    sums[KW] = sums[KW] + gp.astype(BF16).astype(F32)
                    g1, g2, g3 = g0, g1, g2
                vg[pair_at, lanes] = jnp.concatenate(vgs, axis=0).astype(BF16)
                gpg[pair_at, lanes] = jnp.concatenate(gpgs, axis=0).astype(BF16)
            return (u, g1, g2, g3, *sums)

        start = [u0_ref[:, lanes]] + [gn_ref[8 * j : 8 * j + 8, lanes] for j in range(3)]
        held = lax.fori_loop(0, blocks, body, (*start, *[jnp.zeros((8, tile_c), F32)] * (KW + 2)))
        for j in range(KW + 2):
            sm[j : j + 1, lanes] = jnp.sum(held[4 + j], axis=0, keepdims=True)
        dv = dot(n1t[...], vg[:, lanes]).astype(BF16)
        dg = dot(n1t[...], gpg[:, lanes]).astype(BF16)
        for s in range(2):
            cols = slice(s * local_c, (s + 1) * local_c)
            st[t, s] = jnp.concatenate([dv[:, cols], dg[:, cols]], axis=1).reshape(st.shape[2:])
        v_units[t].step1()
    stages = [[] for _ in range(2 * n_a)]
    final = [[] for _ in range(blocks)]

    def later(at, action):
        if at < 2 * n_a - 1:
            stages[at].append(action)
        else:
            final[min(at - (2 * n_a - 1), blocks - 1)].append(action)

    end = 2 * n_a - 1
    for t in range(n_a):
        later(t + 1, f_units[t].step3)
        later(t + 3, f_units[t].step4)
        late = t == n_a - 1
        later(end + 2 if late else 2 * t + 2, v_units[t].step2)
        later(end + 6 if late else 2 * t + 4, v_units[t].step3)
        later(end + 7 if late else 2 * t + 6 + (t == n_a - 2) * 2, v_units[t].step4)
    final[min(4, blocks - 1)].append(f_end.sum_line)

    def run(actions):
        for action in actions:
            action()

    for t in range(n_a):
        tile_pass(t, functools.partial(run, stages[2 * t]))
        if t < n_a - 1:
            run(stages[2 * t + 1])

    def sm_copy(k):
        return remote(sm, smr.at[here.dp], m_send.at[k], m_recv.at[k], (lax.rem(here.dp + k, n_dp), here.mp))

    def tile_copy(dm):
        tile = lax.rem(here.mp + dm, n_mp) // 2
        lanes = pl.ds(pl.multiple_of(tile * tile_c, tile_c), tile_c)
        return remote(sm.at[:, lanes], sm2.at[here.mp], k_send.at[dm], k_recv.at[dm], here.other(dm))

    def sm_round():
        for k in range(1, n_dp):
            sm_copy(k).wait()
        sm_sum = smr[0]
        for k in range(1, n_dp):
            sm_sum = sm_sum + smr[k]
        sm[...] = sm_sum
        for dm in range(1, n_mp):
            tile_copy(dm).start()

    for k in range(1, n_dp):
        sm_copy(k).start()
    smr[here.dp] = sm[...]
    final[min(2, blocks - 1)].append(sm_round)
    rg_copy.wait()

    @pl.loop(0, blocks)
    def _(i):
        at = pl.ds(pl.multiple_of(i * rows, rows), rows)
        ngrad = dot(vg[at], wv_ref[...]) + dot(gpg[at], wg_ref[...])
        unit, inv = unit_of(i)
        weighted = ngrad * gain
        inner = jnp.mean(weighted * unit, axis=1, keepdims=True)
        tg_ref[:, pl.ds(pl.multiple_of(i * BP, BP), BP), :] = to_row_major(rgb[at] + inv * (weighted - unit * inner))
        part = jnp.sum((ngrad * unit).reshape(BP, 8, -1), axis=0)
        dg1[...] = jnp.where(i == 0, part, dg1[...] + part)
        for k in range(blocks):
            if final[k]:

                @pl.when(i == k)
                def _():
                    run(final[k])

    for k, g in enumerate((dg1[...], dgain2_ref[...])):
        row = jnp.sum(g, axis=0, keepdims=True)
        for j in range(dim // 128):
            at = k * (dim // 128) + j
            ga[at : at + 1] = row[:, j * 128 : (j + 1) * 128]

    def ga_copy(k):
        return remote(ga, gar.at[here.dp], g_send.at[0, k], g_recv.at[0, k], (lax.rem(here.dp + k, n_dp), here.mp))

    def gb_copy(dm):
        return remote(gs, gbr.at[here.mp], g_send.at[1, dm], g_recv.at[1, dm], here.other(dm))

    for k in range(1, n_dp):
        ga_copy(k).start()
    gar[here.dp] = ga[...]
    v_end.sum_line()
    for k in range(1, n_dp):
        ga_copy(k).wait_recv()
    g_sum = gar[0]
    for k in range(1, n_dp):
        g_sum = g_sum + gar[k]
    gs[...] = g_sum
    for dm in range(1, n_mp):
        gb_copy(dm).start()
    gbr[here.mp] = g_sum
    own_lanes = pl.ds(pl.multiple_of(here.a * tile_c, tile_c), tile_c)
    sm2[here.mp] = sm[:, own_lanes]
    for dm in range(1, n_mp):
        tile_copy(dm).wait_recv()
    last_sum = sm2[0]
    for m in range(1, n_mp):
        last_sum = last_sum + sm2[m]
    small_grad[...] = last_sum
    f_end.write(f_grad)
    v_end.write(vg_grad)
    for dm in range(1, n_mp):
        gb_copy(dm).wait_recv()
    g_sum = gbr[0]
    for m in range(1, n_mp):
        g_sum = g_sum + gbr[m]
    gain_grad[...] = g_sum

    for unit in f_units + v_units + [f_end, v_end]:
        unit.close()
    for k in range(1, n_dp):
        ga_copy(k).wait_send()
    for dm in range(1, n_mp):
        tile_copy(dm).wait_send()
        gb_copy(dm).wait_send()

        @pl.when(here.mp - dm >= 0)
        def _():
            if dm == 1:
                msg_copy().wait_send()
            ba_copy(dm).wait_send()


def pack_kernel(vg_ref, f_ref, h_ref, small_ref, gains_ref, *outs):
    gain1_out, value_out, gate_out, gb_out, taps_out, cb_out, wo_out, gain2_out, up_out, down_out = outs
    local_c, local_h = value_out.shape[1], h_ref.shape[1] // 2
    value_out[...] = vg_ref[:, 0:local_c]
    gate_out[...] = vg_ref[:, local_c : 2 * local_c]
    up_out[:, 0:local_h] = h_ref[:, 0:local_h]
    up_out[:, local_h : 2 * local_h] = f_ref[:, 0:local_h]
    down_out[0:local_h] = h_ref[:, local_h : 2 * local_h].T
    down_out[local_h : 2 * local_h] = f_ref[:, local_h : 2 * local_h].T
    wo_out[...] = f_ref[:, 2 * local_h : 2 * local_h + local_c].T
    second = lax.axis_index("mp") % 2 == 1
    small = jnp.where(second, small_ref[:, local_c : 2 * local_c], small_ref[:, 0:local_c])
    taps_out[...] = small[0:KW]
    gb_out[...] = small[KW : KW + 1]
    cb_out[...] = small[KW + 1 : KW + 2]
    per = gains_ref.shape[0] // 2
    for j in range(per):
        lanes = slice(j * 128, (j + 1) * 128)
        gain1_out[:, lanes] = gains_ref[j : j + 1]
        gain2_out[:, lanes] = gains_ref[per + j : per + j + 1]


def whole(shape):
    return pl.BlockSpec(shape, lambda i: (0,) * len(shape))


def resident(shape):
    return pl.BlockSpec(shape, lambda i: (0,) * len(shape), pipeline_mode=pl.Buffered(1))


def per_device(tokens, lengths, cotangent, norm1_gain, value_proj, gate_proj, gate_bias, conv_taps, conv_bias, out_proj,
               norm2_gain, up_proj, down_proj):
    rows, span, dim = tokens.shape
    n_mp = lax.axis_size("mp")
    n_a = n_mp // 2
    total = rows * span
    blocks = span // BP
    tile = BP * 8
    local_c, local_f = value_proj.shape[1], up_proj.shape[1]
    width, units = local_c * n_mp, local_f * n_mp

    pad_c = max(local_c, 128)
    slots = lengths.shape[1]
    gains_f = jnp.stack([norm1_gain, norm2_gain]).astype(F32)
    slot_lengths = lengths.T
    gate_b, conv_b = gate_bias[None], conv_bias[None]

    def sds(shape, t=F32):
        return jax.ShapeDtypeStruct(shape, t)

    dma = pltpu.SemaphoreType.DMA
    vmem = pltpu.VMEM
    tile_c = 2 * local_c
    n_dp = lax.axis_size("dp")
    groups = n_dp // 4
    full = pl.BlockSpec(memory_space=pltpu.VMEM)
    quarter = dim // 4
    local_h = local_f // 2
    pad = -(-(2 * local_h + local_c) // 128) * 128

    def buffers(w):
        return [vmem((n_a, 2, 2, quarter, w), BF16), vmem((n_a, 2, quarter, w), BF16), vmem((n_a, quarter, w), BF16),
                vmem((n_a - 1, quarter, w), BF16), vmem((dim, w), BF16), vmem((groups, quarter, w), BF16)]

    cot_spec = pl.BlockSpec((rows, BP, dim), lambda i: (0, lax.rem(jnp.maximum(i - n_a, 0), blocks), 0))
    out_spec = pl.BlockSpec((rows, BP, dim), lambda i: (0, jnp.maximum(i - n_a - blocks, 0), 0))
    output, dgain2, b_msg, msg, a_all, smalls, h_grad, x_tm, gate, z, vals, sg, rg, wv, wg, f_grads = pl.pallas_call(
        functools.partial(front_kernel, span),
        grid=(n_a + 2 * blocks,),
        in_specs=[cot_spec, resident(value_proj.shape), resident(gate_proj.shape), resident(out_proj.shape),
                  resident(up_proj.shape), resident(down_proj.shape), resident(conv_taps.shape), resident((1, local_c)), resident((1, local_c)),
                  resident((2, dim)), resident(slot_lengths.shape), ANY],
        out_specs=[out_spec, resident((8, dim)), resident((16, width)), resident((48, width)), resident((n_mp, 8, width)),
                   resident((n_mp, 8, pad_c)),
                   resident((dim, 2 * local_h))] + [ANY] * 9,
        out_shape=[sds(tokens.shape, BF16), sds((8, dim)), sds((16, width), BF16), sds((48, width), BF16), sds((n_mp, 8, width)), sds((n_mp, 8, pad_c)),
                   sds((dim, 2 * local_h)), sds((total, dim), BF16), sds((total, width)), sds((total, width)), sds((total, width), BF16),
                   sds((total, width)), sds((total, dim)), sds((width, dim), BF16), sds((width, dim), BF16), sds((n_mp, 4, quarter, pad), BF16)],
        scratch_shapes=[
            vmem((3 * width + 2 * units, dim), BF16), vmem((total, dim), BF16), vmem((total + 32, dim), BF16), vmem((total, width), F32),
            vmem((total, width), F32), vmem((total, width), BF16), vmem((total, dim), F32), vmem((total, dim), F32),
            vmem((tile + 32, tile_c), F32), vmem((tile, tile_c), F32), vmem((tile, 128), F32),
            vmem((n_mp, 8, pad_c), F32), vmem((32, dim), BF16), vmem((n_mp, 16, width), F32), vmem((8, width), F32),
            vmem((8, width), F32), vmem((8, width), F32), vmem((16, width), F32),
            vmem((slots, 8, 128), F32), vmem((1, dim), F32), vmem((1, dim), F32),
            vmem((tile, min(FT, units // 2)), F32), vmem((tile, min(FT, units // 2)), F32), vmem((tile, units // 2), BF16),
            vmem((tile, units // 2), BF16),
            vmem((dim, width), F32), vmem((dim, units // 2), F32), vmem((dim, units // 2), F32), vmem((2, 4, quarter, pad), BF16),
            vmem((n_mp, 4, quarter, 2 * local_h), BF16), *buffers(2 * local_h),
            dma((7, 8 * n_a)), dma((7, 8 * n_a)), dma((n_mp,)), dma((n_mp,)), dma((2,)), dma((n_mp, n_a)), dma((n_mp, n_a)), dma((3,)),
            dma((2, n_a)), dma((blocks,)), dma((blocks,)), dma((blocks,)), dma((2,)), dma((8,)), dma((n_a, 4)), dma((n_a, 4)),
            dma((2 + groups,)), dma((2 + groups,)), dma((n_mp,)), dma((n_mp,)),
        ],
        compiler_params=pltpu.CompilerParams(collective_id=0, has_side_effects=True, vmem_limit_bytes=60 * MIB),
        name="front",
    )(cotangent, value_proj, gate_proj, out_proj, up_proj, down_proj, conv_taps, gate_b, conv_b, gains_f, slot_lengths, tokens)

    tokens_grad, vg_grad, f_grad, small_grad, gain_grad = pl.pallas_call(
        functools.partial(back_kernel, span),
        in_specs=[full] * 7 + [ANY] * 9,
        out_specs=[full] * 5,
        out_shape=[sds(tokens.shape), sds((dim, tile_c)), sds((dim, pad)), sds((8, tile_c)), sds((8, 128))],
        scratch_shapes=[
            vmem((2, total, tile_c), F32), vmem((2, total, tile_c), F32), vmem((2, total, tile_c), F32), vmem((2, total, tile_c), BF16),
            vmem((total, width), BF16), vmem((total, width), BF16), vmem((dim, total), BF16), vmem((total, dim), F32),
            vmem((total + 32, 128), F32), vmem((n_mp, 16, width), BF16), vmem((48, width), BF16), vmem((8, width), F32),
            vmem((24, width), F32), vmem((8, width), F32), vmem((n_dp, 8, width), F32), vmem((n_mp, 8, tile_c), F32),
            vmem((n_a, 2, 4, quarter, tile_c), BF16), *buffers(tile_c), vmem((n_a, 2, 2, quarter, pad), BF16), *buffers(pad),
            vmem((8, dim), F32), vmem((8, 128), F32), vmem((n_dp, 8, 128), F32), vmem((8, 128), F32), vmem((n_mp, 8, 128), F32),
            vmem((slots, 8, 128), F32), vmem((1, dim), F32), vmem((total, dim), BF16), vmem((width, dim), BF16), vmem((width, dim), BF16), dma((3,)),
            dma((n_mp,)), dma((n_mp,)), dma((2, 4)), dma((n_a,)), dma, dma((n_a, 4)), dma((n_a, 4)), dma((n_a, 4)), dma((n_a, 4)),
            dma((2 + groups,)), dma((2 + groups,)), dma((2 + groups,)), dma((2 + groups,)), dma((n_dp,)), dma((n_dp,)),
            dma((n_mp,)), dma((n_mp,)), dma((2, max(n_mp, n_dp))), dma((2, max(n_mp, n_dp))),
        ],
        compiler_params=pltpu.CompilerParams(collective_id=1, has_side_effects=True, vmem_limit_bytes=60 * MIB),
        name="back",
    )(smalls, dgain2, b_msg, msg, a_all, gains_f, slot_lengths, x_tm, wv, wg, sg, gate, z, vals, rg, f_grads)

    gain1_grad, value_grad, gate_grad, gb_grad, taps_grad, cb_grad, wo_grad, gain2_grad, up_grad, down_grad = pl.pallas_call(
        pack_kernel,
        out_shape=[sds((1, dim)), sds(value_proj.shape), sds(gate_proj.shape), sds((1, local_c)), sds(conv_taps.shape),
                   sds((1, local_c)), sds(out_proj.shape), sds((1, dim)), sds(up_proj.shape), sds(down_proj.shape)],
        name="pack",
    )(vg_grad, f_grad, h_grad, small_grad, gain_grad)
    return (output, tokens_grad, gain1_grad[0], value_grad, gate_grad, gb_grad[0], taps_grad, cb_grad[0], wo_grad, gain2_grad[0],
            up_grad, down_grad)


def solution(mesh):
    in_specs = (
        P("dp", "mp", None),
        P("dp", None),
        P("dp", "mp", None),
        P(),
        P(None, "mp"),
        P(None, "mp"),
        P("mp"),
        P(None, "mp"),
        P("mp"),
        P("mp", None),
        P(),
        P(None, "mp"),
        P("mp", None),
    )
    out_specs = (
        P("dp", "mp", None),
        P("dp", "mp", None),
        P(),
        P(None, "mp"),
        P(None, "mp"),
        P("mp"),
        P(None, "mp"),
        P("mp"),
        P("mp", None),
        P(),
        P(None, "mp"),
        P("mp", None),
    )
    return jax.shard_map(per_device, mesh=mesh, in_specs=in_specs, out_specs=out_specs, check_vma=False)
```

time: 603 us -> 190 us (0.32)
  waiting for transfers between devices: 225 us -> 0 us
  blocking collectives: 156 us -> 0 us
  Pallas kernels: 156 us -> 182 us
  local copies, waits for them, and re-layouts: 29.5 us -> 6.31 us
  other arithmetic: 19.1 us -> 0.6 us
  between operations: 14.4 us -> 0.68 us
    reduce_scatter x4 -> x0, waiting for transfers between devices: 113 us -> none  [the longest x3 57.5 us: total_first(): lax.psum_scatter(g, 'mp', scatter_dimension=0, tiled=False).astype(F32)]
    all_gather x3 -> x0, blocking collectives: 93.3 us -> none  [the longest x1 31.3 us: per_device(): a_all = lax.all_gather(a_end, 'mp')]
    unnamed x9 -> x0, waiting for transfers between devices: 89.9 us -> none
    psum x2 -> x0, blocking collectives: 62.3 us -> none  [the longest x1 40.1 us: per_device(): gains = lax.psum(jnp.stack([dgain1.sum(0), dgain2.sum(0)]), ('dp', 'mp'))]
    pallas_call x2 -> x3, Pallas kernels: 156 us -> 182 us  [the longest x1 122 us: per_device(): pl.pallas_call(functools.partial(front_kernel, span), grid=(n_a + 2 * blo...]
    psum x1 -> x0, waiting for transfers between devices: 22.4 us -> none  [total_first(): lax.psum(lax.psum_scatter(g, 'mp', scatter_dimension=0, tiled=False).asty...]
    reshape x2 -> x0, local copies, waits for them, and re-layouts: 8.67 us -> none  [row_major(): return jnp.transpose(a.reshape(span, rows, dim), (1, 0, 2))]
    transpose x2 -> x0, local copies, waits for them, and re-layouts: 6.59 us -> none  [time_major(): return jnp.transpose(a, (1, 0, 2)).reshape(-1, a.shape[2])]
  transfers between devices with their start and end apart: 8 -> 0, of which waited for: 5 -> 0; matrix products, arithmetic and copies ran while one was open for 5% -> 0% of each run, Pallas kernels for 4% -> 0%
where the time goes in v4:
time: 190 us
  Pallas kernels  182 us (96%)
  local copies, waits for them, and re-layouts  6.31 us (3%)
    pallas_call x1, Pallas kernels, per_device(): pl.pallas_call(functools.partial(front_kernel, span), grid=(n_a + 2 * blo...  122 us
    pallas_call x1, Pallas kernels, per_device(): pl.pallas_call(functools.partial(back_kernel, span), in_specs=[full] * 7...  57.1 us
    unnamed x6, local copies, waits for them, and re-layouts  4.95 us

profile of v4, /device:TPU:0, one launch (start us, length us, event | category | flops | bytes accessed | tf_op | source)
XLA Modules:
  0.0 190.0 jit_solution(9087406890938193065)
XLA Ops:
  0.6 0.7 stack.9
  1.3 0.7 stack.10
  2.0 0.6 maximum_convert_fusion.gain_in
  2.6 122.4 %front.1 = (bf16[8,256,512]{2,1,0:T(8,128)(2,1)}, f32[8,512]{1,0:T(8,128)}, bf16[16,1024]{1,0:T(8,128)(2,1)}, bf16[48,1024]{1,0:T(8,128)(2,1)}, f32[8,8,1024]{2,...) custom-call(bf16[8,256,512]{2,1,0:T(8,128)(2,1)} %cot_ref.1, ...), custom_call_target="tpu_custom_call" | custom-call | tf_op jit(solution)/shard_map/front/pallas_call | solution.py:1194
  125.0 0.0 copy-start.1
  125.0 57.1 %back.1 = (f32[8,256,512]{2,1,0:T(8,128)}, f32[512,256]{1,0:T(8,128)}, f32[512,384]{1,0:T(8,128)}, f32[8,256]{1,0:T(8,128)}, f32[8,128]{1,0:T(8,128)}) custom-call(f32[8,8,128]{2,1,0:T(8,128)} %get-tuple-element.44.small_ref, f32[8,512]{1,0:T(8,128)} %get-tuple-element.45.dgain2_ref, bf16[16,1024]{1,0:T(8,128)(2,1)} %get-tuple-element.46.b_ref, ...), custom_call_target="tpu_custom_call" | custom-call | tf_op jit(solution)/shard_map/back/pallas_call | solution.py:1225
  182.1 2.9 %pack.1 = (f32[1,512]{1,0:T(1,128)}, f32[512,128]{1,0:T(8,128)}, f32[512,128]{1,0:T(8,128)}, f32[1,128]{1,0:T(1,128)}, f32[4,128]{1,0:T(4,128)}, /*index=5*/f32[...) custom-call(f32[512,256]{1,0:T(8,128)} %get-tuple-element.59.vg_ref, ...), custom_call_target="tpu_custom_call" | custom-call | tf_op jit(solution)/shard_map/pack/pallas_call | solution.py:1246
  185.0 0.0 copy-start
  185.0 0.0 copy-done.1
  185.1 1.3 copy.27
  186.4 1.6 copy-done
  188.0 2.0 %copy.28 = f32[8,256,512]{2,1,0:T(8,128)} copy(f32[8,256,512]{2,1,0:T(8,128)S(1)} %copy-done) | data formatting | bytes 8388608
Async XLA Ops:
  125.0 60.0 %copy-start.1 = (bf16[8,256,512]{2,1,0:T(8,128)(2,1)S(1)}, bf16[8,256,512]{2,1,0:T(8,128)(2,1)}, u32[]{:S(2)}) copy-start(bf16[8,256,512]{2,1,0:T(8,128)(2,1)} %get-tuple-element.86) | copy-start | bytes 6291460
  185.0 2.9 %copy-start = (f32[8,256,512]{2,1,0:T(8,128)S(1)}, f32[8,256,512]{2,1,0:T(8,128)}, u32[]{:S(2)}) copy-start(f32[8,256,512]{2,1,0:T(8,128)} %get-tuple-element.87) | copy-start | bytes 12582916

commit v5 on v4

--- a/solution.py
+++ b/solution.py
@@ -10,6 +10,8 @@
 KW = 4
 NORM_EPS = 1e-06
 BP = 32
+BF = 32
+ST = 1024
 CT = 256
 FT = 512
 MIB = 2**20
@@ -303,9 +305,12 @@
         for k in range(3):
             self.copy(k).start()
 
-    def write(self, out):
+    def gathered(self):
         for k in range(3):
             self.copy(k).wait_recv()
+
+    def write(self, out):
+        self.gathered()
         step = 32
 
         @pl.loop(0, 4 * self.n // step)
@@ -338,7 +343,7 @@
 
 
 def front_kernel(span, cot_ref, wv_in, wg_in, wo_in, wu_in, wd_in, taps_in, gb_in, cb_in, gain_in, len_in, x_in,
-                 out_ref, dgain_ref, b_ref, msg_ref, a_out, small_out, h_grad, x_out, g_out, z_out, v_out, sg_out, rg_out, wv_out, wg_out,
+                 out_ref, dgain_ref, b_ref, msg_ref, small_out, a_out, h_grad, x_out, g_out, z_out, v_out, sg_out, rg_out, wv_out, wg_out,
                  f_out,
                  wall, x_tm, nbuf, gsc, msc, vsc, rbuf, ngp, vbuf, gbuf, dbuf, smalls, halo, carry, state_ref, acc_ref, c2_ref,
                  sg_head, bounds_ref, gain1_ref, gain2_ref, hp, dh, hb, hg, dwo, du, dd, stage, st, r1, r2, r3, r4, rw, rgroups,
@@ -350,8 +355,8 @@
     local_c, local_h = wv_in.shape[1], wu_in.shape[1] // 2
     width, units = local_c * n_mp, local_h * n_mp
     tile_c = 2 * local_c
-    rows = BP * 8
-    blocks = span // BP
+    rows, rows_f = BP * 8, BF * 8
+    blocks, blocks_f = span // BP, span // BF
     step = pl.program_id(0)
     sections, first = {}, 0
     for k, (name, count) in enumerate((("wu1", local_h), ("wd1", local_h), ("wu2", local_h), ("wd2", local_h),
@@ -397,7 +402,7 @@
         return pltpu.make_async_copy(x_tm, x_out, l_sem.at[0])
 
     def block_copy(src, dst, sem, i):
-        at = pl.ds(pl.multiple_of(i * rows, rows), rows)
+        at = pl.ds(pl.multiple_of(i * rows_f, rows_f), rows_f)
         return pltpu.make_async_copy(src.at[at], dst.at[at], sem.at[i])
 
     z_copy = functools.partial(block_copy, msc, z_out, z_sem)
@@ -633,9 +638,9 @@
         return wall[s.first + lo : s.first + (s.rows * n_mp if hi is None else hi)]
 
     def inside_of(i):
-        place = (lax.broadcasted_iota(jnp.int32, (BP, 8, 128), 0) + (here.mp * span + i * BP)).astype(F32)
+        place = (lax.broadcasted_iota(jnp.int32, (BF, 8, 128), 0) + (here.mp * span + i * BF)).astype(F32)
         last = bounds_ref.shape[0] - 1
-        return jnp.where(place < bounds_ref[last][None], 1.0, 0.0).reshape(rows, 128)[:, 0:1]
+        return jnp.where(place < bounds_ref[last][None], 1.0, 0.0).reshape(rows_f, 128)[:, 0:1]
 
     def feed(n2, fg, up, down):
         tile_f = min(FT, units)
@@ -643,7 +648,7 @@
             cols = slice(f, f + tile_f)
             hp[...] = dot_nt(n2, part(up, f, f + tile_f))
             dh[...] = dot_nt(fg, part(down, f, f + tile_f))
-            for r in range(0, rows, 16):
+            for r in range(0, rows_f, 16):
                 at = slice(r, r + 16)
                 hidden, slope = gelu_parts(hp[at])
                 hb[at, cols] = hidden.astype(BF16)
@@ -653,19 +658,19 @@
         du[...] += dot_tn(n2, hg[...])
         return out, ngrad
 
-    @pl.when((step >= n_a) & (step < n_a + blocks))
+    @pl.when((step >= n_a) & (step < n_a + blocks_f))
     def _():
         i = step - n_a
-        base = pl.multiple_of(i * rows, rows)
-        dbuf[0:rows] = dist_of(bounds_ref, here.mp * span + i * BP, BP)
-        for c in range(0, width, CT):
-            lanes = slice(c, c + CT)
+        base = pl.multiple_of(i * rows_f, rows_f)
+        dbuf[0:rows_f] = dist_of(bounds_ref, here.mp * span + i * BF, BF)
+        for c in range(0, width, ST):
+            lanes = slice(c, c + ST)
             state = state_ref[:, lanes]
-            for p in range(0, BP, 2):
+            for p in range(0, BF, 2):
                 pair = []
                 for q in (p, p + 1):
                     at = pl.ds(pl.multiple_of(base + 8 * q, 8), 8)
-                    linked = jnp.where(wide(dbuf[8 * q : 8 * q + 8]) >= 1.0, state, 0.0)
+                    linked = jnp.where(wide(dbuf[8 * q : 8 * q + 8], ST) >= 1.0, state, 0.0)
                     z = msc[at, lanes] - linked
                     state = linked + gsc[at, lanes] * z
                     msc[at, lanes] = z
@@ -673,21 +678,21 @@
                 vsc[pl.ds(pl.multiple_of(base + 8 * p, 16), 16), lanes] = jnp.concatenate(pair, axis=0).astype(BF16)
             state_ref[:, lanes] = state
         z_copy(i).start()
-        at = pl.ds(base, rows)
+        at = pl.ds(base, rows_f)
         residual = x_tm[at].astype(F32) + dot(vsc[at], part(wo))
         resid_b = residual.astype(BF16)
         x_tm[at] = resid_b
         resid = resid_b.astype(F32)
         inv = lax.rsqrt(jnp.mean(resid * resid, axis=1, keepdims=True) + NORM_EPS)
         n2 = (resid * inv * gain2_ref[...]).astype(BF16)
-        nbuf[pl.ds(pl.multiple_of(32 + base, 16), rows)] = n2
+        nbuf[pl.ds(pl.multiple_of(32 + base, 16), rows_f)] = n2
         fg = (to_time_major([cot_ref[r] for r in range(8)]) * inside_of(i)).astype(BF16)
         out, ngrad = feed(n2, fg, *ffn1)
         rbuf[at] = residual + out
         ngp[at] = ngrad
 
         def when_a(k, *calls):
-            @pl.when(i == min(k, blocks - 1))
+            @pl.when(i == k * blocks_f // 8)
             def _():
                 for method, *args in calls:
                     for action in each(ffn2, method, *args):
@@ -697,7 +702,7 @@
         when_a(4, *[("from_pair", da) for da in far])
         when_a(6, ("from_beside", 0, True), *[("from_beside", da, False) for da in far], *[("from_beside", da, True) for da in far])
 
-    @pl.when(step == n_a + blocks - 1)
+    @pl.when(step == n_a + blocks_f - 1)
     def _():
         for s in range(n_mp):
             cols = slice(s * local_h, (s + 1) * local_h)
@@ -710,16 +715,16 @@
         for s in ffn2:
             from_twin(s)
 
-    @pl.when(step >= n_a + blocks)
+    @pl.when(step >= n_a + blocks_f)
     def _():
-        i = step - n_a - blocks
-        base = pl.multiple_of(i * rows, rows)
-        at = pl.ds(base, rows)
-        dbuf[0:rows] = dist_of(bounds_ref, here.mp * span + i * BP, BP)
+        i = step - n_a - blocks_f
+        base = pl.multiple_of(i * rows_f, rows_f)
+        at = pl.ds(base, rows_f)
+        dbuf[0:rows_f] = dist_of(bounds_ref, here.mp * span + i * BF, BF)
         inside = inside_of(i)
         grad_out = to_time_major([cot_ref[r] for r in range(8)]) * inside
         fg = grad_out.astype(BF16)
-        out, ngrad = feed(nbuf[pl.ds(pl.multiple_of(32 + base, 16), rows)], fg, *ffn2)
+        out, ngrad = feed(nbuf[pl.ds(pl.multiple_of(32 + base, 16), rows_f)], fg, *ffn2)
         out_ref[...] = to_row_major((rbuf[at] + out) * inside).astype(BF16)
         ngrad = ngp[at] + ngrad
         resid = x_tm[at].astype(F32)
@@ -730,7 +735,7 @@
         rgrad = grad_out + inv * (weighted - unit * inner)
         ngp[at] = rgrad
         rg_copy(i).start()
-        dgain_ref[...] += jnp.sum((ngrad * unit).reshape(BP, 8, -1), axis=0)
+        dgain_ref[...] += jnp.sum((ngrad * unit).reshape(BF, 8, -1), axis=0)
         mix = rgrad.astype(BF16)
         dwo[...] += dot_tn(mix, vsc[at])
         z_copy(i).wait()
@@ -741,12 +746,12 @@
         def _():
             sg_head[...] = msc[0:16]
 
-        for c in range(0, width, CT):
-            lanes = slice(c, c + CT)
+        for c in range(0, width, ST):
+            lanes = slice(c, c + ST)
             acc, decay = acc_ref[:, lanes], c2_ref[:, lanes]
-            for p in range(BP):
+            for p in range(BF):
                 one = pl.ds(pl.multiple_of(base + 8 * p, 8), 8)
-                keep = jnp.where(wide(dbuf[8 * p : 8 * p + 8]) >= 1.0, 1.0 - gsc[one, lanes], 0.0)
+                keep = jnp.where(wide(dbuf[8 * p : 8 * p + 8], ST) >= 1.0, 1.0 - gsc[one, lanes], 0.0)
                 if p < 3:
                     keep = jnp.where(i == 0, 1.0, keep)
                 decay = decay * keep
@@ -757,7 +762,7 @@
             acc_ref[:, lanes], c2_ref[:, lanes] = acc, decay
 
         def when(k, actions):
-            @pl.when(i == min(k, blocks - 2))
+            @pl.when(i == min(k * blocks_f // 8, blocks_f - 2))
             def _():
                 for action in actions:
                     action()
@@ -768,7 +773,7 @@
         when(4, [unit.step4 for unit in h_units[n_a // 2 :]])
         when(6, [h_end.sum_line])
 
-    @pl.when(step == n_a + 2 * blocks - 1)
+    @pl.when(step == n_a + 2 * blocks_f - 1)
     def _():
         d3 = dist_of(bounds_ref, here.mp * span, 3)
         for c in range(0, width, CT):
@@ -793,12 +798,21 @@
                 block = acc[:, s * local : (s + 1) * local].astype(BF16)
                 stage[s % 2, :, :, k * local_h : k * local_h + local] = block.reshape(4, dim // 4, local)
             out_copy(s).start()
-        h_end.write(h_grad)
+        h_end.gathered()
+        for dm in range(1, n_mp):
+
+            @pl.when(here.mp + dm < n_mp)
+            def _():
+                decay_copy(dm).wait_recv()
+
+        tail = [pltpu.make_async_copy(rw, h_grad, l_sem.at[0]), pltpu.make_async_copy(carry.at[:, pl.ds(8, 8)], a_out, l_sem.at[3])]
+        for copy in tail:
+            copy.start()
         for s in (n_mp - 2, n_mp - 1):
             out_copy(s).wait()
         for copy in weight_copies():
             copy.wait()
-        for i in range(blocks):
+        for i in range(blocks_f):
             sg_copy(i).wait()
             rg_copy(i).wait()
         for s in [wv, wg, wo] + ffn1 + ffn2:
@@ -815,11 +829,11 @@
 
             @pl.when(here.mp + dm < n_mp)
             def _():
-                decay_copy(dm).wait_recv()
                 for t in range(n_a):
                     carry_copy(dm, t).wait_send()
 
-        a_out[...] = carry[:, 8:16]
+        for copy in tail:
+            copy.wait()
 
 
 def back_kernel(span, small_ref, dgain2_ref, b_ref, msg_ref, a_ref, gain_in, len_in, x_in, wv_in, wg_in,
@@ -1130,9 +1144,9 @@
     local_c, local_h = value_out.shape[1], h_ref.shape[1] // 2
     value_out[...] = vg_ref[:, 0:local_c]
     gate_out[...] = vg_ref[:, local_c : 2 * local_c]
-    up_out[:, 0:local_h] = h_ref[:, 0:local_h]
+    up_out[:, 0:local_h] = h_ref[:, 0:local_h].astype(F32)
     up_out[:, local_h : 2 * local_h] = f_ref[:, 0:local_h]
-    down_out[0:local_h] = h_ref[:, local_h : 2 * local_h].T
+    down_out[0:local_h] = h_ref[:, local_h : 2 * local_h].astype(F32).T
     down_out[local_h : 2 * local_h] = f_ref[:, local_h : 2 * local_h].T
     wo_out[...] = f_ref[:, 2 * local_h : 2 * local_h + local_c].T
     second = lax.axis_index("mp") % 2 == 1
@@ -1162,7 +1176,8 @@
     n_a = n_mp // 2
     total = rows * span
     blocks = span // BP
-    tile = BP * 8
+    tile, tile_f = BP * 8, BF * 8
+    blocks_f = span // BF
     local_c, local_f = value_proj.shape[1], up_proj.shape[1]
     width, units = local_c * n_mp, local_f * n_mp
 
@@ -1189,33 +1204,31 @@
         return [vmem((n_a, 2, 2, quarter, w), BF16), vmem((n_a, 2, quarter, w), BF16), vmem((n_a, quarter, w), BF16),
                 vmem((n_a - 1, quarter, w), BF16), vmem((dim, w), BF16), vmem((groups, quarter, w), BF16)]
 
-    cot_spec = pl.BlockSpec((rows, BP, dim), lambda i: (0, lax.rem(jnp.maximum(i - n_a, 0), blocks), 0))
-    out_spec = pl.BlockSpec((rows, BP, dim), lambda i: (0, jnp.maximum(i - n_a - blocks, 0), 0))
-    output, dgain2, b_msg, msg, a_all, smalls, h_grad, x_tm, gate, z, vals, sg, rg, wv, wg, f_grads = pl.pallas_call(
+    cot_spec = pl.BlockSpec((rows, BF, dim), lambda i: (0, lax.rem(jnp.maximum(i - n_a, 0), blocks_f), 0))
+    out_spec = pl.BlockSpec((rows, BF, dim), lambda i: (0, jnp.maximum(i - n_a - blocks_f, 0), 0))
+    output, dgain2, b_msg, msg, smalls, a_all, h_grad, x_tm, gate, z, vals, sg, rg, wv, wg, f_grads = pl.pallas_call(
         functools.partial(front_kernel, span),
-        grid=(n_a + 2 * blocks,),
+        grid=(n_a + 2 * blocks_f,),
         in_specs=[cot_spec, resident(value_proj.shape), resident(gate_proj.shape), resident(out_proj.shape),
                   resident(up_proj.shape), resident(down_proj.shape), resident(conv_taps.shape), resident((1, local_c)), resident((1, local_c)),
                   resident((2, dim)), resident(slot_lengths.shape), ANY],
-        out_specs=[out_spec, resident((8, dim)), resident((16, width)), resident((48, width)), resident((n_mp, 8, width)),
-                   resident((n_mp, 8, pad_c)),
-                   resident((dim, 2 * local_h))] + [ANY] * 9,
-        out_shape=[sds(tokens.shape, BF16), sds((8, dim)), sds((16, width), BF16), sds((48, width), BF16), sds((n_mp, 8, width)), sds((n_mp, 8, pad_c)),
-                   sds((dim, 2 * local_h)), sds((total, dim), BF16), sds((total, width)), sds((total, width)), sds((total, width), BF16),
+        out_specs=[out_spec, resident((8, dim)), resident((16, width)), resident((48, width)), resident((n_mp, 8, pad_c))] + [ANY] * 11,
+        out_shape=[sds(tokens.shape, BF16), sds((8, dim)), sds((16, width), BF16), sds((48, width), BF16), sds((n_mp, 8, pad_c)), sds((n_mp, 8, width)),
+                   sds((dim, 2 * local_h), BF16), sds((total, dim), BF16), sds((total, width)), sds((total, width)), sds((total, width), BF16),
                    sds((total, width)), sds((total, dim)), sds((width, dim), BF16), sds((width, dim), BF16), sds((n_mp, 4, quarter, pad), BF16)],
         scratch_shapes=[
             vmem((3 * width + 2 * units, dim), BF16), vmem((total, dim), BF16), vmem((total + 32, dim), BF16), vmem((total, width), F32),
             vmem((total, width), F32), vmem((total, width), BF16), vmem((total, dim), F32), vmem((total, dim), F32),
-            vmem((tile + 32, tile_c), F32), vmem((tile, tile_c), F32), vmem((tile, 128), F32),
+            vmem((tile + 32, tile_c), F32), vmem((tile, tile_c), F32), vmem((tile_f, 128), F32),
             vmem((n_mp, 8, pad_c), F32), vmem((32, dim), BF16), vmem((n_mp, 16, width), F32), vmem((8, width), F32),
             vmem((8, width), F32), vmem((8, width), F32), vmem((16, width), F32),
             vmem((slots, 8, 128), F32), vmem((1, dim), F32), vmem((1, dim), F32),
-            vmem((tile, min(FT, units // 2)), F32), vmem((tile, min(FT, units // 2)), F32), vmem((tile, units // 2), BF16),
-            vmem((tile, units // 2), BF16),
+            vmem((tile_f, min(FT, units // 2)), F32), vmem((tile_f, min(FT, units // 2)), F32), vmem((tile_f, units // 2), BF16),
+            vmem((tile_f, units // 2), BF16),
             vmem((dim, width), F32), vmem((dim, units // 2), F32), vmem((dim, units // 2), F32), vmem((2, 4, quarter, pad), BF16),
             vmem((n_mp, 4, quarter, 2 * local_h), BF16), *buffers(2 * local_h),
-            dma((7, 8 * n_a)), dma((7, 8 * n_a)), dma((n_mp,)), dma((n_mp,)), dma((2,)), dma((n_mp, n_a)), dma((n_mp, n_a)), dma((3,)),
-            dma((2, n_a)), dma((blocks,)), dma((blocks,)), dma((blocks,)), dma((2,)), dma((8,)), dma((n_a, 4)), dma((n_a, 4)),
+            dma((7, 8 * n_a)), dma((7, 8 * n_a)), dma((n_mp,)), dma((n_mp,)), dma((2,)), dma((n_mp, n_a)), dma((n_mp, n_a)), dma((4,)),
+            dma((2, n_a)), dma((blocks_f,)), dma((blocks_f,)), dma((blocks_f,)), dma((2,)), dma((8,)), dma((n_a, 4)), dma((n_a, 4)),
             dma((2 + groups,)), dma((2 + groups,)), dma((n_mp,)), dma((n_mp,)),
         ],
         compiler_params=pltpu.CompilerParams(collective_id=0, has_side_effects=True, vmem_limit_bytes=60 * MIB),

time: 190 us -> 186 us (0.979)
  Pallas kernels: 182 us -> 178 us
    pallas_call x1, Pallas kernels: 122 us -> 118 us  [per_device(): pl.pallas_call(functools.partial(front_kernel, span), grid=(n_a + 2 * blo...]
where the time goes in v5:
time: 186 us
  Pallas kernels  178 us (96%)
  local copies, waits for them, and re-layouts  6.31 us (3%)
    pallas_call x1, Pallas kernels, per_device(): pl.pallas_call(functools.partial(front_kernel, span), grid=(n_a + 2 * blo...  118 us
    pallas_call x1, Pallas kernels, per_device(): pl.pallas_call(functools.partial(back_kernel, span), in_specs=[full] * 7...  57.1 us
    unnamed x6, local copies, waits for them, and re-layouts  4.95 us

profile of v5, /device:TPU:0, one launch (start us, length us, event | category | flops | bytes accessed | tf_op | source)
XLA Modules:
  0.0 185.7 jit_solution(4770139798257444374)
XLA Ops:
  0.6 0.7 stack.9
  1.3 0.7 stack.10
  2.0 0.6 maximum_convert_fusion.gain_in
  2.6 118.3 %front.1 = (bf16[8,256,512]{2,1,0:T(8,128)(2,1)}, f32[8,512]{1,0:T(8,128)}, bf16[16,1024]{1,0:T(8,128)(2,1)}, bf16[48,1024]{1,0:T(8,128)(2,1)}, f32[8,8,128]{2,1...) custom-call(bf16[8,256,512]{2,1,0:T(8,128)(2,1)} %cot_ref.1, ...), custom_call_target="tpu_custom_call" | custom-call | tf_op jit(solution)/shard_map/front/pallas_call | solution.py:1209
  120.9 0.0 copy-start.1
  120.9 57.1 %back.1 = (f32[8,256,512]{2,1,0:T(8,128)}, f32[512,256]{1,0:T(8,128)}, f32[512,384]{1,0:T(8,128)}, f32[8,256]{1,0:T(8,128)}, f32[8,128]{1,0:T(8,128)}) custom-call(f32[8,8,128]{2,1,0:T(8,128)} %get-tuple-element.44.small_ref, f32[8,512]{1,0:T(8,128)} %get-tuple-element.45.dgain2_ref, bf16[16,1024]{1,0:T(8,128)(2,1)} %get-tuple-element.46.b_ref, ...), custom_call_target="tpu_custom_call" | custom-call | tf_op jit(solution)/shard_map/back/pallas_call | solution.py:1238
  178.0 2.8 %pack.1 = (f32[1,512]{1,0:T(1,128)}, f32[512,128]{1,0:T(8,128)}, f32[512,128]{1,0:T(8,128)}, f32[1,128]{1,0:T(1,128)}, f32[4,128]{1,0:T(4,128)}, /*index=5*/f32[...) custom-call(f32[512,256]{1,0:T(8,128)} %get-tuple-element.59.vg_ref, ...), custom_call_target="tpu_custom_call" | custom-call | tf_op jit(solution)/shard_map/pack/pallas_call | solution.py:1259
  180.8 0.0 copy-start
  180.8 0.0 copy-done.1
  180.8 1.3 copy.27
  182.1 1.6 copy-done
  183.7 2.0 %copy.28 = f32[8,256,512]{2,1,0:T(8,128)} copy(f32[8,256,512]{2,1,0:T(8,128)S(1)} %copy-done) | data formatting | bytes 8388608
Async XLA Ops:
  120.9 59.8 %copy-start.1 = (bf16[8,256,512]{2,1,0:T(8,128)(2,1)S(1)}, bf16[8,256,512]{2,1,0:T(8,128)(2,1)}, u32[]{:S(2)}) copy-start(bf16[8,256,512]{2,1,0:T(8,128)(2,1)} %get-tuple-element.86) | copy-start | bytes 6291460
  180.8 2.9 %copy-start = (f32[8,256,512]{2,1,0:T(8,128)S(1)}, f32[8,256,512]{2,1,0:T(8,128)}, u32[]{:S(2)}) copy-start(f32[8,256,512]{2,1,0:T(8,128)} %get-tuple-element.87) | copy-start | bytes 12582916

commit v6 on v5

--- a/solution.py
+++ b/solution.py
@@ -316,7 +316,7 @@
         @pl.loop(0, 4 * self.n // step)
         def _(i):
             at = pl.ds(pl.multiple_of(i * step, step), step)
-            out[at] = self.whole[at].astype(F32)
+            out[at] = self.whole[at]
 
     def close(self):
         for k in range(3):
@@ -361,7 +361,7 @@
     sections, first = {}, 0
     for k, (name, count) in enumerate((("wu1", local_h), ("wd1", local_h), ("wu2", local_h), ("wd2", local_h),
                                        ("wv", local_c), ("wg", local_c), ("wo", local_c))):
-        sections[name] = Gather(here, wall, first, count, w_send.at[k], w_recv.at[k], routed=name == "wo")
+        sections[name] = Gather(here, wall, first, count, w_send.at[k], w_recv.at[k], routed=name in ("wo", "wu2", "wd2"))
         first += count * n_mp
     wv, wg, wo = (sections[name] for name in ("wv", "wg", "wo"))
     ffn1, ffn2 = [sections["wu1"], sections["wd1"]], [sections["wu2"], sections["wd2"]]
@@ -1142,13 +1142,13 @@
 def pack_kernel(vg_ref, f_ref, h_ref, small_ref, gains_ref, *outs):
     gain1_out, value_out, gate_out, gb_out, taps_out, cb_out, wo_out, gain2_out, up_out, down_out = outs
     local_c, local_h = value_out.shape[1], h_ref.shape[1] // 2
-    value_out[...] = vg_ref[:, 0:local_c]
-    gate_out[...] = vg_ref[:, local_c : 2 * local_c]
+    value_out[...] = vg_ref[:, 0:local_c].astype(F32)
+    gate_out[...] = vg_ref[:, local_c : 2 * local_c].astype(F32)
     up_out[:, 0:local_h] = h_ref[:, 0:local_h].astype(F32)
-    up_out[:, local_h : 2 * local_h] = f_ref[:, 0:local_h]
+    up_out[:, local_h : 2 * local_h] = f_ref[:, 0:local_h].astype(F32)
     down_out[0:local_h] = h_ref[:, local_h : 2 * local_h].astype(F32).T
-    down_out[local_h : 2 * local_h] = f_ref[:, local_h : 2 * local_h].T
-    wo_out[...] = f_ref[:, 2 * local_h : 2 * local_h + local_c].T
+    down_out[local_h : 2 * local_h] = f_ref[:, local_h : 2 * local_h].astype(F32).T
+    wo_out[...] = f_ref[:, 2 * local_h : 2 * local_h + local_c].astype(F32).T
     second = lax.axis_index("mp") % 2 == 1
     small = jnp.where(second, small_ref[:, local_c : 2 * local_c], small_ref[:, 0:local_c])
     taps_out[...] = small[0:KW]
@@ -1239,7 +1239,7 @@
         functools.partial(back_kernel, span),
         in_specs=[full] * 7 + [ANY] * 9,
         out_specs=[full] * 5,
-        out_shape=[sds(tokens.shape), sds((dim, tile_c)), sds((dim, pad)), sds((8, tile_c)), sds((8, 128))],
+        out_shape=[sds(tokens.shape), sds((dim, tile_c), BF16), sds((dim, pad), BF16), sds((8, tile_c)), sds((8, 128))],
         scratch_shapes=[
             vmem((2, total, tile_c), F32), vmem((2, total, tile_c), F32), vmem((2, total, tile_c), F32), vmem((2, total, tile_c), BF16),
             vmem((total, width), BF16), vmem((total, width), BF16), vmem((dim, total), BF16), vmem((total, dim), F32),

time: 186 us -> 185 us (level)
    pallas_call x1, Pallas kernels: 57.1 us -> 54.2 us  [per_device(): pl.pallas_call(functools.partial(back_kernel, span), in_specs=[full] * 7...]
    pallas_call x1, Pallas kernels: 118 us -> 121 us  [per_device(): pl.pallas_call(functools.partial(front_kernel, span), grid=(n_a + 2 * blo...]
where the time goes in v6:
time: 185 us
  Pallas kernels  177 us (96%)
  local copies, waits for them, and re-layouts  6.32 us (3%)
    pallas_call x1, Pallas kernels, per_device(): pl.pallas_call(functools.partial(front_kernel, span), grid=(n_a + 2 * blo...  121 us
    pallas_call x1, Pallas kernels, per_device(): pl.pallas_call(functools.partial(back_kernel, span), in_specs=[full] * 7...  54.2 us
    unnamed x6, local copies, waits for them, and re-layouts  4.96 us

profile of v6, /device:TPU:0, one launch (start us, length us, event | category | flops | bytes accessed | tf_op | source)
XLA Modules:
  0.0 184.9 jit_solution(5038237278368700328)
XLA Ops:
  0.6 0.7 stack.9
  1.3 0.7 stack.10
  2.0 0.6 maximum_convert_fusion.gain_in
  2.6 120.6 %front.1 = (bf16[8,256,512]{2,1,0:T(8,128)(2,1)}, f32[8,512]{1,0:T(8,128)}, bf16[16,1024]{1,0:T(8,128)(2,1)}, bf16[48,1024]{1,0:T(8,128)(2,1)}, f32[8,8,128]{2,1...) custom-call(bf16[8,256,512]{2,1,0:T(8,128)(2,1)} %cot_ref.1, ...), custom_call_target="tpu_custom_call" | custom-call | tf_op jit(solution)/shard_map/front/pallas_call | solution.py:1209
  123.3 0.0 copy-start.1
  123.3 54.2 %back.1 = (f32[8,256,512]{2,1,0:T(8,128)}, bf16[512,256]{1,0:T(8,128)(2,1)}, bf16[512,384]{1,0:T(8,128)(2,1)}, f32[8,256]{1,0:T(8,128)}, f32[8,128]{1,0:T(8,128)}) custom-call(f32[8,8,128]{2,1,0:T(8,128)} %get-tuple-element.44.small_ref, f32[8,512]{1,0:T(8,128)} %get-tuple-element.45.dgain2_ref, bf16[16,1024]{1,0:T(8,128)(2,1)} %get-tuple-element.46.b_ref, ...), custom_call_target="tpu_custom_call" | custom-call | tf_op jit(solution)/shard_map/back/pallas_call | solution.py:1238
  177.4 2.5 %pack.1 = (f32[1,512]{1,0:T(1,128)}, f32[512,128]{1,0:T(8,128)}, f32[512,128]{1,0:T(8,128)}, f32[1,128]{1,0:T(1,128)}, f32[4,128]{1,0:T(4,128)}, /*index=5*/f32[...) custom-call(bf16[512,256]{1,0:T(8,128)(2,1)} %get-tuple-element.59.vg_ref, ...), custom_call_target="tpu_custom_call" | custom-call | tf_op jit(solution)/shard_map/pack/pallas_call | solution.py:1259
  180.0 0.0 copy-start
  180.0 0.0 copy-done.1
  180.0 1.3 copy.27
  181.3 1.6 copy-done
  182.9 2.0 %copy.28 = f32[8,256,512]{2,1,0:T(8,128)} copy(f32[8,256,512]{2,1,0:T(8,128)S(1)} %copy-done) | data formatting | bytes 8388608
Async XLA Ops:
  123.3 56.7 %copy-start.1 = (bf16[8,256,512]{2,1,0:T(8,128)(2,1)S(1)}, bf16[8,256,512]{2,1,0:T(8,128)(2,1)}, u32[]{:S(2)}) copy-start(bf16[8,256,512]{2,1,0:T(8,128)(2,1)} %get-tuple-element.86) | copy-start | bytes 6291460
  180.0 2.9 %copy-start = (f32[8,256,512]{2,1,0:T(8,128)S(1)}, f32[8,256,512]{2,1,0:T(8,128)}, u32[]{:S(2)}) copy-start(f32[8,256,512]{2,1,0:T(8,128)} %get-tuple-element.87) | copy-start | bytes 12582916
